TPU v7x, 256 devices: a whole 4x4x8 slice. The times are simulated.
256 devices in a mesh: ctx: 16 (over z_lo, x), tp: 16 (over y, z_hi, core).
Axes of the slice: x: 4, y: 4, z: 8 (z_hi: 2, z_lo: 4; z = z_hi * 4 + z_lo), core: 2. Of those that a mesh axis runs over, the one named last changes fastest.
Arguments:
- query_rows: bfloat16 [6144, 8192], P('ctx', 'tp'), may hold values from -5 to 5
- key_rows: bfloat16 [6144, 1024], P('ctx'), may hold values from -5 to 5
- value_rows: bfloat16 [6144, 1024], P('ctx'), may hold values from -18 to 18
- out_weight: bfloat16 [8192, 16384], P('tp', 'ctx'), may hold values from -0.25 to 0.25
- block_order: int32 [32], replicated, may hold values from 0 to 31, as said below
- doc_lengths: int32 [4], replicated, may hold values from 1 to 3072, 6144 in all
Outputs:
- projected: bfloat16 [6144, 16384], P(('ctx', 'tp'))
Inputs may be any that keep to these rules, and one draw needn't show every extreme that they name: A permutation of 0 to 31 in which block_order[2 c] + block_order[2 c + 1] = 31 for every c.
All inputs are finite; a program needn't handle non-finite values.
Results may differ from a plain program's by a relative error of at most 0.017.
Values may be sent and summed in bfloat16 or wider, within the bound.
No kernel may reach another device: no remote copies, remote signals or barrier semaphores. Data moves between devices by JAX's collectives and lax.ppermute only.
A program may use at most 128 MiB of HBM per device.

v0:
```python
import jax
import jax.numpy as jnp
from jax import lax
from jax.sharding import PartitionSpec as P

HD = 128
GROUP = 8


def local(query_rows, key_rows, value_rows, out_weight, block_order, doc_lengths):
    tok_count = query_rows.shape[0]
    width_local = query_rows.shape[1]
    head_count = width_local // HD
    kv_local = max(1, head_count // GROUP)
    per_kv = head_count // kv_local
    ctx_rank = lax.axis_index("ctx")
    tp_rank = lax.axis_index("tp")
    half_rows = tok_count // 2
    doc_ends = jnp.cumsum(doc_lengths)
    order_slots = jnp.arange(block_order.shape[0], dtype=jnp.int32)

    def locate(first_row, row_count):
        storage = first_row + jnp.arange(row_count, dtype=jnp.int32)
        block_index = storage // half_rows
        lookup = jnp.sum(
            jnp.where(block_index[:, None] == order_slots[None, :], block_order[None, :], 0), axis=1
        )
        position = lookup * half_rows + storage % half_rows
        document = jnp.sum((position[:, None] >= doc_ends[None, :]).astype(jnp.int32), axis=1)
        return (position, document)

    query_pos, query_doc = locate(ctx_rank * tok_count, tok_count)
    first_kv = tp_rank * head_count // GROUP
    key_local = lax.dynamic_slice_in_dim(key_rows, first_kv * HD, kv_local * HD, 1)
    value_local = lax.dynamic_slice_in_dim(value_rows, first_kv * HD, kv_local * HD, 1)
    grouped = query_rows.reshape(tok_count, kv_local, per_kv, HD)
    score_scale = HD ** (-0.5)
    key_piece = lax.all_gather(key_local, "ctx", axis=0, tiled=True)
    value_piece = lax.all_gather(value_local, "ctx", axis=0, tiled=True)
    row_count = key_piece.shape[0]
    key_pos, key_doc = locate(jnp.int32(0), row_count)
    allowed = (key_pos[None, :] <= query_pos[:, None]) & (key_doc[None, :] == query_doc[:, None])
    running_max = jnp.full((kv_local, per_kv, tok_count), -1e30, jnp.float32)
    scores = (
        jnp.einsum(
            "qkgd,nkd->kgqn",
            grouped,
            key_piece.reshape(row_count, kv_local, HD),
            preferred_element_type=jnp.float32,
        )
        * score_scale
    )
    scores = jnp.where(allowed[None, None], scores, -1e30)
    new_max = jnp.maximum(running_max, jnp.max(scores, axis=-1))
    weights = jnp.where(allowed[None, None], jnp.exp(scores - new_max[..., None]), 0.0)
    denominator = jnp.sum(weights, axis=-1)
    mixed = jnp.einsum(
        "kgqn,nkd->kgqd",
        weights.astype(jnp.bfloat16),
        value_piece.reshape(row_count, kv_local, HD),
        preferred_element_type=jnp.float32,
    )
    running_max, denominator, weighted = (new_max, denominator, mixed)
    attended = (
        (weighted / denominator[..., None])
        .transpose(2, 0, 1, 3)
        .reshape(tok_count, width_local)
        .astype(jnp.bfloat16)
    )
    full_weight = lax.all_gather(out_weight, "ctx", axis=1, tiled=True)
    return lax.psum_scatter(
        jnp.dot(attended, full_weight, preferred_element_type=jnp.float32).astype(jnp.bfloat16),
        "tp",
        scatter_dimension=0,
        tiled=True,
    )


def solution(mesh):
    in_specs = (P("ctx", "tp"), P("ctx", None), P("ctx", None), P("tp", "ctx"), P(), P())
    out_specs = P(("ctx", "tp"), None)
    return jax.shard_map(local, mesh=mesh, in_specs=in_specs, out_specs=out_specs, check_vma=False)
```

profile of v0, /device:TPU:8, one launch (start us, length us, event | category | flops | bytes accessed | tf_op | source)
XLA Modules:
  0.0 558.0 jit_solution(6507690274980863217)
XLA Ops:
  6.5 0.0 copy-start
  6.5 0.0 all-gather.4.cloned.1.call-start
  6.5 1.1 copy-done
  7.7 0.7 constant_dynamic-slice_fusion
  8.3 0.0 all-gather.4.cloned.1.call-update
  8.4 0.0 all-gather.6.cloned.1.call-start
  8.4 0.9 constant_dynamic-slice_fusion.1
  9.3 0.7 copy.14
  10.1 0.0 all-gather.6.cloned.1.call-update
  10.1 0.0 all-gather.8.cloned.1.call-start
  10.1 0.7 all-gather.8.cloned.1.call-update
  10.8 0.0 reduce-scatter.2.cloned.1.call-start
  10.9 0.8 reduce-window.8
  11.7 0.7 select_reduce_fusion.1
  12.5 0.1 convert_reduce_fusion.1
  12.6 0.9 select_reduce_fusion
  13.5 0.1 convert_reduce_fusion
  13.6 4.4 compare_and_fusion
  18.0 76.2 %all-gather.4.cloned.1.call-done = bf16[6144,128]{1,0:T(8,128)(2,1)} async-done(((bf16[384,128]{1,0:T(8,128)(2,1)}), bf16[6144,128]{1,0:T(8,128)(2,1)}) %all-gather.4.cloned.1.call-update) | async-done | bytes 1572880 | tf_op jit(solution)/shard_map/all_gather | solution.py:38
  94.2 16.9 %fusion = (f32[4,384]{1,0:T(4,128)S(1)}, f32[6144,384,4]{1,0,2:T(8,128)}) fusion(pred[384,6144]{0,1:T(8,128)(4,1)S(1)} %compare_and_fusion, bf16[6144,128]{1,0:T(8,128)(2,1)} %all-gather.4.cloned.1.call-done, bf16[384,512]{1,0:T(8,128)(2,1)} %param.6), kind=kOutput, calls=%fused_computation.2 | convolution fusion | flops 2444229120 | bytes 42080256 | tf_op jit(solution)/shard_map/qkgd,nkd->kgqn/dot_general | solution.py:45
  111.1 16.8 %fusion.1 = f32[4,384]{1,0:T(4,128)S(1)} fusion(f32[6144,384,4]{1,0,2:T(8,128)} %get-tuple-element.6, f32[4,384]{1,0:T(4,128)S(1)} %broadcast_maximum_fusion, pred[384,6144]{0,1:T(8,128)(4,1)S(1)} %compare_and_fusion), kind=kLoop, calls=%fused_computation.3 | loop fusion | flops 47184384 | bytes 40120320 | tf_op jit(solution)/shard_map/reduce_sum | solution.py:56
  128.0 48.7 %all-gather.6.cloned.1.call-done = bf16[6144,128]{0,1:T(8,128)(2,1)} async-done(((bf16[384,128]{0,1:T(8,128)(2,1)}), bf16[6144,128]{0,1:T(8,128)(2,1)}) %all-gather.6.cloned.1.call-update) | async-done | bytes 1572880 | tf_op jit(solution)/shard_map/all_gather | solution.py:39
  176.6 15.8 %fusion.15 = bf16[4,384,128]{1,2,0:T(8,128)(2,1)S(1)} fusion(f32[6144,384,4]{1,0,2:T(8,128)} %get-tuple-element.6, f32[4,384]{1,0:T(4,128)S(1)} %broadcast_maximum_fusion, pred[384,6144]{0,1:T(8,128)(4,1)S(1)} %compare_and_fusion, bf16[6144,128]{0,1:T(8,128)(2,1)} %all-gather.6.cloned.1.call-done, f32[4,384]{1,0:T(4,128)S(1)} %fusion.1), kind=kOutput, calls=%fused_computation.14 | convolution fusion | flops 2463498240 | bytes 42086400 | tf_op jit(solution)/shard_map/kgqn,nkd->kgqd/dot_general | solution.py:57
  192.4 170.7 %all-gather.8.cloned.1.call-done = bf16[512,16384]{1,0:T(8,128)(2,1)} async-done(((bf16[512,1024]{1,0:T(8,128)(2,1)}), bf16[512,16384]{1,0:T(8,128)(2,1)}) %all-gather.8.cloned.1.call-update) | async-done | bytes 16777232 | tf_op jit(solution)/shard_map/all_gather | solution.py:70
  363.1 0.0 copy-start.1
  363.1 15.1 %convolution_convert_fusion = bf16[384,16384]{1,0:T(8,128)(2,1)} fusion(bf16[384,512]{0,1:T(8,128)(2,1)S(1)} %bitcast.56, bf16[512,16384]{1,0:T(8,128)(2,1)} %all-gather.8.cloned.1.call-done), kind=kOutput, calls=%fused_computation.5 | convolution fusion | flops 6448742400 | bytes 29753344 | tf_op jit(solution)/shard_map/dot_general | solution.py:72
  378.3 0.0 reduce-scatter.2.cloned.1.call-update
  378.3 173.1 %reduce-scatter.2.cloned.1.call-done = bf16[24,16384]{1,0:T(8,128)(2,1)} async-done(((bf16[384,16384]{1,0:T(8,128)(2,1)}), bf16[24,16384]{1,0:T(8,128)(2,1)}) %reduce-scatter.2.cloned.1.call-update) | async-done | bytes 786448 | tf_op jit(solution)/shard_map/reduce_scatter | solution.py:71
  551.4 0.0 copy-done.1
  (5 shorter events, 0.1 us)
Async XLA Ops:
  6.5 1.1 copy-start
  6.5 87.7 %all-gather.4.cloned.1.call-start = ((), (), s32[]{:S(2)}) async-start(), calls=%async_computation.1 | async-start | bytes 1671168 | tf_op jit(solution)/shard_map/all_gather | solution.py:38
  8.4 168.3 %all-gather.6.cloned.1.call-start = ((), (), s32[]{:S(2)}) async-start(), calls=%async_computation.2 | async-start | bytes 1671168 | tf_op jit(solution)/shard_map/all_gather | solution.py:39
  10.1 353.1 %all-gather.8.cloned.1.call-start = ((), (), s32[]{:S(2)}) async-start(), calls=%async_computation.3 | async-start | bytes 17825792 | tf_op jit(solution)/shard_map/all_gather | solution.py:70
  10.8 540.6 %reduce-scatter.2.cloned.1.call-start = ((), (), s32[]{:S(2)}) async-start(), calls=%async_computation.4 | async-start | bytes 13369344 | tf_op jit(solution)/shard_map/reduce_scatter | solution.py:71
  363.1 188.3 %copy-start.1 = (bf16[384,1024]{1,0:T(8,128)(2,1)S(1)}, bf16[384,1024]{1,0:T(8,128)(2,1)}, u32[]{:S(2)}) copy-start(bf16[384,1024]{1,0:T(8,128)(2,1)} %param.7) | copy-start | bytes 2359300
Sparse Core Ops, SparseCore 0:
  9.1 85.0 all-gather.3
  96.0 80.5 all-gather.5
  178.4 184.6 all-gather.7
  378.4 172.9 reduce-scatter.1
where the time goes:
time: 559 us; the launch traced here: 558 us
  waiting for transfers between devices  469 us (84%)
  matrix products  47.8 us (9%)
  other arithmetic  24 us (4%)
  between operations  13.2 us (2%)
    reduce_scatter x1, waiting for transfers between devices, local(): lax.psum_scatter(jnp.dot(attended, full_weight, preferred_element_type=jn...  173 us
    all_gather x1, waiting for transfers between devices, local(): full_weight = lax.all_gather(out_weight, 'ctx', axis=1, tiled=True)  171 us
    all_gather x1, waiting for transfers between devices, local(): key_piece = lax.all_gather(key_local, 'ctx', axis=0, tiled=True)  76.2 us
    all_gather x1, waiting for transfers between devices, local(): value_piece = lax.all_gather(value_local, 'ctx', axis=0, tiled=True)  48.7 us
    dot_general x1, matrix products, local(): jnp.einsum('qkgd,nkd->kgqn', grouped, key_piece.reshape(row_count, kv_loc...  16.9 us
    reduce_sum x1, other arithmetic, local(): denominator = jnp.sum(weights, axis=-1)  16.8 us
    dot_general x1, matrix products, local(): jnp.einsum('kgqn,nkd->kgqd', weights.astype(jnp.bfloat16), value_piece.re...  15.8 us
    dot_general x1, matrix products, local(): jnp.dot(attended, full_weight, preferred_element_type=jnp.float32)  15.1 us
  transfers between devices with their start and end apart: 4, of which 4 were waited for; matrix products, arithmetic and copies ran while one was open for 10% of the time, Pallas kernels for 0%

commit v1 on v0

v1 whole, which is shorter than its diff:
```python
import functools

import jax
import jax.numpy as jnp
from jax import lax
from jax.experimental import pallas as pl
from jax.experimental.pallas import tpu as pltpu
from jax.sharding import PartitionSpec as P

HD = 128
BLK = 192
TILE = 384
HEADS = 4
NZ, NX, NY = 8, 4, 4
SCALE = HD ** (-0.5) * 1.4426950408889634
LOW = -1e30


def flat(z, x, y, c):
    return ((z % 4) * 4 + x) * 16 + y * 4 + (z // 4) * 2 + c


def perm(dz=0, dx=0, dy=0, dc=0):
    pairs = []
    for z in range(NZ):
        for x in range(NX):
            for y in range(NY):
                for c in range(2):
                    to = flat((z + dz) % NZ, (x + dx) % NX, (y + dy) % NY, (c + dc) % 2)
                    pairs.append((flat(z, x, y, c), to))
    return pairs


def send(a, **step):
    return lax.ppermute(a, ("ctx", "tp"), perm(**step))


def attend_kernel(meta, q_ref, mine_ref, theirs_ref, o_ref, ks, vs, m_s, l_s, acc_s):
    ctx = meta[36]
    core = meta[37]
    ks[0:BLK, :] = jnp.zeros((BLK, HD), ks.dtype)
    vs[0:BLK, :] = jnp.zeros((BLK, HD), vs.dtype)

    def place(k_from, v_from):
        for slot in range(16):
            owner = meta[38 + slot]
            for i in range(2):
                at = pl.multiple_of((meta[2 * owner + i] + 1) * BLK, BLK)
                ks[pl.ds(at, BLK), :] = k_from[slot, i * BLK:(i + 1) * BLK, :]
                vs[pl.ds(at, BLK), :] = v_from[slot, i * BLK:(i + 1) * BLK, :]

    @pl.when(core == 0)
    def _():
        place(mine_ref, theirs_ref)

    @pl.when(core != 0)
    def _():
        place(theirs_ref, mine_ref)

    end1 = meta[32]
    end2 = end1 + meta[33]
    end3 = end2 + meta[34]

    def start_of(pos):
        s = jnp.where(pos >= end1, end1, 0)
        s = jnp.where(pos >= end2, end2, s)
        return jnp.where(pos >= end3, end3, s)

    for i in range(2):
        base = meta[2 * ctx + i] * BLK
        top = base + BLK
        low_first = start_of(base)
        low_last = start_of(base + BLK - 1)
        row_pos = base + lax.broadcasted_iota(jnp.int32, (BLK, 1), 0)
        row_start = start_of(row_pos)
        rows = slice(i * BLK, (i + 1) * BLK)

        def scores(t, h, kind):
            first = top - (t + 1) * TILE
            at = pl.multiple_of(first + BLK, BLK)
            k = ks[pl.ds(at, TILE), :]
            s = lax.dot_general(
                q_ref[rows, h * HD:(h + 1) * HD], k, (((1,), (1,)), ((), ())),
                preferred_element_type=jnp.float32,
            ) * SCALE
            if kind != "inner":
                col = first + lax.broadcasted_iota(jnp.int32, (BLK, TILE), 1)
                ok = col >= row_start
                if kind == "diagonal":
                    ok = ok & (col <= row_pos)
                s = jnp.where(ok, s, LOW)
            return s, vs[pl.ds(at, TILE), :]

        for h in range(HEADS):
            s, v = scores(0, h, "diagonal")
            peak = jnp.max(s, axis=1, keepdims=True)
            p = jnp.exp2(s - peak)
            m_s[h] = peak
            l_s[h] = jnp.sum(p, axis=1, keepdims=True)
            acc_s[h] = jnp.dot(p.astype(jnp.bfloat16), v, preferred_element_type=jnp.float32)

        def step(t, kind):
            for h in range(HEADS):
                s, v = scores(t, h, kind)
                old = m_s[h]
                peak = jnp.maximum(old, jnp.max(s, axis=1, keepdims=True))
                fade = jnp.exp2(old - peak)
                p = jnp.exp2(s - peak)
                m_s[h] = peak
                l_s[h] = l_s[h] * fade + jnp.sum(p, axis=1, keepdims=True)
                acc_s[h] = acc_s[h] * fade + jnp.dot(
                    p.astype(jnp.bfloat16), v, preferred_element_type=jnp.float32
                )

        inner = jnp.maximum(1, (top - low_last) // TILE)
        total = (top - low_first + TILE - 1) // TILE

        @pl.loop(1, inner)
        def _(t):
            step(t, "inner")

        @pl.loop(inner, total)
        def _(t):
            step(t, "edge")

        for h in range(HEADS):
            o_ref[rows, h * HD:(h + 1) * HD] = (acc_s[h] / l_s[h]).astype(jnp.bfloat16)


def attend(meta, q, mine, theirs):
    return pl.pallas_call(
        attend_kernel,
        out_shape=jax.ShapeDtypeStruct((2 * BLK, HEADS * HD), jnp.bfloat16),
        in_specs=[pl.BlockSpec(memory_space=pltpu.SMEM)] + [pl.BlockSpec(memory_space=pltpu.VMEM)] * 3,
        out_specs=pl.BlockSpec(memory_space=pltpu.VMEM),
        scratch_shapes=[
            pltpu.VMEM((33 * BLK, HD), jnp.bfloat16),
            pltpu.VMEM((33 * BLK, HD), jnp.bfloat16),
            pltpu.VMEM((HEADS, BLK, 1), jnp.float32),
            pltpu.VMEM((HEADS, BLK, 1), jnp.float32),
            pltpu.VMEM((HEADS, BLK, HD), jnp.float32),
        ],
        compiler_params=pltpu.CompilerParams(vmem_limit_bytes=32 * 2**20),
        cost_estimate=pl.CostEstimate(flops=4 * 10**9, bytes_accessed=4 * 10**6, transcendentals=3 * 10**6),
        name="attend",
    )(meta, q, mine, theirs)


def project_kernel(es, meta, *refs):
    n = len(es)
    a_refs = refs[:2 * n]
    w_own, w_oth = refs[2 * n:2 * n + 2]
    outs = refs[2 * n + 2:2 * n + 6]
    total = refs[2 * n + 6]
    zl, y = meta[0], meta[1]
    for j, e in enumerate(es):
        left, right = a_refs[2 * j], a_refs[2 * j + 1]

        def put(own, oth):
            t = jnp.dot(own[0], w_own[0, 0], preferred_element_type=jnp.float32)
            t += jnp.dot(own[1], w_oth[0, 0], preferred_element_type=jnp.float32)
            t += jnp.dot(oth[0], w_own[0, 1], preferred_element_type=jnp.float32)
            t += jnp.dot(oth[1], w_oth[0, 1], preferred_element_type=jnp.float32)
            total[...] = t

        if e == 0:
            put(left, right)
        else:
            @pl.when(zl + e < 4)
            def _():
                put(left, right)

            @pl.when(zl + e >= 4)
            def _():
                put(right, left)

        for k in range(4):
            at = pl.multiple_of(lax.rem(y + k, 4) * 48, 48)
            outs[k][j] = total[pl.ds(at, 48), :].astype(jnp.bfloat16)


def project(es, meta, pairs, w_own, w_oth):
    n = len(es)
    a_list = [a for pair in pairs for a in pair]
    whole = pl.BlockSpec((2, 192, 512), lambda i: (0, 0, 0))
    w_spec = pl.BlockSpec((1, 2, 512, 512), lambda i: (i, 0, 0, 0))
    return pl.pallas_call(
        functools.partial(project_kernel, es),
        grid=(4,),
        out_shape=[jax.ShapeDtypeStruct((n, 48, 2048), jnp.bfloat16)] * 4,
        in_specs=[pl.BlockSpec(memory_space=pltpu.SMEM)] + [whole] * (2 * n) + [w_spec] * 2,
        out_specs=[pl.BlockSpec((n, 48, 512), lambda i: (0, 0, i))] * 4,
        scratch_shapes=[pltpu.VMEM((192, 512), jnp.float32)],
        compiler_params=pltpu.CompilerParams(vmem_limit_bytes=32 * 2**20),
        cost_estimate=pl.CostEstimate(flops=n * 2 * 192 * 2048 * 2048, bytes_accessed=10**7, transcendentals=0),
        name="project",
    )(meta, *a_list, w_own, w_oth)


def assemble_kernel(meta, *refs):
    out = refs[8]
    z = meta[2]
    for d in range(8):
        src = lax.rem(z + d, 8)
        for x in range(4):
            at = pl.multiple_of((lax.rem(src, 4) * 4 + x) * 1024 + (src // 4) * 512, 512)
            out[:, pl.ds(at, 512)] = refs[d][:, x * 512:(x + 1) * 512]


def assemble(meta, pieces):
    return pl.pallas_call(
        assemble_kernel,
        out_shape=jax.ShapeDtypeStruct((24, 16384), jnp.bfloat16),
        in_specs=[pl.BlockSpec(memory_space=pltpu.SMEM)] + [pl.BlockSpec(memory_space=pltpu.VMEM)] * 8,
        out_specs=pl.BlockSpec(memory_space=pltpu.VMEM),
        name="assemble",
    )(meta, *pieces)


def local(query_rows, key_rows, value_rows, out_weight, block_order, doc_lengths):
    ctx = lax.axis_index("ctx")
    tp = lax.axis_index("tp")
    zl, x = ctx // 4, ctx % 4
    y, zh, core = tp // 4, (tp // 2) % 2, tp % 2
    z = zh * 4 + zl

    def shard_for(zh_to):
        at = (y * 2 + zh_to) * HD
        k = lax.dynamic_slice_in_dim(key_rows, at, HD, 1)
        v = lax.dynamic_slice_in_dim(value_rows, at, HD, 1)
        return jnp.where(core == 0, k, v)

    with jax.named_scope("kv"):
        near = [shard_for(((z + d) % 8) // 4) for d in (0, 1, 7, 2)]
        four = jnp.stack([near[0], send(near[1], dz=1), send(near[2], dz=-1), send(near[3], dz=2)])
        up, down, far = send(four, dx=1), send(four, dx=-1), send(four, dx=2)
        mine = jnp.concatenate([four, up, down, far])
        theirs = send(mine, dc=1)
        steps = [(a, b) for b in (0, -1, 1, 2) for a in (0, -1, 1, 2)]
        owners = [((zl + a + 4) % 4) * 4 + (x + b + 4) % 4 for a, b in steps]
        meta = jnp.concatenate([
            block_order.astype(jnp.int32), doc_lengths.astype(jnp.int32),
            jnp.stack([ctx, core] + owners).astype(jnp.int32),
        ])

    with jax.named_scope("weights"):
        w_keep = lax.dynamic_slice_in_dim(out_weight, zh * 512, 512, 1)
        w_give = lax.dynamic_slice_in_dim(out_weight, (1 - zh) * 512, 512, 1)
        w_pair = jnp.stack([w_keep, send(w_give, dz=4)])
        groups = [[g * 4 + i for i in range(4)] for g in range(4)]
        w_own = lax.all_gather(w_pair, "ctx", axis_index_groups=groups, axis=0, tiled=False)
        w_oth = send(w_own, dc=1)

    with jax.named_scope("attend"):
        attended = attend(meta, query_rows, mine, theirs)

    with jax.named_scope("rows"):
        split = attended.reshape(8, 2, 24, 512)
        keep = lax.dynamic_index_in_dim(split, core, 1, keepdims=False).reshape(192, 512)
        give = lax.dynamic_index_in_dim(split, 1 - core, 1, keepdims=False).reshape(192, 512)
        a0 = jnp.stack([keep, send(give, dc=1)])
        right, left = [a0], [a0]
        for _ in range(3):
            right.append(send(right[-1], dz=1))
            left.append(send(left[-1], dz=-1))
        opposite = jnp.stack([send(right[3][0], dz=1), send(left[3][1], dz=-1)])
        right.append(opposite)
        left.append(opposite)

    where = jnp.stack([zl, y, z]).astype(jnp.int32)
    pieces = [None] * 8
    for es in ((2,), (1, 3), (0,)):
        with jax.named_scope("project"):
            pairs = [(left[e], right[4 - e]) for e in es]
            o = project(es, where, pairs, w_own, w_oth)
        with jax.named_scope("sum"):
            got = [o[0], send(o[1], dy=1), send(o[3], dy=-1), send(o[2], dy=2)]
            summed = sum(g.astype(jnp.float32) for g in got).astype(jnp.bfloat16)
        with jax.named_scope("home"):
            for j, e in enumerate(es):
                part = summed[j].reshape(2, 24, 2048)
                sel = ((z + e) % 8) // 4
                near_part = lax.dynamic_index_in_dim(part, sel, 0, keepdims=False)
                far_part = lax.dynamic_index_in_dim(part, 1 - sel, 0, keepdims=False)
                pieces[(8 - e) % 8] = near_part if e == 0 else send(near_part, dz=e)
                pieces[(12 - e) % 8] = send(far_part, dz=e - 4)
    return assemble(where, pieces)


def solution(mesh):
    in_specs = (P("ctx", "tp"), P("ctx", None), P("ctx", None), P("tp", "ctx"), P(), P())
    out_specs = P(("ctx", "tp"), None)
    return jax.shard_map(local, mesh=mesh, in_specs=in_specs, out_specs=out_specs, check_vma=False)
```

time: 559 us -> 241 us (0.43)
  waiting for transfers between devices: 469 us -> 118 us
  starting transfers between devices: 0.12 us -> 63 us
  matrix products: 47.8 us -> 0 us
  Pallas kernels: 0 us -> 33.1 us
  other arithmetic: 24 us -> 3.77 us
    all_gather x3 -> x1, waiting for transfers between devices: 296 us -> 16.4 us  [local(): lax.all_gather(w_pair, 'ctx', axis_index_groups=groups, axis=0, tiled=False)]
    reduce_scatter x1 -> x0, waiting for transfers between devices: 173 us -> none  [local(): lax.psum_scatter(jnp.dot(attended, full_weight, preferred_element_type=jn...]
    ppermute x0 -> x34, waiting for transfers between devices: none -> 102 us  [send(): return lax.ppermute(a, ('ctx', 'tp'), perm(**step))]
    ppermute x0 -> x34, starting transfers between devices: none -> 63 us  [send(): return lax.ppermute(a, ('ctx', 'tp'), perm(**step))]
    dot_general x3 -> x0, matrix products: 47.8 us -> none  [the longest x1 16.9 us: local(): jnp.einsum('qkgd,nkd->kgqn', grouped, key_piece.reshape(row_count, kv_loc...]
    pallas_call x0 -> x5, Pallas kernels: none -> 33.1 us  [the longest x1 15.7 us: attend(): pl.pallas_call(attend_kernel, out_shape=jax.ShapeDtypeStruct((2 * BLK, HE...]
    reduce_sum x5 -> x0, other arithmetic: 18.7 us -> none  [the longest x1 16.8 us: local(): denominator = jnp.sum(weights, axis=-1)]
  transfers between devices with their start and end apart: 4 -> 35, of which waited for: 4 -> 21; matrix products, arithmetic and copies ran while one was open for 10% -> 2% of each run, Pallas kernels for 0% -> 11%
where the time goes in v1:
time: 241 us; the launch traced here: 237 us
  waiting for transfers between devices  118 us (49%)
  starting transfers between devices  63 us (26%)
  Pallas kernels  33.1 us (14%)
  between operations  14 us (6%)
  local copies, waits for them, and re-layouts  5.36 us (2%)
  other arithmetic  3.77 us (2%)
    ppermute x34, waiting for transfers between devices, send(): return lax.ppermute(a, ('ctx', 'tp'), perm(**step))  102 us
    ppermute x34, starting transfers between devices, send(): return lax.ppermute(a, ('ctx', 'tp'), perm(**step))  63 us
    all_gather x1, waiting for transfers between devices, local(): lax.all_gather(w_pair, 'ctx', axis_index_groups=groups, axis=0, tiled=False)  16.4 us
    pallas_call x1, Pallas kernels, attend(): pl.pallas_call(attend_kernel, out_shape=jax.ShapeDtypeStruct((2 * BLK, HE...  15.7 us
    pallas_call x3, Pallas kernels, project(): pl.pallas_call(functools.partial(project_kernel, es), grid=(4,), out_shap...  15.2 us
  transfers between devices with their start and end apart: 35, of which 21 were waited for; matrix products, arithmetic and copies ran while one was open for 2% of the time, Pallas kernels for 11%

profile of v1, /device:TPU:8, one launch (start us, length us, event | category | flops | bytes accessed | tf_op | source)
XLA Modules:
  0.0 237.4 jit_solution(9323341949503331515)
XLA Ops:
  6.5 1.3 dynamic-slice_bitcast_fusion
  7.8 7.3 %collective-permute-start.16 = (bf16[512,512]{1,0:T(8,128)(2,1)S(1)}, bf16[512,512]{1,0:T(8,128)(2,1)S(1)}, u32[]{:S(2)}, u32[]{:S(2)}) collective-permute-start(bf16[512,512]{1,0:T(8,128)(2,1)S(1)} %get-tuple-element.35), channel_id=1, source_target_pairs={{0,2},{1,3},{4,6},{5,7},{8,10},{9,11},{12,14},{13,15},{16,18},{17,... | collective-permute-start | bytes 1572872 | tf_op jit(solution)/shard_map/weights/ppermute | solution.py:35
  15.1 14.2 %collective-permute-done.16 = bf16[512,512]{1,0:T(8,128)(2,1)S(1)} collective-permute-done((bf16[512,512]{1,0:T(8,128)(2,1)S(1)}, bf16[512,512]{1,0:T(8,128)(2,1)S(1)}, u32[]{:S(2)}, u32[]{:S(2)}) %collective-permute-start.16) | collective-permute-done | bytes 524320 | tf_op jit(solution)/shard_map/weights/ppermute | solution.py:35
  29.3 1.1 pad_maximum_fusion
  30.6 0.1 copy-done.3
  30.7 1.1 dynamic-slice_select_fusion
  31.8 10.3 %collective-permute-start = (bf16[384,128]{1,0:T(8,128)(2,1)S(1)}, bf16[384,128]{1,0:T(8,128)(2,1)S(1)}, u32[]{:S(2)}, u32[]{:S(2)}) collective-permute-start(bf16[384,128]{1,0:T(8,128)(2,1)S(1)} %get-tuple-element.32), channel_id=1, source_target_pairs={{0,64},{1,65},{4,68},{5,69},{8,72},{9,73},{12,76},{13,77},{16,80},... | collective-permute-start | bytes 294920 | tf_op jit(solution)/shard_map/kv/ppermute | solution.py:35
  42.1 2.7 %collective-permute-start.2 = (bf16[384,128]{1,0:T(8,128)(2,1)S(1)}, bf16[384,128]{1,0:T(8,128)(2,1)S(1)}, u32[]{:S(2)}, u32[]{:S(2)}) collective-permute-start(bf16[384,128]{1,0:T(8,128)(2,1)S(1)} %get-tuple-element.31), channel_id=1, source_target_pairs={{0,128},{1,129},{4,132},{5,133},{8,136},{9,137},{12,140},{13,141},... | collective-permute-start | bytes 294920 | tf_op jit(solution)/shard_map/kv/ppermute | solution.py:35
  44.8 0.9 constant_dynamic-update-slice_fusion.6
  45.7 1.0 collective-permute-done.1
  46.7 4.4 %collective-permute-done.2 = bf16[384,128]{1,0:T(8,128)(2,1)S(1)} collective-permute-done((bf16[384,128]{1,0:T(8,128)(2,1)S(1)}, bf16[384,128]{1,0:T(8,128)(2,1)S(1)}, u32[]{:S(2)}, u32[]{:S(2)}) %collective-permute-start.2) | collective-permute-done | bytes 98336 | tf_op jit(solution)/shard_map/kv/ppermute | solution.py:35
  51.2 1.6 collective-permute-start.3
  52.7 1.7 collective-permute-start.4
  54.5 1.8 collective-permute-start.5
  56.4 14.9 %collective-permute-done.3 = bf16[4,384,128]{2,1,0:T(8,128)(2,1)S(1)} collective-permute-done((bf16[4,384,128]{2,1,0:T(8,128)(2,1)S(1)}, bf16[4,384,128]{2,1,0:T(8,128)(2,1)S(1)}, u32[]{:S(2)}, u32[]{:S(2)}) %collective-permute-start.3) | collective-permute-done | bytes 393248 | tf_op jit(solution)/shard_map/kv/ppermute | solution.py:35
  71.4 1.7 collective-permute-done.4
  73.1 14.8 %collective-permute-done.5 = bf16[4,384,128]{2,1,0:T(8,128)(2,1)S(1)} collective-permute-done((bf16[4,384,128]{2,1,0:T(8,128)(2,1)S(1)}, bf16[4,384,128]{2,1,0:T(8,128)(2,1)S(1)}, u32[]{:S(2)}, u32[]{:S(2)}) %collective-permute-start.5) | collective-permute-done | bytes 393248 | tf_op jit(solution)/shard_map/kv/ppermute | solution.py:35
  88.0 0.1 collective-permute-start.6
  88.1 16.4 %all-gather.3.cloned.1.call-done = bf16[8,512,512]{2,1,0:T(8,128)(2,1)} async-done(((bf16[2,512,512]{2,1,0:T(8,128)(2,1)}), bf16[8,512,512]{2,1,0:T(8,128)(2,1)}) %all-gather.3.cloned.1.call-update) | async-done | bytes 4194320 | tf_op jit(solution)/shard_map/weights/all_gather | solution.py:251
  104.6 0.1 concatenate.7.meta
  104.7 15.7 %attend.1 = bf16[384,512]{1,0:T(8,128)(2,1)S(1)} custom-call(s32[54]{0:T(128)S(1)} %concatenate.7.meta, bf16[384,512]{1,0:T(8,128)(2,1)S(1)} %copy-done.2, bf16[16,384,128]{2,1,0:T(8,128)(2,1)S(1)} %constant_dynamic-update-slice_fusion.mine_ref, bf16[16,384,128]{2,1,0:T(8,128)(2,1)S(1)} %collective-permute-done.6.theirs_ref), custom_call_target="tpu_custom_call" | custom-call | flops 4000000000 | bytes 4000000 | tf_op jit(solution)/shard_map/attend/attend/pallas_call | solution.py:131
  120.5 0.5 collective-permute-start.7
  121.0 1.1 collective-permute-done.7
  122.1 0.7 collective-permute-start.12
  122.8 1.8 collective-permute-start.8
  124.6 9.5 %collective-permute-done.12.refs_0_ = bf16[2,192,512]{2,1,0:T(8,128)(2,1)S(1)} collective-permute-done((bf16[2,192,512]{2,1,0:T(8,128)(2,1)S(1)}, bf16[2,192,512]{2,1,0:T(8,128)(2,1)S(1)}, u32[]{:S(2)}, u32[]{:S(2)}) %collective-permute-start.12) | collective-permute-done | bytes 393248 | tf_op jit(solution)/shard_map/rows/ppermute | solution.py:35
  134.1 1.2 collective-permute-start.13
  135.4 0.8 collective-permute-start.9
  136.2 8.8 %collective-permute-done.13.refs_0_ = bf16[2,192,512]{2,1,0:T(8,128)(2,1)S(1)} collective-permute-done((bf16[2,192,512]{2,1,0:T(8,128)(2,1)S(1)}, bf16[2,192,512]{2,1,0:T(8,128)(2,1)S(1)}, u32[]{:S(2)}, u32[]{:S(2)}) %collective-permute-start.13) | collective-permute-done | bytes 393248 | tf_op jit(solution)/shard_map/rows/ppermute | solution.py:35
  145.0 3.0 %collective-permute-start.14 = (bf16[2,192,512]{2,1,0:T(8,128)(2,1)S(1)}, bf16[2,192,512]{2,1,0:T(8,128)(2,1)S(1)}, u32[]{:S(2)}, u32[]{:S(2)}) collective-permute-start(bf16[2,192,512]{2,1,0:T(8,128)(2,1)S(1)} %collective-permute-done.13.refs_0_), channel_id=1, source_target_pairs={{0,194},{1,195},{4,198},{5,199},{8,202},{9,203},{12,206},{13,207},... | collective-permute-start | bytes 1179656 | tf_op jit(solution)/shard_map/rows/ppermute | solution.py:35
  147.9 1.2 collective-permute-done.9.refs_1_
  149.1 6.0 %collective-permute-done.14.refs_2_ = bf16[2,192,512]{2,1,0:T(8,128)(2,1)S(1)} collective-permute-done((bf16[2,192,512]{2,1,0:T(8,128)(2,1)S(1)}, bf16[2,192,512]{2,1,0:T(8,128)(2,1)S(1)}, u32[]{:S(2)}, u32[]{:S(2)}) %collective-permute-start.14) | collective-permute-done | bytes 393248 | tf_op jit(solution)/shard_map/rows/ppermute | solution.py:35
  155.1 3.8 %collective-permute-start.15 = (bf16[192,512]{1,0:T(8,128)(2,1)S(1)}, bf16[192,512]{1,0:T(8,128)(2,1)S(1)}, u32[]{:S(2)}, u32[]{:S(2)}) collective-permute-start(bf16[192,512]{1,0:T(8,128)(2,1)S(1)} %slice_bitcast_fusion), channel_id=1, source_target_pairs={{0,194},{1,195},{4,198},{5,199},{8,202},{9,203},{12,206},{13,207},... | collective-permute-start | bytes 589832 | tf_op jit(solution)/shard_map/rows/ppermute | solution.py:35
  158.9 1.4 collective-permute-done.10.refs_1_
  160.3 0.1 collective-permute-start.11
  160.6 1.5 collective-permute-done.15
  162.1 5.2 %collective-permute-done.11 = bf16[192,512]{1,0:T(8,128)(2,1)S(1)} collective-permute-done((bf16[192,512]{1,0:T(8,128)(2,1)S(1)}, bf16[192,512]{1,0:T(8,128)(2,1)S(1)}, u32[]{:S(2)}, u32[]{:S(2)}) %collective-permute-start.11) | collective-permute-done | bytes 196640 | tf_op jit(solution)/shard_map/rows/ppermute | solution.py:35
  167.4 2.2 copy-done
  169.6 4.5 %project.3 = (bf16[1,48,2048]{2,1,0:T(8,128)(2,1)S(1)}, bf16[1,48,2048]{2,1,0:T(8,128)(2,1)S(1)}, bf16[1,48,2048]{2,1,0:T(8,128)(2,1)S(1)}, bf16[1,48,2048]{2,1,0:T(8,128)(2,1)S(1)}) custom-call(s32[3]{0:T(128)S(1)} %pad_add_fusion.meta, bf16[2,192,512]{2,1,0:T(8,128)(2,1)S(1)} %pad_maximum_fusion.2.refs_0_, ...), custom_call_target="tpu_custom_call" | custom-call | flops 1610612736 | bytes 10000000 | tf_op jit(solution)/shard_map/project/project/pallas_call | solution.py:187
  174.0 2.4 %collective-permute-start.20 = (bf16[1,48,2048]{2,1,0:T(8,128)(2,1)S(1)}, bf16[1,48,2048]{2,1,0:T(8,128)(2,1)S(1)}, u32[]{:S(2)}, u32[]{:S(2)}) collective-permute-start(bf16[1,48,2048]{2,1,0:T(8,128)(2,1)S(1)} %get-tuple-element.20), channel_id=1, source_target_pairs={{0,8},{1,9},{4,12},{5,13},{8,0},{9,1},{12,4},{13,5},{16,24},{17,25... | collective-permute-start | bytes 589832 | tf_op jit(solution)/shard_map/sum/ppermute | solution.py:35
  176.4 1.3 collective-permute-start.19
  177.8 4.5 %project.5 = (bf16[1,48,2048]{2,1,0:T(8,128)(2,1)S(1)}, bf16[1,48,2048]{2,1,0:T(8,128)(2,1)S(1)}, bf16[1,48,2048]{2,1,0:T(8,128)(2,1)S(1)}, bf16[1,48,2048]{2,1,0:T(8,128)(2,1)S(1)}) custom-call(s32[3]{0:T(128)S(1)} %pad_add_fusion.meta, bf16[2,192,512]{2,1,0:T(8,128)(2,1)S(1)} %collective-permute-done.13.refs_0_, ...), custom_call_target="tpu_custom_call" | custom-call | flops 1610612736 | bytes 10000000 | tf_op jit(solution)/shard_map/project/project/pallas_call | solution.py:187
  182.2 0.1 collective-permute-start.27
  182.3 2.7 %collective-permute-start.26 = (bf16[1,48,2048]{2,1,0:T(8,128)(2,1)S(1)}, bf16[1,48,2048]{2,1,0:T(8,128)(2,1)S(1)}, u32[]{:S(2)}, u32[]{:S(2)}) collective-permute-start(bf16[1,48,2048]{2,1,0:T(8,128)(2,1)S(1)} %get-tuple-element.27), channel_id=1, source_target_pairs={{0,12},{1,13},{4,0},{5,1},{8,4},{9,5},{12,8},{13,9},{16,28},{17,29... | collective-permute-start | bytes 589832 | tf_op jit(solution)/shard_map/sum/ppermute | solution.py:35
  185.1 6.2 %project.4 = (bf16[2,48,2048]{2,1,0:T(8,128)(2,1)S(1)}, bf16[2,48,2048]{2,1,0:T(8,128)(2,1)S(1)}, bf16[2,48,2048]{2,1,0:T(8,128)(2,1)S(1)}, bf16[2,48,2048]{2,1,0:T(8,128)(2,1)S(1)}) custom-call(s32[3]{0:T(128)S(1)} %pad_add_fusion.meta, bf16[2,192,512]{2,1,0:T(8,128)(2,1)S(1)} %collective-permute-done.12.refs_0_, ...), custom_call_target="tpu_custom_call" | custom-call | flops 3221225472 | bytes 10000000 | tf_op jit(solution)/shard_map/project/project/pallas_call | solution.py:187
  191.3 1.9 collective-permute-start.18
  193.2 2.3 collective-permute-start.23
  195.6 2.5 %collective-permute-start.22 = (bf16[2,48,2048]{2,1,0:T(8,128)(2,1)S(1)}, bf16[2,48,2048]{2,1,0:T(8,128)(2,1)S(1)}, u32[]{:S(2)}, u32[]{:S(2)}) collective-permute-start(bf16[2,48,2048]{2,1,0:T(8,128)(2,1)S(1)} %get-tuple-element.23), channel_id=1, source_target_pairs={{0,12},{1,13},{4,0},{5,1},{8,4},{9,5},{12,8},{13,9},{16,28},{17,29... | collective-permute-start | bytes 1179656 | tf_op jit(solution)/shard_map/sum/ppermute | solution.py:35
  198.1 0.1 add_convert_fusion.1
  198.3 0.6 collective-permute-start.28
  199.0 4.5 %collective-permute-done.18 = bf16[1,48,2048]{2,1,0:T(8,128)(2,1)S(1)} collective-permute-done((bf16[1,48,2048]{2,1,0:T(8,128)(2,1)S(1)}, bf16[1,48,2048]{2,1,0:T(8,128)(2,1)S(1)}, u32[]{:S(2)}, u32[]{:S(2)}) %collective-permute-start.18) | collective-permute-done | bytes 196640 | tf_op jit(solution)/shard_map/sum/ppermute | solution.py:35
  203.5 0.1 add_convert_fusion.2
  203.6 0.7 dynamic-slice_bitcast_fusion.4
  204.3 4.4 %collective-permute-start.30 = (bf16[24,2048]{1,0:T(8,128)(2,1)S(1)}, bf16[24,2048]{1,0:T(8,128)(2,1)S(1)}, u32[]{:S(2)}, u32[]{:S(2)}) collective-permute-start(bf16[24,2048]{1,0:T(8,128)(2,1)S(1)} %get-tuple-element.46), channel_id=1, source_target_pairs={{0,2},{1,3},{4,6},{5,7},{8,10},{9,11},{12,14},{13,15},{16,18},{17,... | collective-permute-start | bytes 294920 | tf_op jit(solution)/shard_map/home/ppermute | solution.py:35
  208.7 2.5 %collective-permute-done.22 = bf16[2,48,2048]{2,1,0:T(8,128)(2,1)S(1)} collective-permute-done((bf16[2,48,2048]{2,1,0:T(8,128)(2,1)S(1)}, bf16[2,48,2048]{2,1,0:T(8,128)(2,1)S(1)}, u32[]{:S(2)}, u32[]{:S(2)}) %collective-permute-start.22) | collective-permute-done | bytes 393248 | tf_op jit(solution)/shard_map/sum/ppermute | solution.py:35
  211.2 1.6 collective-permute-done.21
  212.9 0.2 add_convert_fusion
  213.3 5.1 %collective-permute-start.29 = (bf16[24,2048]{1,0:T(8,128)(2,1)S(1)}, bf16[24,2048]{1,0:T(8,128)(2,1)S(1)}, u32[]{:S(2)}, u32[]{:S(2)}) collective-permute-start(bf16[24,2048]{1,0:T(8,128)(2,1)S(1)} %get-tuple-element.41), channel_id=1, source_target_pairs={{0,66},{1,67},{4,70},{5,71},{8,74},{9,75},{12,78},{13,79},{16,82},... | collective-permute-start | bytes 294920 | tf_op jit(solution)/shard_map/home/ppermute | solution.py:35
  218.4 2.0 collective-permute-start.33
  220.4 1.1 collective-permute-done.24.refs_1_
  221.6 0.7 collective-permute-done.29.refs_3_
  222.3 5.4 %collective-permute-done.31.refs_5_ = bf16[24,2048]{1,0:T(8,128)(2,1)S(1)} collective-permute-done((bf16[24,2048]{1,0:T(8,128)(2,1)S(1)}, bf16[24,2048]{1,0:T(8,128)(2,1)S(1)}, u32[]{:S(2)}, u32[]{:S(2)}) %collective-permute-start.31) | collective-permute-done | bytes 98336 | tf_op jit(solution)/shard_map/home/ppermute | solution.py:35
  227.8 0.6 copy-done.9
  228.4 2.2 assemble.1
  (64 shorter events, 0.9 us)
Async XLA Ops:
  6.5 98.0 %all-gather.3.cloned.1.call-start = ((), (), s32[]{:S(2)}) async-start(), calls=%async_computation | async-start | bytes 5242880 | tf_op jit(solution)/shard_map/weights/all_gather | solution.py:251
  7.8 21.5 %collective-permute-start.16 = (bf16[512,512]{1,0:T(8,128)(2,1)S(1)}, bf16[512,512]{1,0:T(8,128)(2,1)S(1)}, u32[]{:S(2)}, u32[]{:S(2)}) collective-permute-start(bf16[512,512]{1,0:T(8,128)(2,1)S(1)} %get-tuple-element.35), channel_id=1, source_target_pairs={{0,2},{1,3},{4,6},{5,7},{8,10},{9,11},{12,14},{13,15},{16,18},{17,... | collective-permute-start | bytes 1572872 | tf_op jit(solution)/shard_map/weights/ppermute | solution.py:35
  29.3 1.4 copy-start.3
  31.8 13.9 %collective-permute-start = (bf16[384,128]{1,0:T(8,128)(2,1)S(1)}, bf16[384,128]{1,0:T(8,128)(2,1)S(1)}, u32[]{:S(2)}, u32[]{:S(2)}) collective-permute-start(bf16[384,128]{1,0:T(8,128)(2,1)S(1)} %get-tuple-element.32), channel_id=1, source_target_pairs={{0,64},{1,65},{4,68},{5,69},{8,72},{9,73},{12,76},{13,77},{16,80},... | collective-permute-start | bytes 294920 | tf_op jit(solution)/shard_map/kv/ppermute | solution.py:35
  42.1 4.6 %collective-permute-start.1 = (bf16[384,128]{1,0:T(8,128)(2,1)S(1)}, bf16[384,128]{1,0:T(8,128)(2,1)S(1)}, u32[]{:S(2)}, u32[]{:S(2)}) collective-permute-start(bf16[384,128]{1,0:T(8,128)(2,1)S(1)} %get-tuple-element.33), channel_id=1, source_target_pairs={{0,194},{1,195},{4,198},{5,199},{8,202},{9,203},{12,206},{13,207},... | collective-permute-start | bytes 294920 | tf_op jit(solution)/shard_map/kv/ppermute | solution.py:35
  42.1 9.1 %collective-permute-start.2 = (bf16[384,128]{1,0:T(8,128)(2,1)S(1)}, bf16[384,128]{1,0:T(8,128)(2,1)S(1)}, u32[]{:S(2)}, u32[]{:S(2)}) collective-permute-start(bf16[384,128]{1,0:T(8,128)(2,1)S(1)} %get-tuple-element.31), channel_id=1, source_target_pairs={{0,128},{1,129},{4,132},{5,133},{8,136},{9,137},{12,140},{13,141},... | collective-permute-start | bytes 294920 | tf_op jit(solution)/shard_map/kv/ppermute | solution.py:35
  51.2 20.2 %collective-permute-start.3 = (bf16[4,384,128]{2,1,0:T(8,128)(2,1)S(1)}, bf16[4,384,128]{2,1,0:T(8,128)(2,1)S(1)}, u32[]{:S(2)}, u32[]{:S(2)}) collective-permute-start(bf16[4,384,128]{2,1,0:T(8,128)(2,1)S(1)} %pad_maximum_fusion.1), channel_id=1, source_target_pairs={{0,16},{1,17},{4,20},{5,21},{8,24},{9,25},{12,28},{13,29},{16,32},... | collective-permute-start | bytes 1179656 | tf_op jit(solution)/shard_map/kv/ppermute | solution.py:35
  52.7 20.3 %collective-permute-start.4 = (bf16[4,384,128]{2,1,0:T(8,128)(2,1)S(1)}, bf16[4,384,128]{2,1,0:T(8,128)(2,1)S(1)}, u32[]{:S(2)}, u32[]{:S(2)}) collective-permute-start(bf16[4,384,128]{2,1,0:T(8,128)(2,1)S(1)} %pad_maximum_fusion.1), channel_id=1, source_target_pairs={{0,48},{1,49},{4,52},{5,53},{8,56},{9,57},{12,60},{13,61},{16,0},{... | collective-permute-start | bytes 1179656 | tf_op jit(solution)/shard_map/kv/ppermute | solution.py:35
  54.5 33.5 %collective-permute-start.5 = (bf16[4,384,128]{2,1,0:T(8,128)(2,1)S(1)}, bf16[4,384,128]{2,1,0:T(8,128)(2,1)S(1)}, u32[]{:S(2)}, u32[]{:S(2)}) collective-permute-start(bf16[4,384,128]{2,1,0:T(8,128)(2,1)S(1)} %pad_maximum_fusion.1), channel_id=1, source_target_pairs={{0,32},{1,33},{4,36},{5,37},{8,40},{9,41},{12,44},{13,45},{16,48},... | collective-permute-start | bytes 1179656 | tf_op jit(solution)/shard_map/kv/ppermute | solution.py:35
  56.3 48.3 %copy-start.11 = (s32[32]{0:T(128)S(1)}, s32[32]{0:T(128)}, u32[]{:S(2)}) copy-start(s32[32]{0:T(128)} %param.10) | copy-start | bytes 388
  56.3 48.3 %copy-start.12 = (s32[4]{0:T(128)S(1)}, s32[4]{0:T(128)}, u32[]{:S(2)}) copy-start(s32[4]{0:T(128)} %param.11) | copy-start | bytes 52
  56.3 48.4 %copy-start.2 = (bf16[384,512]{1,0:T(8,128)(2,1)S(1)}, bf16[384,512]{1,0:T(8,128)(2,1)}, u32[]{:S(2)}) copy-start(bf16[384,512]{1,0:T(8,128)(2,1)} %q_ref.1) | copy-start | bytes 1179652
  88.0 16.7 %collective-permute-start.6 = (bf16[16,384,128]{2,1,0:T(8,128)(2,1)S(1)}, bf16[16,384,128]{2,1,0:T(8,128)(2,1)S(1)}, u32[]{:S(2)}, u32[]{:S(2)}) collective-permute-start(bf16[16,384,128]{2,1,0:T(8,128)(2,1)S(1)} %constant_dynamic-update-slice_fusion.mine_ref), channel_id=1, source_target_pairs={{0,1},{1,0},{4,5},{5,4},{8,9},{9,8},{12,13},{13,12},{16,17},{17,16... | collective-permute-start | bytes 4718600 | tf_op jit(solution)/shard_map/kv/ppermute | solution.py:35
  104.5 62.8 %collective-permute-start.17 = (bf16[4,2,512,512]{3,2,1,0:T(8,128)(2,1)}, bf16[4,2,512,512]{3,2,1,0:T(8,128)(2,1)}, u32[]{:S(2)}, u32[]{:S(2)}) collective-permute-start(bf16[4,2,512,512]{3,2,1,0:T(8,128)(2,1)} %bitcast.68), channel_id=1, source_target_pairs={{0,1},{1,0},{4,5},{5,4},{8,9},{9,8},{12,13},{13,12},{16,17},{17,16... | collective-permute-start | bytes 12582920 | tf_op jit(solution)/shard_map/weights/ppermute | solution.py:35
  120.5 1.6 collective-permute-start.7
  122.1 12.0 %collective-permute-start.12 = (bf16[2,192,512]{2,1,0:T(8,128)(2,1)S(1)}, bf16[2,192,512]{2,1,0:T(8,128)(2,1)S(1)}, u32[]{:S(2)}, u32[]{:S(2)}) collective-permute-start(bf16[2,192,512]{2,1,0:T(8,128)(2,1)S(1)} %pad_maximum_fusion.2.refs_0_), channel_id=1, source_target_pairs={{0,194},{1,195},{4,198},{5,199},{8,202},{9,203},{12,206},{13,207},... | collective-permute-start | bytes 1179656 | tf_op jit(solution)/shard_map/rows/ppermute | solution.py:35
  122.8 12.6 %collective-permute-start.8 = (bf16[2,192,512]{2,1,0:T(8,128)(2,1)S(1)}, bf16[2,192,512]{2,1,0:T(8,128)(2,1)S(1)}, u32[]{:S(2)}, u32[]{:S(2)}) collective-permute-start(bf16[2,192,512]{2,1,0:T(8,128)(2,1)S(1)} %pad_maximum_fusion.2.refs_0_), channel_id=1, source_target_pairs={{0,64},{1,65},{4,68},{5,69},{8,72},{9,73},{12,76},{13,77},{16,80},... | collective-permute-start | bytes 1179656 | tf_op jit(solution)/shard_map/rows/ppermute | solution.py:35
  134.1 10.8 %collective-permute-start.13 = (bf16[2,192,512]{2,1,0:T(8,128)(2,1)S(1)}, bf16[2,192,512]{2,1,0:T(8,128)(2,1)S(1)}, u32[]{:S(2)}, u32[]{:S(2)}) collective-permute-start(bf16[2,192,512]{2,1,0:T(8,128)(2,1)S(1)} %collective-permute-done.12.refs_0_), channel_id=1, source_target_pairs={{0,194},{1,195},{4,198},{5,199},{8,202},{9,203},{12,206},{13,207},... | collective-permute-start | bytes 1179656 | tf_op jit(solution)/shard_map/rows/ppermute | solution.py:35
  135.4 13.8 %collective-permute-start.9 = (bf16[2,192,512]{2,1,0:T(8,128)(2,1)S(1)}, bf16[2,192,512]{2,1,0:T(8,128)(2,1)S(1)}, u32[]{:S(2)}, u32[]{:S(2)}) collective-permute-start(bf16[2,192,512]{2,1,0:T(8,128)(2,1)S(1)} %collective-permute-done.8.refs_3_), channel_id=1, source_target_pairs={{0,64},{1,65},{4,68},{5,69},{8,72},{9,73},{12,76},{13,77},{16,80},... | collective-permute-start | bytes 1179656 | tf_op jit(solution)/shard_map/rows/ppermute | solution.py:35
  145.0 10.2 %collective-permute-start.14 = (bf16[2,192,512]{2,1,0:T(8,128)(2,1)S(1)}, bf16[2,192,512]{2,1,0:T(8,128)(2,1)S(1)}, u32[]{:S(2)}, u32[]{:S(2)}) collective-permute-start(bf16[2,192,512]{2,1,0:T(8,128)(2,1)S(1)} %collective-permute-done.13.refs_0_), channel_id=1, source_target_pairs={{0,194},{1,195},{4,198},{5,199},{8,202},{9,203},{12,206},{13,207},... | collective-permute-start | bytes 1179656 | tf_op jit(solution)/shard_map/rows/ppermute | solution.py:35
  149.1 11.2 %collective-permute-start.10 = (bf16[2,192,512]{2,1,0:T(8,128)(2,1)S(1)}, bf16[2,192,512]{2,1,0:T(8,128)(2,1)S(1)}, u32[]{:S(2)}, u32[]{:S(2)}) collective-permute-start(bf16[2,192,512]{2,1,0:T(8,128)(2,1)S(1)} %collective-permute-done.9.refs_1_), channel_id=1, source_target_pairs={{0,64},{1,65},{4,68},{5,69},{8,72},{9,73},{12,76},{13,77},{16,80},... | collective-permute-start | bytes 1179656 | tf_op jit(solution)/shard_map/rows/ppermute | solution.py:35
  155.1 7.0 %collective-permute-start.15 = (bf16[192,512]{1,0:T(8,128)(2,1)S(1)}, bf16[192,512]{1,0:T(8,128)(2,1)S(1)}, u32[]{:S(2)}, u32[]{:S(2)}) collective-permute-start(bf16[192,512]{1,0:T(8,128)(2,1)S(1)} %slice_bitcast_fusion), channel_id=1, source_target_pairs={{0,194},{1,195},{4,198},{5,199},{8,202},{9,203},{12,206},{13,207},... | collective-permute-start | bytes 589832 | tf_op jit(solution)/shard_map/rows/ppermute | solution.py:35
  160.3 7.0 %collective-permute-start.11 = (bf16[192,512]{1,0:T(8,128)(2,1)S(1)}, bf16[192,512]{1,0:T(8,128)(2,1)S(1)}, u32[]{:S(2)}, u32[]{:S(2)}) collective-permute-start(bf16[192,512]{1,0:T(8,128)(2,1)S(1)} %slice_bitcast_fusion.1), channel_id=1, source_target_pairs={{0,64},{1,65},{4,68},{5,69},{8,72},{9,73},{12,76},{13,77},{16,80},... | collective-permute-start | bytes 589832 | tf_op jit(solution)/shard_map/rows/ppermute | solution.py:35
  160.6 24.5 %copy-start.1 = (s32[3]{0:T(128)}, s32[3]{0:T(128)S(1)}, u32[]{:S(2)}) copy-start(s32[3]{0:T(128)S(1)} %pad_add_fusion.meta) | copy-start | bytes 40
  167.4 2.2 copy-start
  174.0 24.2 %collective-permute-start.20 = (bf16[1,48,2048]{2,1,0:T(8,128)(2,1)S(1)}, bf16[1,48,2048]{2,1,0:T(8,128)(2,1)S(1)}, u32[]{:S(2)}, u32[]{:S(2)}) collective-permute-start(bf16[1,48,2048]{2,1,0:T(8,128)(2,1)S(1)} %get-tuple-element.20), channel_id=1, source_target_pairs={{0,8},{1,9},{4,12},{5,13},{8,0},{9,1},{12,4},{13,5},{16,24},{17,25... | collective-permute-start | bytes 589832 | tf_op jit(solution)/shard_map/sum/ppermute | solution.py:35
  176.4 21.9 %collective-permute-start.19 = (bf16[1,48,2048]{2,1,0:T(8,128)(2,1)S(1)}, bf16[1,48,2048]{2,1,0:T(8,128)(2,1)S(1)}, u32[]{:S(2)}, u32[]{:S(2)}) collective-permute-start(bf16[1,48,2048]{2,1,0:T(8,128)(2,1)S(1)} %get-tuple-element.19), channel_id=1, source_target_pairs={{0,12},{1,13},{4,0},{5,1},{8,4},{9,5},{12,8},{13,9},{16,28},{17,29... | collective-permute-start | bytes 589832 | tf_op jit(solution)/shard_map/sum/ppermute | solution.py:35
  182.2 9.1 %collective-permute-start.27 = (bf16[1,48,2048]{2,1,0:T(8,128)(2,1)S(1)}, bf16[1,48,2048]{2,1,0:T(8,128)(2,1)S(1)}, u32[]{:S(2)}, u32[]{:S(2)}) collective-permute-start(bf16[1,48,2048]{2,1,0:T(8,128)(2,1)S(1)} %get-tuple-element.28), channel_id=1, source_target_pairs={{0,8},{1,9},{4,12},{5,13},{8,0},{9,1},{12,4},{13,5},{16,24},{17,25... | collective-permute-start | bytes 589832 | tf_op jit(solution)/shard_map/sum/ppermute | solution.py:35
  182.3 10.9 %collective-permute-start.26 = (bf16[1,48,2048]{2,1,0:T(8,128)(2,1)S(1)}, bf16[1,48,2048]{2,1,0:T(8,128)(2,1)S(1)}, u32[]{:S(2)}, u32[]{:S(2)}) collective-permute-start(bf16[1,48,2048]{2,1,0:T(8,128)(2,1)S(1)} %get-tuple-element.27), channel_id=1, source_target_pairs={{0,12},{1,13},{4,0},{5,1},{8,4},{9,5},{12,8},{13,9},{16,28},{17,29... | collective-permute-start | bytes 589832 | tf_op jit(solution)/shard_map/sum/ppermute | solution.py:35
  185.1 10.5 %collective-permute-start.25 = (bf16[1,48,2048]{2,1,0:T(8,128)(2,1)S(1)}, bf16[1,48,2048]{2,1,0:T(8,128)(2,1)S(1)}, u32[]{:S(2)}, u32[]{:S(2)}) collective-permute-start(bf16[1,48,2048]{2,1,0:T(8,128)(2,1)S(1)} %get-tuple-element.26), channel_id=1, source_target_pairs={{0,4},{1,5},{4,8},{5,9},{8,12},{9,13},{12,0},{13,1},{16,20},{17,21... | collective-permute-start | bytes 589832 | tf_op jit(solution)/shard_map/sum/ppermute | solution.py:35
  191.3 12.2 %collective-permute-start.18 = (bf16[1,48,2048]{2,1,0:T(8,128)(2,1)S(1)}, bf16[1,48,2048]{2,1,0:T(8,128)(2,1)S(1)}, u32[]{:S(2)}, u32[]{:S(2)}) collective-permute-start(bf16[1,48,2048]{2,1,0:T(8,128)(2,1)S(1)} %get-tuple-element.18), channel_id=1, source_target_pairs={{0,4},{1,5},{4,8},{5,9},{8,12},{9,13},{12,0},{13,1},{16,20},{17,21... | collective-permute-start | bytes 589832 | tf_op jit(solution)/shard_map/sum/ppermute | solution.py:35
  193.2 15.5 %collective-permute-start.23 = (bf16[2,48,2048]{2,1,0:T(8,128)(2,1)S(1)}, bf16[2,48,2048]{2,1,0:T(8,128)(2,1)S(1)}, u32[]{:S(2)}, u32[]{:S(2)}) collective-permute-start(bf16[2,48,2048]{2,1,0:T(8,128)(2,1)S(1)} %get-tuple-element.24), channel_id=1, source_target_pairs={{0,8},{1,9},{4,12},{5,13},{8,0},{9,1},{12,4},{13,5},{16,24},{17,25... | collective-permute-start | bytes 1179656 | tf_op jit(solution)/shard_map/sum/ppermute | solution.py:35
  195.6 15.7 %collective-permute-start.22 = (bf16[2,48,2048]{2,1,0:T(8,128)(2,1)S(1)}, bf16[2,48,2048]{2,1,0:T(8,128)(2,1)S(1)}, u32[]{:S(2)}, u32[]{:S(2)}) collective-permute-start(bf16[2,48,2048]{2,1,0:T(8,128)(2,1)S(1)} %get-tuple-element.23), channel_id=1, source_target_pairs={{0,12},{1,13},{4,0},{5,1},{8,4},{9,5},{12,8},{13,9},{16,28},{17,29... | collective-permute-start | bytes 1179656 | tf_op jit(solution)/shard_map/sum/ppermute | solution.py:35
  198.2 14.6 %collective-permute-start.21 = (bf16[2,48,2048]{2,1,0:T(8,128)(2,1)S(1)}, bf16[2,48,2048]{2,1,0:T(8,128)(2,1)S(1)}, u32[]{:S(2)}, u32[]{:S(2)}) collective-permute-start(bf16[2,48,2048]{2,1,0:T(8,128)(2,1)S(1)} %get-tuple-element.22), channel_id=1, source_target_pairs={{0,4},{1,5},{4,8},{5,9},{8,12},{9,13},{12,0},{13,1},{16,20},{17,21... | collective-permute-start | bytes 1179656 | tf_op jit(solution)/shard_map/sum/ppermute | solution.py:35
  198.3 20.0 %collective-permute-start.28 = (bf16[24,2048]{1,0:T(8,128)(2,1)S(1)}, bf16[24,2048]{1,0:T(8,128)(2,1)S(1)}, u32[]{:S(2)}, u32[]{:S(2)}) collective-permute-start(bf16[24,2048]{1,0:T(8,128)(2,1)S(1)} %get-tuple-element.43), channel_id=1, source_target_pairs={{0,130},{1,131},{4,134},{5,135},{8,138},{9,139},{12,142},{13,143},... | collective-permute-start | bytes 294920 | tf_op jit(solution)/shard_map/home/ppermute | solution.py:35
  204.3 14.1 %collective-permute-start.30 = (bf16[24,2048]{1,0:T(8,128)(2,1)S(1)}, bf16[24,2048]{1,0:T(8,128)(2,1)S(1)}, u32[]{:S(2)}, u32[]{:S(2)}) collective-permute-start(bf16[24,2048]{1,0:T(8,128)(2,1)S(1)} %get-tuple-element.46), channel_id=1, source_target_pairs={{0,2},{1,3},{4,6},{5,7},{8,10},{9,11},{12,14},{13,15},{16,18},{17,... | collective-permute-start | bytes 294920 | tf_op jit(solution)/shard_map/home/ppermute | solution.py:35
  208.7 11.7 %collective-permute-start.32 = (bf16[24,2048]{1,0:T(8,128)(2,1)S(1)}, bf16[24,2048]{1,0:T(8,128)(2,1)S(1)}, u32[]{:S(2)}, u32[]{:S(2)}) collective-permute-start(bf16[24,2048]{1,0:T(8,128)(2,1)S(1)} %get-tuple-element.42), channel_id=1, source_target_pairs={{0,128},{1,129},{4,132},{5,133},{8,136},{9,137},{12,140},{13,141},... | collective-permute-start | bytes 294920 | tf_op jit(solution)/shard_map/home/ppermute | solution.py:35
  213.2 8.4 %collective-permute-start.24 = (bf16[24,2048]{1,0:T(8,128)(2,1)S(1)}, bf16[24,2048]{1,0:T(8,128)(2,1)S(1)}, u32[]{:S(2)}, u32[]{:S(2)}) collective-permute-start(bf16[24,2048]{1,0:T(8,128)(2,1)S(1)} %get-tuple-element.45), channel_id=1, source_target_pairs={{0,194},{1,195},{4,198},{5,199},{8,202},{9,203},{12,206},{13,207},... | collective-permute-start | bytes 294920 | tf_op jit(solution)/shard_map/home/ppermute | solution.py:35
  213.3 9.0 %collective-permute-start.29 = (bf16[24,2048]{1,0:T(8,128)(2,1)S(1)}, bf16[24,2048]{1,0:T(8,128)(2,1)S(1)}, u32[]{:S(2)}, u32[]{:S(2)}) collective-permute-start(bf16[24,2048]{1,0:T(8,128)(2,1)S(1)} %get-tuple-element.41), channel_id=1, source_target_pairs={{0,66},{1,67},{4,70},{5,71},{8,74},{9,75},{12,78},{13,79},{16,82},... | collective-permute-start | bytes 294920 | tf_op jit(solution)/shard_map/home/ppermute | solution.py:35
  218.4 9.4 %copy-start.4 = (bf16[24,2048]{1,0:T(8,128)(2,1)}, bf16[24,2048]{1,0:T(8,128)(2,1)S(1)}, u32[]{:S(2)}) copy-start(bf16[24,2048]{1,0:T(8,128)(2,1)S(1)} %collective-permute-done.28.refs_2_) | copy-start | bytes 294916
  218.4 9.3 %collective-permute-start.31 = (bf16[24,2048]{1,0:T(8,128)(2,1)S(1)}, bf16[24,2048]{1,0:T(8,128)(2,1)S(1)}, u32[]{:S(2)}, u32[]{:S(2)}) collective-permute-start(bf16[24,2048]{1,0:T(8,128)(2,1)S(1)} %get-tuple-element.44), channel_id=1, source_target_pairs={{0,192},{1,193},{4,196},{5,197},{8,200},{9,201},{12,204},{13,205},... | collective-permute-start | bytes 294920 | tf_op jit(solution)/shard_map/home/ppermute | solution.py:35
  218.4 9.3 %copy-start.5 = (bf16[24,2048]{1,0:T(8,128)(2,1)}, bf16[24,2048]{1,0:T(8,128)(2,1)S(1)}, u32[]{:S(2)}) copy-start(bf16[24,2048]{1,0:T(8,128)(2,1)S(1)} %collective-permute-done.30.refs_4_) | copy-start | bytes 294916
  218.4 9.3 %collective-permute-start.33 = (bf16[24,2048]{1,0:T(8,128)(2,1)S(1)}, bf16[24,2048]{1,0:T(8,128)(2,1)S(1)}, u32[]{:S(2)}, u32[]{:S(2)}) collective-permute-start(bf16[24,2048]{1,0:T(8,128)(2,1)S(1)} %get-tuple-element.40), channel_id=1, source_target_pairs={{0,64},{1,65},{4,68},{5,69},{8,72},{9,73},{12,76},{13,77},{16,80},... | collective-permute-start | bytes 294920 | tf_op jit(solution)/shard_map/home/ppermute | solution.py:35
  220.4 7.3 %copy-start.6 = (bf16[24,2048]{1,0:T(8,128)(2,1)}, bf16[24,2048]{1,0:T(8,128)(2,1)S(1)}, u32[]{:S(2)}) copy-start(bf16[24,2048]{1,0:T(8,128)(2,1)S(1)} %collective-permute-done.32.refs_6_) | copy-start | bytes 294916
  221.6 6.2 %copy-start.7 = (bf16[24,2048]{1,0:T(8,128)(2,1)}, bf16[24,2048]{1,0:T(8,128)(2,1)S(1)}, u32[]{:S(2)}) copy-start(bf16[24,2048]{1,0:T(8,128)(2,1)S(1)} %collective-permute-done.24.refs_1_) | copy-start | bytes 294916
  222.3 5.5 %copy-start.8 = (bf16[24,2048]{1,0:T(8,128)(2,1)}, bf16[24,2048]{1,0:T(8,128)(2,1)S(1)}, u32[]{:S(2)}) copy-start(bf16[24,2048]{1,0:T(8,128)(2,1)S(1)} %collective-permute-done.29.refs_3_) | copy-start | bytes 294916
  227.7 0.6 copy-start.9
  227.7 0.7 copy-start.10
Sparse Core Ops, SparseCore 0:
  30.5 73.9 all-gather.2

commit v2 on v1

v2 whole, which is shorter than its diff:
```python
import functools

import jax
import jax.numpy as jnp
from jax import lax
from jax.experimental import pallas as pl
from jax.experimental.pallas import tpu as pltpu
from jax.sharding import PartitionSpec as P

HD = 128
BLK = 192
TILE = 384
HEADS = 4
GROUPS, WIDE = 3, 256
SPLIT = (2, 2)
X_STEPS = (0, 3, 1, 2)
NZ, NX, NY = 8, 4, 4
SCALE = HD ** (-0.5) * 1.4426950408889634
LOW = -1e30


def flat(z, x, y, c):
    return ((z % 4) * 4 + x) * 16 + y * 4 + (z // 4) * 2 + c


def perm(dz=0, dx=0, dy=0, dc=0):
    pairs = []
    for z in range(NZ):
        for x in range(NX):
            for y in range(NY):
                for c in range(2):
                    to = flat((z + dz) % NZ, (x + dx) % NX, (y + dy) % NY, (c + dc) % 2)
                    pairs.append((flat(z, x, y, c), to))
    return pairs


def send(a, **step):
    return lax.ppermute(a, ("ctx", "tp"), perm(**step))


def attend_kernel(meta, q_ref, mine_ref, theirs_ref, *refs):
    o_refs = refs[:4]
    ks, vs, qs, m_s, l_s, acc_s, o_s = refs[4:]
    zh = meta[54]
    ctx = meta[36]
    core = meta[37]
    ks[0:BLK, :] = jnp.zeros((BLK, HD), ks.dtype)
    vs[0:BLK, :] = jnp.zeros((BLK, HD), vs.dtype)

    def place(k_from, v_from):
        for slot in range(16):
            owner = meta[38 + slot]
            for i in range(2):
                at = pl.multiple_of((meta[2 * owner + i] + 1) * BLK, BLK)
                ks[pl.ds(at, BLK), :] = k_from[slot, i * BLK:(i + 1) * BLK, :]
                vs[pl.ds(at, BLK), :] = v_from[slot, i * BLK:(i + 1) * BLK, :]

    @pl.when(core == 0)
    def _():
        place(mine_ref, theirs_ref)

    @pl.when(core != 0)
    def _():
        place(theirs_ref, mine_ref)

    end1 = meta[32]
    end2 = end1 + meta[33]
    end3 = end2 + meta[34]

    def start_of(pos):
        s = jnp.where(pos >= end1, end1, 0)
        s = jnp.where(pos >= end2, end2, s)
        return jnp.where(pos >= end3, end3, s)

    for i in range(2):
        base = meta[2 * ctx + i] * BLK
        top = base + BLK
        low_first = start_of(base)
        low_last = start_of(base + BLK - 1)
        rows = slice(i * BLK, (i + 1) * BLK)
        for h in range(HEADS):
            qs[h * BLK:(h + 1) * BLK, :] = q_ref[rows, h * HD:(h + 1) * HD]

        def scores(t, g, kind):
            first = top - (t + 1) * TILE
            at = pl.multiple_of(first + BLK, BLK)
            s = lax.dot_general(
                ks[pl.ds(at, TILE), :], qs[g * WIDE:(g + 1) * WIDE, :], (((1,), (1,)), ((), ())),
                preferred_element_type=jnp.float32,
            ) * SCALE
            if kind != "inner":
                row = g * WIDE + lax.broadcasted_iota(jnp.int32, (1, WIDE), 1)
                for _ in range(HEADS - 1):
                    row = jnp.where(row >= BLK, row - BLK, row)
                row = row + base
                key = first + lax.broadcasted_iota(jnp.int32, (TILE, WIDE), 0)
                ok = key >= start_of(row)
                if kind == "diagonal":
                    ok = ok & (key <= row)
                s = jnp.where(ok, s, LOW)
            return s, vs[pl.ds(at, TILE), :]

        def mix(v, p):
            return lax.dot_general(
                v, p.astype(jnp.bfloat16), (((0,), (0,)), ((), ())), preferred_element_type=jnp.float32
            )

        for g in range(GROUPS):
            cols = slice(g * WIDE, (g + 1) * WIDE)
            s, v = scores(0, g, "diagonal")
            peak = jnp.max(s, axis=0, keepdims=True)
            p = jnp.exp2(s - peak)
            m_s[:, cols] = peak
            l_s[:, cols] = jnp.sum(p, axis=0, keepdims=True)
            acc_s[:, cols] = mix(v, p)

        def step(t, kind):
            for g in range(GROUPS):
                cols = slice(g * WIDE, (g + 1) * WIDE)
                s, v = scores(t, g, kind)
                old = m_s[:, cols]
                peak = jnp.maximum(old, jnp.max(s, axis=0, keepdims=True))
                fade = jnp.exp2(old - peak)
                p = jnp.exp2(s - peak)
                m_s[:, cols] = peak
                l_s[:, cols] = l_s[:, cols] * fade + jnp.sum(p, axis=0, keepdims=True)
                acc_s[:, cols] = acc_s[:, cols] * fade + mix(v, p)

        inner = jnp.maximum(1, (top - low_last) // TILE)
        total = (top - low_first + TILE - 1) // TILE

        @pl.loop(1, inner)
        def _(t):
            step(t, "inner")

        @pl.loop(inner, total)
        def _(t):
            step(t, "edge")

        o = (acc_s[...] / l_s[...]).T
        for h in range(HEADS):
            for zc in range(4):
                pick = [o[h * BLK + yy * 96 + zc * 24:h * BLK + yy * 96 + (zc + 1) * 24] for yy in range(2)]
                r = (zh + zc // 2) % 2 * 2 + (core + zc % 2) % 2
                o_s[r, i * 48:(i + 1) * 48, h * HD:(h + 1) * HD] = jnp.concatenate(pick).astype(jnp.bfloat16)

    for r in range(4):
        o_refs[r][...] = o_s[r]


def attend(meta, q, mine, theirs):
    return pl.pallas_call(
        attend_kernel,
        out_shape=[jax.ShapeDtypeStruct((96, HEADS * HD), jnp.bfloat16)] * 4,
        in_specs=[pl.BlockSpec(memory_space=pltpu.SMEM)] + [pl.BlockSpec(memory_space=pltpu.VMEM)] * 3,
        out_specs=[pl.BlockSpec(memory_space=pltpu.VMEM)] * 4,
        scratch_shapes=[
            pltpu.VMEM((33 * BLK, HD), jnp.bfloat16),
            pltpu.VMEM((33 * BLK, HD), jnp.bfloat16),
            pltpu.VMEM((HEADS * BLK, HD), jnp.bfloat16),
            pltpu.VMEM((1, HEADS * BLK), jnp.float32),
            pltpu.VMEM((1, HEADS * BLK), jnp.float32),
            pltpu.VMEM((HD, HEADS * BLK), jnp.float32),
            pltpu.VMEM((4, 96, HEADS * HD), jnp.bfloat16),
        ],
        compiler_params=pltpu.CompilerParams(vmem_limit_bytes=32 * 2**20),
        cost_estimate=pl.CostEstimate(flops=4 * 10**9, bytes_accessed=4 * 10**6, transcendentals=3 * 10**6),
        name="attend",
    )(meta, q, mine, theirs)


def project_kernel(meta, *refs):
    a_refs, w_refs, outs = refs[:4], refs[4:8], refs[8:12]
    rows, total = refs[12:]
    y = meta[2]

    @pl.when(pl.program_id(0) == 0)
    def _():
        for i in range(4):
            for r in range(4):
                rows[r, i * 96:(i + 1) * 96, :] = a_refs[i][r]

    t = jnp.dot(rows[0], w_refs[0][0, 0, 0], preferred_element_type=jnp.float32)
    for r in range(1, 4):
        t += jnp.dot(rows[r], w_refs[r][0, 0, 0], preferred_element_type=jnp.float32)
    total[...] = t
    for k in range(4):
        at = lax.rem(y + k, 4) * 24
        four = [total[pl.ds(pl.multiple_of(i * 96 + at, 8), 24), :] for i in range(4)]
        outs[k][...] = jnp.concatenate(four).astype(jnp.bfloat16)


def project(first, count, meta, pieces, w):
    whole = pl.BlockSpec((4, 96, 512), lambda i, m: (0, 0, 0))

    def w_spec(r):
        return pl.BlockSpec(
            (1, 1, 1, 512, 512),
            lambda i, m: ((m[0] + r // 2) % 2, first + i // 2, (m[1] + r % 2) % 2, 0, i % 2),
        )

    with jax.named_scope("project"):
        return pl.pallas_call(
            project_kernel,
            grid_spec=pltpu.PrefetchScalarGridSpec(
                num_scalar_prefetch=1,
                grid=(2 * count,),
                in_specs=[whole] * 4 + [w_spec(r) for r in range(4)],
                out_specs=[pl.BlockSpec((96, 512), lambda i, m: (0, i))] * 4,
                scratch_shapes=[pltpu.VMEM((4, 384, 512), jnp.bfloat16), pltpu.VMEM((384, 512), jnp.float32)],
            ),
            out_shape=[jax.ShapeDtypeStruct((96, count * 1024), jnp.bfloat16)] * 4,
            compiler_params=pltpu.CompilerParams(vmem_limit_bytes=48 * 2**20),
            cost_estimate=pl.CostEstimate(
                flops=count * 2 * 384 * 2048 * 1024, bytes_accessed=count * 5 * 10**6, transcendentals=0),
            name="project",
        )(meta, *pieces, *([w] * 4))


def assemble_kernel(meta, *refs):
    out = refs[-1]
    x = meta[3]
    at_z = 0
    for j, group in enumerate(SPLIT):
        for i, step in enumerate(X_STEPS):
            for g in range(group):
                col = pl.multiple_of(((at_z + g) * 4 + lax.rem(x + step, 4)) * 1024, 1024)
                out[:, pl.ds(col, 1024)] = refs[j * 4 + i][:, g * 1024:(g + 1) * 1024]
        at_z += group


def assemble(meta, pieces):
    return pl.pallas_call(
        assemble_kernel,
        out_shape=jax.ShapeDtypeStruct((24, 16384), jnp.bfloat16),
        in_specs=[pl.BlockSpec(memory_space=pltpu.SMEM)] + [pl.BlockSpec(memory_space=pltpu.VMEM)] * len(pieces),
        out_specs=pl.BlockSpec(memory_space=pltpu.VMEM),
        name="assemble",
    )(meta, *pieces)


def local(query_rows, key_rows, value_rows, out_weight, block_order, doc_lengths):
    ctx = lax.axis_index("ctx")
    tp = lax.axis_index("tp")
    zl, x = ctx // 4, ctx % 4
    y, zh, core = tp // 4, (tp // 2) % 2, tp % 2
    z = zh * 4 + zl

    def shard_for(zh_to):
        at = (y * 2 + zh_to) * HD
        k = lax.dynamic_slice_in_dim(key_rows, at, HD, 1)
        v = lax.dynamic_slice_in_dim(value_rows, at, HD, 1)
        return jnp.where(core == 0, k, v)

    with jax.named_scope("kv"):
        near = [shard_for(((z + d) % 8) // 4) for d in (0, 1, 7, 2)]
        four = jnp.stack([near[0], send(near[1], dz=1), send(near[2], dz=-1), send(near[3], dz=2)])

    with jax.named_scope("weights"):
        groups = [[flat(zz, xx, yy, cc) for zz in range(8) for cc in range(2)] for xx in range(4) for yy in range(4)]
        w = lax.all_gather(out_weight, ("ctx", "tp"), axis_index_groups=groups, axis=0)
        w = w.reshape(2, 4, 2, 512, 1024)

    with jax.named_scope("kv"):
        up, down, far = send(four, dx=1), send(four, dx=-1), send(four, dx=2)
        mine = jnp.concatenate([four, up, down, far])
        theirs = send(mine, dc=1)
        steps = [(a, b) for b in (0, -1, 1, 2) for a in (0, -1, 1, 2)]
        owners = [((zl + a + 4) % 4) * 4 + (x + b + 4) % 4 for a, b in steps]
        meta = jnp.concatenate([
            block_order.astype(jnp.int32), doc_lengths.astype(jnp.int32),
            jnp.stack([ctx, core] + owners + [zh]).astype(jnp.int32),
        ])

    with jax.named_scope("attend"):
        a = attend(meta, query_rows, mine, theirs)

    with jax.named_scope("rows"):
        here = jnp.stack([a[0], send(a[1], dc=1), send(a[2], dz=4), send(a[3], dz=4, dc=1)])
        pieces = [here, send(here, dx=1), send(here, dx=-1), send(here, dx=2)]

    where = jnp.stack([zh, core, y, x]).astype(jnp.int32)
    done = []
    first = 0
    outs = []
    for count in SPLIT:
        outs.append(project(first, count, where, pieces, w))
        first += count
    for o in outs:
        with jax.named_scope("sum"):
            got = [o[0], send(o[1], dy=1), send(o[3], dy=-1), send(o[2], dy=2)]
            total = sum(g.astype(jnp.float32) for g in got).astype(jnp.bfloat16)
        with jax.named_scope("home"):
            own, down, up, far = [total[i * 24:(i + 1) * 24] for i in range(4)]
            up, down = send(up, dx=1), send(down, dx=-1)
            done += [own, up, down, send(far, dx=2)]
    return assemble(where, done)


def solution(mesh):
    in_specs = (P("ctx", "tp"), P("ctx", None), P("ctx", None), P("tp", "ctx"), P(), P())
    out_specs = P(("ctx", "tp"), None)
    return jax.shard_map(local, mesh=mesh, in_specs=in_specs, out_specs=out_specs, check_vma=False)
```

time: 241 us -> 182 us (0.76); the launches traced: 237 us -> 182 us
  waiting for transfers between devices: 118 us -> 95.3 us
  starting transfers between devices: 63 us -> 44.8 us
  Pallas kernels: 33.1 us -> 22.5 us
  local copies, waits for them, and re-layouts: 5.36 us -> 2.27 us
    ppermute x34 -> x25, waiting for transfers between devices: 102 us -> 75.7 us  [send(): return lax.ppermute(a, ('ctx', 'tp'), perm(**step))]
    ppermute x34 -> x25, starting transfers between devices: 63 us -> 44.8 us  [send(): return lax.ppermute(a, ('ctx', 'tp'), perm(**step))]
    pallas_call x4 -> x3, Pallas kernels: 30.9 us -> 20.3 us  [the longest x2 14.4 us: project(): pl.pallas_call(project_kernel, grid_spec=pltpu.PrefetchScalarGridSpec(num...]
    all_gather x1, waiting for transfers between devices: 16.4 us -> 18.9 us  [local(): lax.all_gather(out_weight, ('ctx', 'tp'), axis_index_groups=groups, axis=0)]
  transfers between devices with their start and end apart: 35 -> 26, of which waited for: 21 -> 18; matrix products, arithmetic and copies ran while one was open for 2% -> 2% of each run, Pallas kernels for 11% -> 7%
where the time goes in v2:
time: 182 us
  waiting for transfers between devices  95.3 us (52%)
  starting transfers between devices  44.8 us (25%)
  Pallas kernels  22.5 us (12%)
  between operations  13.9 us (8%)
  other arithmetic  2.86 us (2%)
  local copies, waits for them, and re-layouts  2.27 us (1%)
    ppermute x25, waiting for transfers between devices, send(): return lax.ppermute(a, ('ctx', 'tp'), perm(**step))  75.7 us
    ppermute x25, starting transfers between devices, send(): return lax.ppermute(a, ('ctx', 'tp'), perm(**step))  44.8 us
    all_gather x1, waiting for transfers between devices, local(): lax.all_gather(out_weight, ('ctx', 'tp'), axis_index_groups=groups, axis=0)  18.9 us
    pallas_call x2, Pallas kernels, project(): pl.pallas_call(project_kernel, grid_spec=pltpu.PrefetchScalarGridSpec(num...  14.4 us
    pallas_call x1, Pallas kernels, attend(): pl.pallas_call(attend_kernel, out_shape=[jax.ShapeDtypeStruct((96, HEADS...  5.88 us
  transfers between devices with their start and end apart: 26, of which 18 were waited for; matrix products, arithmetic and copies ran while one was open for 2% of the time, Pallas kernels for 7%

profile of v2, /device:TPU:8, one launch (start us, length us, event | category | flops | bytes accessed | tf_op | source)
XLA Modules:
  0.0 181.6 jit_solution(4230827809902003647)
XLA Ops:
  6.5 0.7 all-gather.3.cloned.1.call-update
  7.4 1.2 dynamic-slice_select_fusion
  8.7 2.0 %collective-permute-start = (bf16[384,128]{1,0:T(8,128)(2,1)S(1)}, bf16[384,128]{1,0:T(8,128)(2,1)S(1)}, u32[]{:S(2)}, u32[]{:S(2)}) collective-permute-start(bf16[384,128]{1,0:T(8,128)(2,1)S(1)} %get-tuple-element.32), channel_id=1, source_target_pairs={{0,64},{1,65},{4,68},{5,69},{8,72},{9,73},{12,76},{13,77},{16,80},... | collective-permute-start | bytes 294920 | tf_op jit(solution)/shard_map/kv/ppermute | solution.py:38
  10.7 4.0 %collective-permute-start.1 = (bf16[384,128]{1,0:T(8,128)(2,1)S(1)}, bf16[384,128]{1,0:T(8,128)(2,1)S(1)}, u32[]{:S(2)}, u32[]{:S(2)}) collective-permute-start(bf16[384,128]{1,0:T(8,128)(2,1)S(1)} %get-tuple-element.33), channel_id=1, source_target_pairs={{0,194},{1,195},{4,198},{5,199},{8,202},{9,203},{12,206},{13,207},... | collective-permute-start | bytes 294920 | tf_op jit(solution)/shard_map/kv/ppermute | solution.py:38
  14.7 0.0 collective-permute-start.2
  14.7 1.0 constant_dynamic-update-slice_fusion.6
  15.7 2.4 %collective-permute-done = bf16[384,128]{1,0:T(8,128)(2,1)S(1)} collective-permute-done((bf16[384,128]{1,0:T(8,128)(2,1)S(1)}, bf16[384,128]{1,0:T(8,128)(2,1)S(1)}, u32[]{:S(2)}, u32[]{:S(2)}) %collective-permute-start) | collective-permute-done | bytes 98336 | tf_op jit(solution)/shard_map/kv/ppermute | solution.py:38
  18.1 0.0 collective-permute-done.1
  18.1 4.9 %collective-permute-done.2 = bf16[384,128]{1,0:T(8,128)(2,1)S(1)} collective-permute-done((bf16[384,128]{1,0:T(8,128)(2,1)S(1)}, bf16[384,128]{1,0:T(8,128)(2,1)S(1)}, u32[]{:S(2)}, u32[]{:S(2)}) %collective-permute-start.2) | collective-permute-done | bytes 98336 | tf_op jit(solution)/shard_map/kv/ppermute | solution.py:38
  23.0 0.1 pad_maximum_fusion
  23.0 1.6 collective-permute-start.3
  24.6 1.7 collective-permute-start.4
  26.4 1.8 collective-permute-start.5
  28.2 7.2 %collective-permute-done.3 = bf16[4,384,128]{2,1,0:T(8,128)(2,1)S(1)} collective-permute-done((bf16[4,384,128]{2,1,0:T(8,128)(2,1)S(1)}, bf16[4,384,128]{2,1,0:T(8,128)(2,1)S(1)}, u32[]{:S(2)}, u32[]{:S(2)}) %collective-permute-start.3) | collective-permute-done | bytes 393248 | tf_op jit(solution)/shard_map/kv/ppermute | solution.py:38
  35.4 0.1 constant_dynamic-update-slice_fusion.2
  35.4 5.3 %collective-permute-done.4 = bf16[4,384,128]{2,1,0:T(8,128)(2,1)S(1)} collective-permute-done((bf16[4,384,128]{2,1,0:T(8,128)(2,1)S(1)}, bf16[4,384,128]{2,1,0:T(8,128)(2,1)S(1)}, u32[]{:S(2)}, u32[]{:S(2)}) %collective-permute-start.4) | collective-permute-done | bytes 393248 | tf_op jit(solution)/shard_map/kv/ppermute | solution.py:38
  40.7 0.1 constant_dynamic-update-slice_fusion.1
  40.8 1.6 collective-permute-done.5
  42.4 0.1 constant_dynamic-update-slice_fusion.mine_ref
  42.4 0.1 collective-permute-start.6
  42.7 0.1 concatenate.7.meta
  42.8 3.2 %collective-permute-done.6.theirs_ref = bf16[16,384,128]{2,1,0:T(8,128)(2,1)S(1)} collective-permute-done((bf16[16,384,128]{2,1,0:T(8,128)(2,1)S(1)}, bf16[16,384,128]{2,1,0:T(8,128)(2,1)S(1)}, u32[]{:S(2)}, u32[]{:S(2)}) %collective-permute-start.6) | collective-permute-done | bytes 1572896 | tf_op jit(solution)/shard_map/kv/ppermute | solution.py:38
  45.9 5.9 %attend.1 = (bf16[96,512]{1,0:T(8,128)(2,1)S(1)}, bf16[96,512]{1,0:T(8,128)(2,1)S(1)}, bf16[96,512]{1,0:T(8,128)(2,1)S(1)}, bf16[96,512]{1,0:T(8,128)(2,1)S(1)}) custom-call(s32[55]{0:T(128)S(1)} %concatenate.7.meta, bf16[384,512]{1,0:T(8,128)(2,1)S(1)} %copy-done.1, bf16[16,384,128]{2,1,0:T(8,128)(2,1)S(1)} %constant_dynamic-update-slice_fusion.mine_ref, ...), custom_call_target="tpu_custom_call" | custom-call | flops 4000000000 | bytes 4000000 | tf_op jit(solution)/shard_map/attend/attend/pallas_call | solution.py:152
  51.8 0.2 collective-permute-start.7
  52.1 6.0 %collective-permute-start.8 = (bf16[96,512]{1,0:T(8,128)(2,1)S(1)}, bf16[96,512]{1,0:T(8,128)(2,1)S(1)}, u32[]{:S(2)}, u32[]{:S(2)}) collective-permute-start(bf16[96,512]{1,0:T(8,128)(2,1)S(1)} %get-tuple-element.19), channel_id=1, source_target_pairs={{0,2},{1,3},{4,6},{5,7},{8,10},{9,11},{12,14},{13,15},{16,18},{17,... | collective-permute-start | bytes 294920 | tf_op jit(solution)/shard_map/rows/ppermute | solution.py:38
  58.0 8.7 %collective-permute-done.8 = bf16[96,512]{1,0:T(8,128)(2,1)S(1)} collective-permute-done((bf16[96,512]{1,0:T(8,128)(2,1)S(1)}, bf16[96,512]{1,0:T(8,128)(2,1)S(1)}, u32[]{:S(2)}, u32[]{:S(2)}) %collective-permute-start.8) | collective-permute-done | bytes 98336 | tf_op jit(solution)/shard_map/rows/ppermute | solution.py:38
  66.7 4.9 %collective-permute-done.9 = bf16[96,512]{1,0:T(8,128)(2,1)S(1)} collective-permute-done((bf16[96,512]{1,0:T(8,128)(2,1)S(1)}, bf16[96,512]{1,0:T(8,128)(2,1)S(1)}, u32[]{:S(2)}, u32[]{:S(2)}) %collective-permute-start.9) | collective-permute-done | bytes 98336 | tf_op jit(solution)/shard_map/rows/ppermute | solution.py:38
  71.6 0.1 pad_maximum_fusion.1.refs_0_
  71.6 0.2 collective-permute-start.10
  71.9 6.2 %collective-permute-start.11 = (bf16[4,96,512]{2,1,0:T(8,128)(2,1)S(1)}, bf16[4,96,512]{2,1,0:T(8,128)(2,1)S(1)}, u32[]{:S(2)}, u32[]{:S(2)}) collective-permute-start(bf16[4,96,512]{2,1,0:T(8,128)(2,1)S(1)} %pad_maximum_fusion.1.refs_0_), channel_id=1, source_target_pairs={{0,48},{1,49},{4,52},{5,53},{8,56},{9,57},{12,60},{13,61},{16,0},{... | collective-permute-start | bytes 1179656 | tf_op jit(solution)/shard_map/rows/ppermute | solution.py:38
  78.1 1.9 %collective-permute-start.12 = (bf16[4,96,512]{2,1,0:T(8,128)(2,1)S(1)}, bf16[4,96,512]{2,1,0:T(8,128)(2,1)S(1)}, u32[]{:S(2)}, u32[]{:S(2)}) collective-permute-start(bf16[4,96,512]{2,1,0:T(8,128)(2,1)S(1)} %pad_maximum_fusion.1.refs_0_), channel_id=1, source_target_pairs={{0,32},{1,33},{4,36},{5,37},{8,40},{9,41},{12,44},{13,45},{16,48},... | collective-permute-start | bytes 1179656 | tf_op jit(solution)/shard_map/rows/ppermute | solution.py:38
  80.0 0.1 pad_add_fusion.meta
  80.1 7.3 %collective-permute-done.10.refs_1_ = bf16[4,96,512]{2,1,0:T(8,128)(2,1)S(1)} collective-permute-done((bf16[4,96,512]{2,1,0:T(8,128)(2,1)S(1)}, bf16[4,96,512]{2,1,0:T(8,128)(2,1)S(1)}, u32[]{:S(2)}, u32[]{:S(2)}) %collective-permute-start.10) | collective-permute-done | bytes 393248 | tf_op jit(solution)/shard_map/rows/ppermute | solution.py:38
  87.4 7.8 %collective-permute-done.11.refs_2_ = bf16[4,96,512]{2,1,0:T(8,128)(2,1)S(1)} collective-permute-done((bf16[4,96,512]{2,1,0:T(8,128)(2,1)S(1)}, bf16[4,96,512]{2,1,0:T(8,128)(2,1)S(1)}, u32[]{:S(2)}, u32[]{:S(2)}) %collective-permute-start.11) | collective-permute-done | bytes 393248 | tf_op jit(solution)/shard_map/rows/ppermute | solution.py:38
  95.2 1.8 collective-permute-done.12.refs_3_
  97.0 18.9 %all-gather.3.cloned.1.call-done = bf16[8192,1024]{1,0:T(8,128)(2,1)} async-done(((bf16[512,1024]{1,0:T(8,128)(2,1)}), bf16[8192,1024]{1,0:T(8,128)(2,1)}) %all-gather.3.cloned.1.call-update) | async-done | bytes 16777232 | tf_op jit(solution)/shard_map/weights/all_gather | solution.py:261
  115.9 7.2 %project.3 = (bf16[96,2048]{1,0:T(8,128)(2,1)S(1)}, bf16[96,2048]{1,0:T(8,128)(2,1)S(1)}, bf16[96,2048]{1,0:T(8,128)(2,1)S(1)}, bf16[96,2048]{1,0:T(8,128)(2,1)S(1)}) custom-call(s32[4]{0:T(128)S(1)} %pad_add_fusion.meta, bf16[4,96,512]{2,1,0:T(8,128)(2,1)S(1)} %pad_maximum_fusion.1.refs_0_, bf16[4,96,512]{2,1,0:T(8,128)(2,1)S(1)} %collective-permute-done.10.refs_1_, ...), custom_call_target="tpu_custom_call" | custom-call | flops 3221225472 | bytes 10000000 | tf_op jit(solution)/shard_map/project/project/pallas_call | solution.py:203
  123.2 1.6 collective-permute-start.19
  124.7 0.5 collective-permute-start.20
  125.3 2.1 %collective-permute-start.21 = (bf16[96,2048]{1,0:T(8,128)(2,1)S(1)}, bf16[96,2048]{1,0:T(8,128)(2,1)S(1)}, u32[]{:S(2)}, u32[]{:S(2)}) collective-permute-start(bf16[96,2048]{1,0:T(8,128)(2,1)S(1)} %get-tuple-element.28), channel_id=1, source_target_pairs={{0,8},{1,9},{4,12},{5,13},{8,0},{9,1},{12,4},{13,5},{16,24},{17,25... | collective-permute-start | bytes 1179656 | tf_op jit(solution)/shard_map/sum/ppermute | solution.py:38
  127.4 7.2 %project.2 = (bf16[96,2048]{1,0:T(8,128)(2,1)S(1)}, bf16[96,2048]{1,0:T(8,128)(2,1)S(1)}, bf16[96,2048]{1,0:T(8,128)(2,1)S(1)}, bf16[96,2048]{1,0:T(8,128)(2,1)S(1)}) custom-call(s32[4]{0:T(128)S(1)} %pad_add_fusion.meta, bf16[4,96,512]{2,1,0:T(8,128)(2,1)S(1)} %pad_maximum_fusion.1.refs_0_, bf16[4,96,512]{2,1,0:T(8,128)(2,1)S(1)} %collective-permute-done.10.refs_1_, ...), custom_call_target="tpu_custom_call" | custom-call | flops 3221225472 | bytes 10000000 | tf_op jit(solution)/shard_map/project/project/pallas_call | solution.py:203
  134.6 1.2 collective-permute-start.13
  135.8 0.9 collective-permute-start.14
  136.7 0.0 collective-permute-done.19
  136.7 1.5 collective-permute-start.15
  138.2 0.0 collective-permute-done.20
  138.2 7.6 %collective-permute-done.21 = bf16[96,2048]{1,0:T(8,128)(2,1)S(1)} collective-permute-done((bf16[96,2048]{1,0:T(8,128)(2,1)S(1)}, bf16[96,2048]{1,0:T(8,128)(2,1)S(1)}, u32[]{:S(2)}, u32[]{:S(2)}) %collective-permute-start.21) | collective-permute-done | bytes 393248 | tf_op jit(solution)/shard_map/sum/ppermute | solution.py:38
  145.8 0.2 add_convert_fusion
  146.1 0.7 fusion
  146.7 1.5 collective-permute-start.22
  148.2 1.8 collective-permute-start.23
  150.0 2.1 %collective-permute-done.13 = bf16[96,2048]{1,0:T(8,128)(2,1)S(1)} collective-permute-done((bf16[96,2048]{1,0:T(8,128)(2,1)S(1)}, bf16[96,2048]{1,0:T(8,128)(2,1)S(1)}, u32[]{:S(2)}, u32[]{:S(2)}) %collective-permute-start.13) | collective-permute-done | bytes 393248 | tf_op jit(solution)/shard_map/sum/ppermute | solution.py:38
  152.1 3.0 %collective-permute-start.24 = (bf16[24,2048]{1,0:T(8,128)(2,1)S(1)}, bf16[24,2048]{1,0:T(8,128)(2,1)S(1)}, u32[]{:S(2)}, u32[]{:S(2)}) collective-permute-start(bf16[24,2048]{1,0:T(8,128)(2,1)S(1)} %get-tuple-element.34), channel_id=1, source_target_pairs={{0,32},{1,33},{4,36},{5,37},{8,40},{9,41},{12,44},{13,45},{16,48},... | collective-permute-start | bytes 294920 | tf_op jit(solution)/shard_map/home/ppermute | solution.py:38
  155.1 6.6 %collective-permute-done.15 = bf16[96,2048]{1,0:T(8,128)(2,1)S(1)} collective-permute-done((bf16[96,2048]{1,0:T(8,128)(2,1)S(1)}, bf16[96,2048]{1,0:T(8,128)(2,1)S(1)}, u32[]{:S(2)}, u32[]{:S(2)}) %collective-permute-start.15) | collective-permute-done | bytes 393248 | tf_op jit(solution)/shard_map/sum/ppermute | solution.py:38
  161.7 0.2 add_convert_fusion.1
  161.9 0.7 fusion.1
  162.6 1.5 collective-permute-start.16
  164.1 1.8 collective-permute-start.17
  165.8 1.8 collective-permute-start.18
  167.6 0.8 collective-permute-done.16.refs_1_
  168.4 1.0 collective-permute-done.17.refs_2_
  169.4 2.5 %collective-permute-done.18.refs_3_ = bf16[24,2048]{1,0:T(8,128)(2,1)S(1)} collective-permute-done((bf16[24,2048]{1,0:T(8,128)(2,1)S(1)}, bf16[24,2048]{1,0:T(8,128)(2,1)S(1)}, u32[]{:S(2)}, u32[]{:S(2)}) %collective-permute-start.18) | collective-permute-done | bytes 98336 | tf_op jit(solution)/shard_map/home/ppermute | solution.py:38
  172.0 0.6 copy-done.7
  172.6 2.2 %assemble.1 = bf16[24,16384]{1,0:T(8,128)(2,1)} custom-call(s32[4]{0:T(128)} %copy-done, bf16[24,2048]{1,0:T(8,128)(2,1)} %get-tuple-element.41.refs_0_, bf16[24,2048]{1,0:T(8,128)(2,1)} %copy-done.5, bf16[24,2048]{1,0:T(8,128)(2,1)} %copy-done.6, bf16[24,2048]{1,0:T(8,128)(2,1)} %copy-done.7, bf16[24,2048]{1,0:T(8,128)(2,1)} %get-tuple-element.37.refs_4_, ...), custom_call_target="tpu_custom_call" | custom-call | tf_op jit(solution)/shard_map/assemble/pallas_call | solution.py:233
  (29 shorter events, 0.1 us)
Async XLA Ops:
  6.5 109.4 %all-gather.3.cloned.1.call-start = ((), (), s32[]{:S(2)}) async-start(), calls=%async_computation | async-start | bytes 17825792 | tf_op jit(solution)/shard_map/weights/all_gather | solution.py:261
  8.7 9.4 %collective-permute-start = (bf16[384,128]{1,0:T(8,128)(2,1)S(1)}, bf16[384,128]{1,0:T(8,128)(2,1)S(1)}, u32[]{:S(2)}, u32[]{:S(2)}) collective-permute-start(bf16[384,128]{1,0:T(8,128)(2,1)S(1)} %get-tuple-element.32), channel_id=1, source_target_pairs={{0,64},{1,65},{4,68},{5,69},{8,72},{9,73},{12,76},{13,77},{16,80},... | collective-permute-start | bytes 294920 | tf_op jit(solution)/shard_map/kv/ppermute | solution.py:38
  10.7 7.4 %collective-permute-start.1 = (bf16[384,128]{1,0:T(8,128)(2,1)S(1)}, bf16[384,128]{1,0:T(8,128)(2,1)S(1)}, u32[]{:S(2)}, u32[]{:S(2)}) collective-permute-start(bf16[384,128]{1,0:T(8,128)(2,1)S(1)} %get-tuple-element.33), channel_id=1, source_target_pairs={{0,194},{1,195},{4,198},{5,199},{8,202},{9,203},{12,206},{13,207},... | collective-permute-start | bytes 294920 | tf_op jit(solution)/shard_map/kv/ppermute | solution.py:38
  14.7 8.3 %collective-permute-start.2 = (bf16[384,128]{1,0:T(8,128)(2,1)S(1)}, bf16[384,128]{1,0:T(8,128)(2,1)S(1)}, u32[]{:S(2)}, u32[]{:S(2)}) collective-permute-start(bf16[384,128]{1,0:T(8,128)(2,1)S(1)} %get-tuple-element.31), channel_id=1, source_target_pairs={{0,128},{1,129},{4,132},{5,133},{8,136},{9,137},{12,140},{13,141},... | collective-permute-start | bytes 294920 | tf_op jit(solution)/shard_map/kv/ppermute | solution.py:38
  23.0 12.4 %collective-permute-start.3 = (bf16[4,384,128]{2,1,0:T(8,128)(2,1)S(1)}, bf16[4,384,128]{2,1,0:T(8,128)(2,1)S(1)}, u32[]{:S(2)}, u32[]{:S(2)}) collective-permute-start(bf16[4,384,128]{2,1,0:T(8,128)(2,1)S(1)} %pad_maximum_fusion), channel_id=1, source_target_pairs={{0,16},{1,17},{4,20},{5,21},{8,24},{9,25},{12,28},{13,29},{16,32},... | collective-permute-start | bytes 1179656 | tf_op jit(solution)/shard_map/kv/ppermute | solution.py:38
  24.6 16.1 %collective-permute-start.4 = (bf16[4,384,128]{2,1,0:T(8,128)(2,1)S(1)}, bf16[4,384,128]{2,1,0:T(8,128)(2,1)S(1)}, u32[]{:S(2)}, u32[]{:S(2)}) collective-permute-start(bf16[4,384,128]{2,1,0:T(8,128)(2,1)S(1)} %pad_maximum_fusion), channel_id=1, source_target_pairs={{0,48},{1,49},{4,52},{5,53},{8,56},{9,57},{12,60},{13,61},{16,0},{... | collective-permute-start | bytes 1179656 | tf_op jit(solution)/shard_map/kv/ppermute | solution.py:38
  26.4 16.0 %collective-permute-start.5 = (bf16[4,384,128]{2,1,0:T(8,128)(2,1)S(1)}, bf16[4,384,128]{2,1,0:T(8,128)(2,1)S(1)}, u32[]{:S(2)}, u32[]{:S(2)}) collective-permute-start(bf16[4,384,128]{2,1,0:T(8,128)(2,1)S(1)} %pad_maximum_fusion), channel_id=1, source_target_pairs={{0,32},{1,33},{4,36},{5,37},{8,40},{9,41},{12,44},{13,45},{16,48},... | collective-permute-start | bytes 1179656 | tf_op jit(solution)/shard_map/kv/ppermute | solution.py:38
  28.2 14.5 %copy-start.8 = (s32[32]{0:T(128)S(1)}, s32[32]{0:T(128)}, u32[]{:S(2)}) copy-start(s32[32]{0:T(128)} %param.10) | copy-start | bytes 388
  28.2 14.5 %copy-start.9 = (s32[4]{0:T(128)S(1)}, s32[4]{0:T(128)}, u32[]{:S(2)}) copy-start(s32[4]{0:T(128)} %param.11) | copy-start | bytes 52
  28.2 17.8 %copy-start.1 = (bf16[384,512]{1,0:T(8,128)(2,1)S(1)}, bf16[384,512]{1,0:T(8,128)(2,1)}, u32[]{:S(2)}) copy-start(bf16[384,512]{1,0:T(8,128)(2,1)} %q_ref.1) | copy-start | bytes 1179652
  42.4 3.5 %collective-permute-start.6 = (bf16[16,384,128]{2,1,0:T(8,128)(2,1)S(1)}, bf16[16,384,128]{2,1,0:T(8,128)(2,1)S(1)}, u32[]{:S(2)}, u32[]{:S(2)}) collective-permute-start(bf16[16,384,128]{2,1,0:T(8,128)(2,1)S(1)} %constant_dynamic-update-slice_fusion.mine_ref), channel_id=1, source_target_pairs={{0,1},{1,0},{4,5},{5,4},{8,9},{9,8},{12,13},{13,12},{16,17},{17,16... | collective-permute-start | bytes 4718600 | tf_op jit(solution)/shard_map/kv/ppermute | solution.py:38
  51.8 6.2 %collective-permute-start.7 = (bf16[96,512]{1,0:T(8,128)(2,1)S(1)}, bf16[96,512]{1,0:T(8,128)(2,1)S(1)}, u32[]{:S(2)}, u32[]{:S(2)}) collective-permute-start(bf16[96,512]{1,0:T(8,128)(2,1)S(1)} %get-tuple-element.18), channel_id=1, source_target_pairs={{0,1},{1,0},{4,5},{5,4},{8,9},{9,8},{12,13},{13,12},{16,17},{17,16... | collective-permute-start | bytes 294920 | tf_op jit(solution)/shard_map/rows/ppermute | solution.py:38
  52.1 14.7 %collective-permute-start.8 = (bf16[96,512]{1,0:T(8,128)(2,1)S(1)}, bf16[96,512]{1,0:T(8,128)(2,1)S(1)}, u32[]{:S(2)}, u32[]{:S(2)}) collective-permute-start(bf16[96,512]{1,0:T(8,128)(2,1)S(1)} %get-tuple-element.19), channel_id=1, source_target_pairs={{0,2},{1,3},{4,6},{5,7},{8,10},{9,11},{12,14},{13,15},{16,18},{17,... | collective-permute-start | bytes 294920 | tf_op jit(solution)/shard_map/rows/ppermute | solution.py:38
  58.0 13.6 %collective-permute-start.9 = (bf16[96,512]{1,0:T(8,128)(2,1)S(1)}, bf16[96,512]{1,0:T(8,128)(2,1)S(1)}, u32[]{:S(2)}, u32[]{:S(2)}) collective-permute-start(bf16[96,512]{1,0:T(8,128)(2,1)S(1)} %get-tuple-element.20), channel_id=1, source_target_pairs={{0,3},{1,2},{4,7},{5,6},{8,11},{9,10},{12,15},{13,14},{16,19},{17,... | collective-permute-start | bytes 294920 | tf_op jit(solution)/shard_map/rows/ppermute | solution.py:38
  71.6 15.8 %collective-permute-start.10 = (bf16[4,96,512]{2,1,0:T(8,128)(2,1)S(1)}, bf16[4,96,512]{2,1,0:T(8,128)(2,1)S(1)}, u32[]{:S(2)}, u32[]{:S(2)}) collective-permute-start(bf16[4,96,512]{2,1,0:T(8,128)(2,1)S(1)} %pad_maximum_fusion.1.refs_0_), channel_id=1, source_target_pairs={{0,16},{1,17},{4,20},{5,21},{8,24},{9,25},{12,28},{13,29},{16,32},... | collective-permute-start | bytes 1179656 | tf_op jit(solution)/shard_map/rows/ppermute | solution.py:38
  71.9 23.3 %collective-permute-start.11 = (bf16[4,96,512]{2,1,0:T(8,128)(2,1)S(1)}, bf16[4,96,512]{2,1,0:T(8,128)(2,1)S(1)}, u32[]{:S(2)}, u32[]{:S(2)}) collective-permute-start(bf16[4,96,512]{2,1,0:T(8,128)(2,1)S(1)} %pad_maximum_fusion.1.refs_0_), channel_id=1, source_target_pairs={{0,48},{1,49},{4,52},{5,53},{8,56},{9,57},{12,60},{13,61},{16,0},{... | collective-permute-start | bytes 1179656 | tf_op jit(solution)/shard_map/rows/ppermute | solution.py:38
  78.1 18.9 %collective-permute-start.12 = (bf16[4,96,512]{2,1,0:T(8,128)(2,1)S(1)}, bf16[4,96,512]{2,1,0:T(8,128)(2,1)S(1)}, u32[]{:S(2)}, u32[]{:S(2)}) collective-permute-start(bf16[4,96,512]{2,1,0:T(8,128)(2,1)S(1)} %pad_maximum_fusion.1.refs_0_), channel_id=1, source_target_pairs={{0,32},{1,33},{4,36},{5,37},{8,40},{9,41},{12,44},{13,45},{16,48},... | collective-permute-start | bytes 1179656 | tf_op jit(solution)/shard_map/rows/ppermute | solution.py:38
  80.1 47.3 %copy-start = (s32[4]{0:T(128)}, s32[4]{0:T(128)S(1)}, u32[]{:S(2)}) copy-start(s32[4]{0:T(128)S(1)} %pad_add_fusion.meta) | copy-start | bytes 52
  123.2 13.6 %collective-permute-start.19 = (bf16[96,2048]{1,0:T(8,128)(2,1)S(1)}, bf16[96,2048]{1,0:T(8,128)(2,1)S(1)}, u32[]{:S(2)}, u32[]{:S(2)}) collective-permute-start(bf16[96,2048]{1,0:T(8,128)(2,1)S(1)} %get-tuple-element.26), channel_id=1, source_target_pairs={{0,4},{1,5},{4,8},{5,9},{8,12},{9,13},{12,0},{13,1},{16,20},{17,21... | collective-permute-start | bytes 1179656 | tf_op jit(solution)/shard_map/sum/ppermute | solution.py:38
  124.7 13.5 %collective-permute-start.20 = (bf16[96,2048]{1,0:T(8,128)(2,1)S(1)}, bf16[96,2048]{1,0:T(8,128)(2,1)S(1)}, u32[]{:S(2)}, u32[]{:S(2)}) collective-permute-start(bf16[96,2048]{1,0:T(8,128)(2,1)S(1)} %get-tuple-element.27), channel_id=1, source_target_pairs={{0,12},{1,13},{4,0},{5,1},{8,4},{9,5},{12,8},{13,9},{16,28},{17,29... | collective-permute-start | bytes 1179656 | tf_op jit(solution)/shard_map/sum/ppermute | solution.py:38
  125.3 20.5 %collective-permute-start.21 = (bf16[96,2048]{1,0:T(8,128)(2,1)S(1)}, bf16[96,2048]{1,0:T(8,128)(2,1)S(1)}, u32[]{:S(2)}, u32[]{:S(2)}) collective-permute-start(bf16[96,2048]{1,0:T(8,128)(2,1)S(1)} %get-tuple-element.28), channel_id=1, source_target_pairs={{0,8},{1,9},{4,12},{5,13},{8,0},{9,1},{12,4},{13,5},{16,24},{17,25... | collective-permute-start | bytes 1179656 | tf_op jit(solution)/shard_map/sum/ppermute | solution.py:38
  134.6 17.5 %collective-permute-start.13 = (bf16[96,2048]{1,0:T(8,128)(2,1)S(1)}, bf16[96,2048]{1,0:T(8,128)(2,1)S(1)}, u32[]{:S(2)}, u32[]{:S(2)}) collective-permute-start(bf16[96,2048]{1,0:T(8,128)(2,1)S(1)} %get-tuple-element.22), channel_id=1, source_target_pairs={{0,4},{1,5},{4,8},{5,9},{8,12},{9,13},{12,0},{13,1},{16,20},{17,21... | collective-permute-start | bytes 1179656 | tf_op jit(solution)/shard_map/sum/ppermute | solution.py:38
  135.8 19.3 %collective-permute-start.14 = (bf16[96,2048]{1,0:T(8,128)(2,1)S(1)}, bf16[96,2048]{1,0:T(8,128)(2,1)S(1)}, u32[]{:S(2)}, u32[]{:S(2)}) collective-permute-start(bf16[96,2048]{1,0:T(8,128)(2,1)S(1)} %get-tuple-element.23), channel_id=1, source_target_pairs={{0,12},{1,13},{4,0},{5,1},{8,4},{9,5},{12,8},{13,9},{16,28},{17,29... | collective-permute-start | bytes 1179656 | tf_op jit(solution)/shard_map/sum/ppermute | solution.py:38
  136.7 25.0 %collective-permute-start.15 = (bf16[96,2048]{1,0:T(8,128)(2,1)S(1)}, bf16[96,2048]{1,0:T(8,128)(2,1)S(1)}, u32[]{:S(2)}, u32[]{:S(2)}) collective-permute-start(bf16[96,2048]{1,0:T(8,128)(2,1)S(1)} %get-tuple-element.24), channel_id=1, source_target_pairs={{0,8},{1,9},{4,12},{5,13},{8,0},{9,1},{12,4},{13,5},{16,24},{17,25... | collective-permute-start | bytes 1179656 | tf_op jit(solution)/shard_map/sum/ppermute | solution.py:38
  146.7 19.1 %collective-permute-start.22 = (bf16[24,2048]{1,0:T(8,128)(2,1)S(1)}, bf16[24,2048]{1,0:T(8,128)(2,1)S(1)}, u32[]{:S(2)}, u32[]{:S(2)}) collective-permute-start(bf16[24,2048]{1,0:T(8,128)(2,1)S(1)} %get-tuple-element.36), channel_id=1, source_target_pairs={{0,16},{1,17},{4,20},{5,21},{8,24},{9,25},{12,28},{13,29},{16,32},... | collective-permute-start | bytes 294920 | tf_op jit(solution)/shard_map/home/ppermute | solution.py:38
  148.2 19.4 %collective-permute-start.23 = (bf16[24,2048]{1,0:T(8,128)(2,1)S(1)}, bf16[24,2048]{1,0:T(8,128)(2,1)S(1)}, u32[]{:S(2)}, u32[]{:S(2)}) collective-permute-start(bf16[24,2048]{1,0:T(8,128)(2,1)S(1)} %get-tuple-element.35), channel_id=1, source_target_pairs={{0,48},{1,49},{4,52},{5,53},{8,56},{9,57},{12,60},{13,61},{16,0},{... | collective-permute-start | bytes 294920 | tf_op jit(solution)/shard_map/home/ppermute | solution.py:38
  152.1 15.5 %collective-permute-start.24 = (bf16[24,2048]{1,0:T(8,128)(2,1)S(1)}, bf16[24,2048]{1,0:T(8,128)(2,1)S(1)}, u32[]{:S(2)}, u32[]{:S(2)}) collective-permute-start(bf16[24,2048]{1,0:T(8,128)(2,1)S(1)} %get-tuple-element.34), channel_id=1, source_target_pairs={{0,32},{1,33},{4,36},{5,37},{8,40},{9,41},{12,44},{13,45},{16,48},... | collective-permute-start | bytes 294920 | tf_op jit(solution)/shard_map/home/ppermute | solution.py:38
  162.6 5.8 %collective-permute-start.16 = (bf16[24,2048]{1,0:T(8,128)(2,1)S(1)}, bf16[24,2048]{1,0:T(8,128)(2,1)S(1)}, u32[]{:S(2)}, u32[]{:S(2)}) collective-permute-start(bf16[24,2048]{1,0:T(8,128)(2,1)S(1)} %get-tuple-element.40), channel_id=1, source_target_pairs={{0,16},{1,17},{4,20},{5,21},{8,24},{9,25},{12,28},{13,29},{16,32},... | collective-permute-start | bytes 294920 | tf_op jit(solution)/shard_map/home/ppermute | solution.py:38
  164.1 5.4 %collective-permute-start.17 = (bf16[24,2048]{1,0:T(8,128)(2,1)S(1)}, bf16[24,2048]{1,0:T(8,128)(2,1)S(1)}, u32[]{:S(2)}, u32[]{:S(2)}) collective-permute-start(bf16[24,2048]{1,0:T(8,128)(2,1)S(1)} %get-tuple-element.39), channel_id=1, source_target_pairs={{0,48},{1,49},{4,52},{5,53},{8,56},{9,57},{12,60},{13,61},{16,0},{... | collective-permute-start | bytes 294920 | tf_op jit(solution)/shard_map/home/ppermute | solution.py:38
  165.8 6.1 %copy-start.2 = (bf16[24,2048]{1,0:T(8,128)(2,1)}, bf16[24,2048]{1,0:T(8,128)(2,1)S(1)}, u32[]{:S(2)}) copy-start(bf16[24,2048]{1,0:T(8,128)(2,1)S(1)} %collective-permute-done.22.refs_5_) | copy-start | bytes 294916
  165.8 6.1 %collective-permute-start.18 = (bf16[24,2048]{1,0:T(8,128)(2,1)S(1)}, bf16[24,2048]{1,0:T(8,128)(2,1)S(1)}, u32[]{:S(2)}, u32[]{:S(2)}) collective-permute-start(bf16[24,2048]{1,0:T(8,128)(2,1)S(1)} %get-tuple-element.38), channel_id=1, source_target_pairs={{0,32},{1,33},{4,36},{5,37},{8,40},{9,41},{12,44},{13,45},{16,48},... | collective-permute-start | bytes 294920 | tf_op jit(solution)/shard_map/home/ppermute | solution.py:38
  167.6 4.4 %copy-start.3 = (bf16[24,2048]{1,0:T(8,128)(2,1)}, bf16[24,2048]{1,0:T(8,128)(2,1)S(1)}, u32[]{:S(2)}) copy-start(bf16[24,2048]{1,0:T(8,128)(2,1)S(1)} %collective-permute-done.23.refs_6_) | copy-start | bytes 294916
  167.6 4.4 %copy-start.4 = (bf16[24,2048]{1,0:T(8,128)(2,1)}, bf16[24,2048]{1,0:T(8,128)(2,1)S(1)}, u32[]{:S(2)}) copy-start(bf16[24,2048]{1,0:T(8,128)(2,1)S(1)} %collective-permute-done.24.refs_7_) | copy-start | bytes 294916
  168.4 3.6 %copy-start.5 = (bf16[24,2048]{1,0:T(8,128)(2,1)}, bf16[24,2048]{1,0:T(8,128)(2,1)S(1)}, u32[]{:S(2)}) copy-start(bf16[24,2048]{1,0:T(8,128)(2,1)S(1)} %collective-permute-done.16.refs_1_) | copy-start | bytes 294916
  169.4 2.6 %copy-start.6 = (bf16[24,2048]{1,0:T(8,128)(2,1)}, bf16[24,2048]{1,0:T(8,128)(2,1)S(1)}, u32[]{:S(2)}) copy-start(bf16[24,2048]{1,0:T(8,128)(2,1)S(1)} %collective-permute-done.17.refs_2_) | copy-start | bytes 294916
  172.0 0.6 copy-start.7
Sparse Core Ops, SparseCore 0:
  9.2 106.7 all-gather.2

commit v3 on v2

--- a/solution.py
+++ b/solution.py
@@ -13,6 +13,7 @@
 HEADS = 4
 GROUPS, WIDE = 3, 256
 SPLIT = (2, 2)
+FLIPS = ((1, 3), (3, 1))
 X_STEPS = (0, 3, 1, 2)
 NZ, NX, NY = 8, 4, 4
 SCALE = HD ** (-0.5) * 1.4426950408889634
@@ -23,13 +24,13 @@
     return ((z % 4) * 4 + x) * 16 + y * 4 + (z // 4) * 2 + c
 
 
-def perm(dz=0, dx=0, dy=0, dc=0):
+def perm(dz=0, dx=0, flip=0, dc=0):
     pairs = []
     for z in range(NZ):
         for x in range(NX):
             for y in range(NY):
                 for c in range(2):
-                    to = flat((z + dz) % NZ, (x + dx) % NX, (y + dy) % NY, (c + dc) % 2)
+                    to = flat((z + dz) % NZ, (x + dx) % NX, y ^ flip, (c + dc) % 2)
                     pairs.append((flat(z, x, y, c), to))
     return pairs
 
@@ -184,10 +185,14 @@
     for r in range(1, 4):
         t += jnp.dot(rows[r], w_refs[r][0, 0, 0], preferred_element_type=jnp.float32)
     total[...] = t
-    for k in range(4):
-        at = lax.rem(y + k, 4) * 24
-        four = [total[pl.ds(pl.multiple_of(i * 96 + at, 8), 24), :] for i in range(4)]
-        outs[k][...] = jnp.concatenate(four).astype(jnp.bfloat16)
+    for h, (a, b) in enumerate(FLIPS):
+        for out, first in ((outs[2 * h], a), (outs[2 * h + 1], 0)):
+            for k, flip in enumerate((first, first ^ b)):
+                at = lax.bitwise_xor(y, flip) * 24
+                four = [
+                    total[pl.ds(pl.multiple_of(i * 96 + at, 8), 24), h * 512:(h + 1) * 512] for i in range(4)
+                ]
+                out[k] = jnp.concatenate(four).astype(jnp.bfloat16)
 
 
 def project(first, count, meta, pieces, w):
@@ -195,8 +200,8 @@
 
     def w_spec(r):
         return pl.BlockSpec(
-            (1, 1, 1, 512, 512),
-            lambda i, m: ((m[0] + r // 2) % 2, first + i // 2, (m[1] + r % 2) % 2, 0, i % 2),
+            (1, 1, 1, 512, 1024),
+            lambda i, m: ((m[0] + r // 2) % 2, first + i, (m[1] + r % 2) % 2, 0, 0),
         )
 
     with jax.named_scope("project"):
@@ -204,12 +209,12 @@
             project_kernel,
             grid_spec=pltpu.PrefetchScalarGridSpec(
                 num_scalar_prefetch=1,
-                grid=(2 * count,),
+                grid=(count,),
                 in_specs=[whole] * 4 + [w_spec(r) for r in range(4)],
-                out_specs=[pl.BlockSpec((96, 512), lambda i, m: (0, i))] * 4,
-                scratch_shapes=[pltpu.VMEM((4, 384, 512), jnp.bfloat16), pltpu.VMEM((384, 512), jnp.float32)],
+                out_specs=[pl.BlockSpec((2, 96, 512), lambda i, m: (0, 0, i))] * 4,
+                scratch_shapes=[pltpu.VMEM((4, 384, 512), jnp.bfloat16), pltpu.VMEM((384, 1024), jnp.float32)],
             ),
-            out_shape=[jax.ShapeDtypeStruct((96, count * 1024), jnp.bfloat16)] * 4,
+            out_shape=[jax.ShapeDtypeStruct((2, 96, count * 512), jnp.bfloat16)] * 4,
             compiler_params=pltpu.CompilerParams(vmem_limit_bytes=48 * 2**20),
             cost_estimate=pl.CostEstimate(
                 flops=count * 2 * 384 * 2048 * 1024, bytes_accessed=count * 5 * 10**6, transcendentals=0),
@@ -224,8 +229,10 @@
     for j, group in enumerate(SPLIT):
         for i, step in enumerate(X_STEPS):
             for g in range(group):
-                col = pl.multiple_of(((at_z + g) * 4 + lax.rem(x + step, 4)) * 1024, 1024)
-                out[:, pl.ds(col, 1024)] = refs[j * 4 + i][:, g * 1024:(g + 1) * 1024]
+                for h in range(2):
+                    col = pl.multiple_of(((at_z + g) * 4 + lax.rem(x + step, 4)) * 1024 + h * 512, 512)
+                    at = (h * group + g) * 512
+                    out[:, pl.ds(col, 512)] = refs[j * 4 + i][:, at:at + 512]
         at_z += group
 
 
@@ -288,8 +295,12 @@
         first += count
     for o in outs:
         with jax.named_scope("sum"):
-            got = [o[0], send(o[1], dy=1), send(o[3], dy=-1), send(o[2], dy=2)]
-            total = sum(g.astype(jnp.float32) for g in got).astype(jnp.bfloat16)
+            halves = []
+            for h, (a, b) in enumerate(FLIPS):
+                got, kept = send(o[2 * h], flip=a).astype(jnp.float32), o[2 * h + 1].astype(jnp.float32)
+                last = send((kept[1] + got[1]).astype(jnp.bfloat16), flip=b)
+                halves.append((kept[0] + got[0] + last.astype(jnp.float32)).astype(jnp.bfloat16))
+            total = jnp.concatenate(halves, axis=1)
         with jax.named_scope("home"):
             own, down, up, far = [total[i * 24:(i + 1) * 24] for i in range(4)]
             up, down = send(up, dx=1), send(down, dx=-1)

time: 182 us -> 176 us (0.967)
  starting transfers between devices: 44.8 us -> 39.9 us
  other arithmetic: 2.86 us -> 4.73 us
    ppermute x25 -> x27, starting transfers between devices: 44.8 us -> 39.9 us  [send(): return lax.ppermute(a, ('ctx', 'tp'), perm(**step))]
    ppermute x25 -> x27, waiting for transfers between devices: 75.7 us -> 71 us  [send(): return lax.ppermute(a, ('ctx', 'tp'), perm(**step))]
    all_gather x1, waiting for transfers between devices: 18.9 us -> 22 us  [local(): lax.all_gather(out_weight, ('ctx', 'tp'), axis_index_groups=groups, axis=0)]
  transfers between devices with their start and end apart: 26 -> 28, of which waited for: 18 -> 17; matrix products, arithmetic and copies ran while one was open for 2% -> 3% of each run, Pallas kernels for 7% -> 8%
where the time goes in v3:
time: 176 us
  waiting for transfers between devices  93.7 us (53%)
  starting transfers between devices  39.9 us (23%)
  Pallas kernels  22.9 us (13%)
  between operations  14 us (8%)
  other arithmetic  4.73 us (3%)
    ppermute x27, waiting for transfers between devices, send(): return lax.ppermute(a, ('ctx', 'tp'), perm(**step))  71 us
    ppermute x27, starting transfers between devices, send(): return lax.ppermute(a, ('ctx', 'tp'), perm(**step))  39.9 us
    all_gather x1, waiting for transfers between devices, local(): lax.all_gather(out_weight, ('ctx', 'tp'), axis_index_groups=groups, axis=0)  22 us
    pallas_call x2, Pallas kernels, project(): pl.pallas_call(project_kernel, grid_spec=pltpu.PrefetchScalarGridSpec(num...  13.6 us
    pallas_call x1, Pallas kernels, attend(): pl.pallas_call(attend_kernel, out_shape=[jax.ShapeDtypeStruct((96, HEADS...  7.1 us
  transfers between devices with their start and end apart: 28, of which 17 were waited for; matrix products, arithmetic and copies ran while one was open for 3% of the time, Pallas kernels for 8%

profile of v3, /device:TPU:8, one launch (start us, length us, event | category | flops | bytes accessed | tf_op | source)
XLA Modules:
  0.0 176.1 jit_solution(3914982049474948775)
XLA Ops:
  6.5 0.7 all-gather.3.cloned.1.call-update
  7.4 1.2 dynamic-slice_select_fusion
  8.7 2.0 %collective-permute-start = (bf16[384,128]{1,0:T(8,128)(2,1)S(1)}, bf16[384,128]{1,0:T(8,128)(2,1)S(1)}, u32[]{:S(2)}, u32[]{:S(2)}) collective-permute-start(bf16[384,128]{1,0:T(8,128)(2,1)S(1)} %get-tuple-element.32), channel_id=1, source_target_pairs={{0,64},{1,65},{4,68},{5,69},{8,72},{9,73},{12,76},{13,77},{16,80},... | collective-permute-start | bytes 294920 | tf_op jit(solution)/shard_map/kv/ppermute | solution.py:39
  10.7 4.0 %collective-permute-start.1 = (bf16[384,128]{1,0:T(8,128)(2,1)S(1)}, bf16[384,128]{1,0:T(8,128)(2,1)S(1)}, u32[]{:S(2)}, u32[]{:S(2)}) collective-permute-start(bf16[384,128]{1,0:T(8,128)(2,1)S(1)} %get-tuple-element.33), channel_id=1, source_target_pairs={{0,194},{1,195},{4,198},{5,199},{8,202},{9,203},{12,206},{13,207},... | collective-permute-start | bytes 294920 | tf_op jit(solution)/shard_map/kv/ppermute | solution.py:39
  14.7 1.0 constant_dynamic-update-slice_fusion.6
  15.7 2.4 %collective-permute-done = bf16[384,128]{1,0:T(8,128)(2,1)S(1)} collective-permute-done((bf16[384,128]{1,0:T(8,128)(2,1)S(1)}, bf16[384,128]{1,0:T(8,128)(2,1)S(1)}, u32[]{:S(2)}, u32[]{:S(2)}) %collective-permute-start) | collective-permute-done | bytes 98336 | tf_op jit(solution)/shard_map/kv/ppermute | solution.py:39
  18.1 4.9 %collective-permute-done.2 = bf16[384,128]{1,0:T(8,128)(2,1)S(1)} collective-permute-done((bf16[384,128]{1,0:T(8,128)(2,1)S(1)}, bf16[384,128]{1,0:T(8,128)(2,1)S(1)}, u32[]{:S(2)}, u32[]{:S(2)}) %collective-permute-start.2) | collective-permute-done | bytes 98336 | tf_op jit(solution)/shard_map/kv/ppermute | solution.py:39
  23.0 1.6 collective-permute-start.3
  24.6 1.7 collective-permute-start.4
  26.4 1.8 %collective-permute-start.5 = (bf16[4,384,128]{2,1,0:T(8,128)(2,1)S(1)}, bf16[4,384,128]{2,1,0:T(8,128)(2,1)S(1)}, u32[]{:S(2)}, u32[]{:S(2)}) collective-permute-start(bf16[4,384,128]{2,1,0:T(8,128)(2,1)S(1)} %pad_maximum_fusion), channel_id=1, source_target_pairs={{0,32},{1,33},{4,36},{5,37},{8,40},{9,41},{12,44},{13,45},{16,48},... | collective-permute-start | bytes 1179656 | tf_op jit(solution)/shard_map/kv/ppermute | solution.py:39
  28.2 7.2 %collective-permute-done.3 = bf16[4,384,128]{2,1,0:T(8,128)(2,1)S(1)} collective-permute-done((bf16[4,384,128]{2,1,0:T(8,128)(2,1)S(1)}, bf16[4,384,128]{2,1,0:T(8,128)(2,1)S(1)}, u32[]{:S(2)}, u32[]{:S(2)}) %collective-permute-start.3) | collective-permute-done | bytes 393248 | tf_op jit(solution)/shard_map/kv/ppermute | solution.py:39
  35.4 5.3 %collective-permute-done.4 = bf16[4,384,128]{2,1,0:T(8,128)(2,1)S(1)} collective-permute-done((bf16[4,384,128]{2,1,0:T(8,128)(2,1)S(1)}, bf16[4,384,128]{2,1,0:T(8,128)(2,1)S(1)}, u32[]{:S(2)}, u32[]{:S(2)}) %collective-permute-start.4) | collective-permute-done | bytes 393248 | tf_op jit(solution)/shard_map/kv/ppermute | solution.py:39
  40.8 1.6 collective-permute-done.5
  42.4 0.1 collective-permute-start.6
  42.7 0.1 concatenate.13.meta
  42.8 3.2 %collective-permute-done.6.theirs_ref = bf16[16,384,128]{2,1,0:T(8,128)(2,1)S(1)} collective-permute-done((bf16[16,384,128]{2,1,0:T(8,128)(2,1)S(1)}, bf16[16,384,128]{2,1,0:T(8,128)(2,1)S(1)}, u32[]{:S(2)}, u32[]{:S(2)}) %collective-permute-start.6) | collective-permute-done | bytes 1572896 | tf_op jit(solution)/shard_map/kv/ppermute | solution.py:39
  45.9 7.1 %attend.1 = (bf16[96,512]{1,0:T(8,128)(2,1)S(1)}, bf16[96,512]{1,0:T(8,128)(2,1)S(1)}, bf16[96,512]{1,0:T(8,128)(2,1)S(1)}, bf16[96,512]{1,0:T(8,128)(2,1)S(1)}) custom-call(s32[55]{0:T(128)S(1)} %concatenate.13.meta, bf16[384,512]{1,0:T(8,128)(2,1)S(1)} %copy-done.1, bf16[16,384,128]{2,1,0:T(8,128)(2,1)S(1)} %constant_dynamic-update-slice_fusion.mine_ref, ...), custom_call_target="tpu_custom_call" | custom-call | flops 4000000000 | bytes 4000000 | tf_op jit(solution)/shard_map/attend/attend/pallas_call | solution.py:153
  53.1 0.2 collective-permute-start.7
  53.3 6.0 %collective-permute-start.8 = (bf16[96,512]{1,0:T(8,128)(2,1)S(1)}, bf16[96,512]{1,0:T(8,128)(2,1)S(1)}, u32[]{:S(2)}, u32[]{:S(2)}) collective-permute-start(bf16[96,512]{1,0:T(8,128)(2,1)S(1)} %get-tuple-element.19), channel_id=1, source_target_pairs={{0,2},{1,3},{4,6},{5,7},{8,10},{9,11},{12,14},{13,15},{16,18},{17,... | collective-permute-start | bytes 294920 | tf_op jit(solution)/shard_map/rows/ppermute | solution.py:39
  59.3 8.2 %collective-permute-done.8 = bf16[96,512]{1,0:T(8,128)(2,1)S(1)} collective-permute-done((bf16[96,512]{1,0:T(8,128)(2,1)S(1)}, bf16[96,512]{1,0:T(8,128)(2,1)S(1)}, u32[]{:S(2)}, u32[]{:S(2)}) %collective-permute-start.8) | collective-permute-done | bytes 98336 | tf_op jit(solution)/shard_map/rows/ppermute | solution.py:39
  67.5 5.2 %collective-permute-done.9 = bf16[96,512]{1,0:T(8,128)(2,1)S(1)} collective-permute-done((bf16[96,512]{1,0:T(8,128)(2,1)S(1)}, bf16[96,512]{1,0:T(8,128)(2,1)S(1)}, u32[]{:S(2)}, u32[]{:S(2)}) %collective-permute-start.9) | collective-permute-done | bytes 98336 | tf_op jit(solution)/shard_map/rows/ppermute | solution.py:39
  72.8 0.1 collective-permute-start.10
  72.9 3.2 %collective-permute-start.11 = (bf16[4,96,512]{2,1,0:T(8,128)(2,1)S(1)}, bf16[4,96,512]{2,1,0:T(8,128)(2,1)S(1)}, u32[]{:S(2)}, u32[]{:S(2)}) collective-permute-start(bf16[4,96,512]{2,1,0:T(8,128)(2,1)S(1)} %pad_maximum_fusion.1.refs_0_), channel_id=1, source_target_pairs={{0,48},{1,49},{4,52},{5,53},{8,56},{9,57},{12,60},{13,61},{16,0},{... | collective-permute-start | bytes 1179656 | tf_op jit(solution)/shard_map/rows/ppermute | solution.py:39
  76.1 0.1 pad_add_fusion.meta
  76.2 17.8 %collective-permute-done.10.refs_1_ = bf16[4,96,512]{2,1,0:T(8,128)(2,1)S(1)} collective-permute-done((bf16[4,96,512]{2,1,0:T(8,128)(2,1)S(1)}, bf16[4,96,512]{2,1,0:T(8,128)(2,1)S(1)}, u32[]{:S(2)}, u32[]{:S(2)}) %collective-permute-start.10) | collective-permute-done | bytes 393248 | tf_op jit(solution)/shard_map/rows/ppermute | solution.py:39
  94.0 22.0 %all-gather.3.cloned.1.call-done = bf16[8192,1024]{1,0:T(8,128)(2,1)} async-done(((bf16[512,1024]{1,0:T(8,128)(2,1)}), bf16[8192,1024]{1,0:T(8,128)(2,1)}) %all-gather.3.cloned.1.call-update) | async-done | bytes 16777232 | tf_op jit(solution)/shard_map/weights/all_gather | solution.py:268
  115.9 6.8 %project.3 = (bf16[2,96,1024]{2,1,0:T(8,128)(2,1)S(1)}, bf16[2,96,1024]{2,1,0:T(8,128)(2,1)S(1)}, bf16[2,96,1024]{2,1,0:T(8,128)(2,1)S(1)}, bf16[2,96,1024]{2,1,0:T(8,128)(2,1)S(1)}) custom-call(s32[4]{0:T(128)S(1)} %pad_add_fusion.meta, bf16[4,96,512]{2,1,0:T(8,128)(2,1)S(1)} %pad_maximum_fusion.1.refs_0_, ...), custom_call_target="tpu_custom_call" | custom-call | flops 3221225472 | bytes 10000000 | tf_op jit(solution)/shard_map/project/project/pallas_call | solution.py:208
  122.8 0.6 collective-permute-start.20
  123.4 2.1 %collective-permute-start.22 = (bf16[2,96,1024]{2,1,0:T(8,128)(2,1)S(1)}, bf16[2,96,1024]{2,1,0:T(8,128)(2,1)S(1)}, u32[]{:S(2)}, u32[]{:S(2)}) collective-permute-start(bf16[2,96,1024]{2,1,0:T(8,128)(2,1)S(1)} %get-tuple-element.28), channel_id=1, source_target_pairs={{0,12},{1,13},{4,8},{5,9},{8,4},{9,5},{12,0},{13,1},{16,28},{17,29... | collective-permute-start | bytes 1179656 | tf_op jit(solution)/shard_map/sum/ppermute | solution.py:39
  125.5 6.8 %project.2 = (bf16[2,96,1024]{2,1,0:T(8,128)(2,1)S(1)}, bf16[2,96,1024]{2,1,0:T(8,128)(2,1)S(1)}, bf16[2,96,1024]{2,1,0:T(8,128)(2,1)S(1)}, bf16[2,96,1024]{2,1,0:T(8,128)(2,1)S(1)}) custom-call(s32[4]{0:T(128)S(1)} %pad_add_fusion.meta, bf16[4,96,512]{2,1,0:T(8,128)(2,1)S(1)} %pad_maximum_fusion.1.refs_0_, ...), custom_call_target="tpu_custom_call" | custom-call | flops 3221225472 | bytes 10000000 | tf_op jit(solution)/shard_map/project/project/pallas_call | solution.py:208
  132.3 0.1 convert_element_type.84
  132.4 0.1 convert_element_type.90
  132.5 1.5 collective-permute-start.13
  134.0 0.1 convert_element_type.72
  134.1 0.6 collective-permute-start.15
  134.7 0.1 convert_element_type.78
  134.8 0.1 convert_element_type.85
  134.9 1.6 collective-permute-start.21
  136.5 0.1 convert_element_type.91
  136.6 1.9 %collective-permute-start.23 = (bf16[96,1024]{1,0:T(8,128)(2,1)S(1)}, bf16[96,1024]{1,0:T(8,128)(2,1)S(1)}, u32[]{:S(2)}, u32[]{:S(2)}) collective-permute-start(bf16[96,1024]{1,0:T(8,128)(2,1)S(1)} %fusion.19), channel_id=1, source_target_pairs={{0,4},{1,5},{4,0},{5,1},{8,12},{9,13},{12,8},{13,9},{16,20},{17,21... | collective-permute-start | bytes 589832 | tf_op jit(solution)/shard_map/sum/ppermute | solution.py:39
  138.5 6.1 %collective-permute-done.13 = bf16[2,96,1024]{2,1,0:T(8,128)(2,1)S(1)} collective-permute-done((bf16[2,96,1024]{2,1,0:T(8,128)(2,1)S(1)}, bf16[2,96,1024]{2,1,0:T(8,128)(2,1)S(1)}, u32[]{:S(2)}, u32[]{:S(2)}) %collective-permute-start.13) | collective-permute-done | bytes 393248 | tf_op jit(solution)/shard_map/sum/ppermute | solution.py:39
  144.6 0.1 convert_element_type.73
  144.7 0.1 collective-permute-start.14
  144.8 1.4 collective-permute-done.15
  146.2 0.1 convert_element_type.79
  146.4 1.9 %collective-permute-start.16 = (bf16[96,1024]{1,0:T(8,128)(2,1)S(1)}, bf16[96,1024]{1,0:T(8,128)(2,1)S(1)}, u32[]{:S(2)}, u32[]{:S(2)}) collective-permute-start(bf16[96,1024]{1,0:T(8,128)(2,1)S(1)} %fusion.17), channel_id=1, source_target_pairs={{0,4},{1,5},{4,0},{5,1},{8,12},{9,13},{12,8},{13,9},{16,20},{17,21... | collective-permute-start | bytes 589832 | tf_op jit(solution)/shard_map/sum/ppermute | solution.py:39
  148.2 2.2 %collective-permute-done.21 = bf16[96,1024]{1,0:T(8,128)(2,1)S(1)} collective-permute-done((bf16[96,1024]{1,0:T(8,128)(2,1)S(1)}, bf16[96,1024]{1,0:T(8,128)(2,1)S(1)}, u32[]{:S(2)}, u32[]{:S(2)}) %collective-permute-start.21) | collective-permute-done | bytes 196640 | tf_op jit(solution)/shard_map/sum/ppermute | solution.py:39
  150.4 0.1 fusion.7
  150.5 0.1 fusion.3
  150.6 0.7 pad_maximum_fusion.2
  151.3 1.5 collective-permute-start.24
  152.7 1.8 %collective-permute-start.25 = (bf16[24,2048]{1,0:T(8,128)(2,1)S(1)}, bf16[24,2048]{1,0:T(8,128)(2,1)S(1)}, u32[]{:S(2)}, u32[]{:S(2)}) collective-permute-start(bf16[24,2048]{1,0:T(8,128)(2,1)S(1)} %get-tuple-element.37), channel_id=1, source_target_pairs={{0,48},{1,49},{4,52},{5,53},{8,56},{9,57},{12,60},{13,61},{16,0},{... | collective-permute-start | bytes 294920 | tf_op jit(solution)/shard_map/home/ppermute | solution.py:39
  154.5 1.8 %collective-permute-start.26 = (bf16[24,2048]{1,0:T(8,128)(2,1)S(1)}, bf16[24,2048]{1,0:T(8,128)(2,1)S(1)}, u32[]{:S(2)}, u32[]{:S(2)}) collective-permute-start(bf16[24,2048]{1,0:T(8,128)(2,1)S(1)} %get-tuple-element.34), channel_id=1, source_target_pairs={{0,32},{1,33},{4,36},{5,37},{8,40},{9,41},{12,44},{13,45},{16,48},... | collective-permute-start | bytes 294920 | tf_op jit(solution)/shard_map/home/ppermute | solution.py:39
  156.3 0.1 fusion.15
  156.4 0.7 pad_maximum_fusion.3
  157.1 0.6 collective-permute-start.17
  157.7 2.7 %collective-permute-start.18 = (bf16[24,2048]{1,0:T(8,128)(2,1)S(1)}, bf16[24,2048]{1,0:T(8,128)(2,1)S(1)}, u32[]{:S(2)}, u32[]{:S(2)}) collective-permute-start(bf16[24,2048]{1,0:T(8,128)(2,1)S(1)} %get-tuple-element.41), channel_id=1, source_target_pairs={{0,48},{1,49},{4,52},{5,53},{8,56},{9,57},{12,60},{13,61},{16,0},{... | collective-permute-start | bytes 294920 | tf_op jit(solution)/shard_map/home/ppermute | solution.py:39
  160.3 0.6 collective-permute-start.19
  160.9 0.4 collective-permute-done.26.refs_7_
  161.3 1.7 collective-permute-done.17.refs_1_
  163.0 0.6 collective-permute-done.18.refs_2_
  163.6 2.9 %collective-permute-done.19.refs_3_ = bf16[24,2048]{1,0:T(8,128)(2,1)S(1)} collective-permute-done((bf16[24,2048]{1,0:T(8,128)(2,1)S(1)}, bf16[24,2048]{1,0:T(8,128)(2,1)S(1)}, u32[]{:S(2)}, u32[]{:S(2)}) %collective-permute-start.19) | collective-permute-done | bytes 98336 | tf_op jit(solution)/shard_map/home/ppermute | solution.py:39
  166.5 0.6 copy-done.7
  167.1 2.2 %assemble.1 = bf16[24,16384]{1,0:T(8,128)(2,1)} custom-call(s32[4]{0:T(128)} %copy-done, bf16[24,2048]{1,0:T(8,128)(2,1)} %get-tuple-element.39.refs_0_, bf16[24,2048]{1,0:T(8,128)(2,1)} %copy-done.5, bf16[24,2048]{1,0:T(8,128)(2,1)} %copy-done.6, bf16[24,2048]{1,0:T(8,128)(2,1)} %copy-done.7, bf16[24,2048]{1,0:T(8,128)(2,1)} %get-tuple-element.35.refs_4_, ...), custom_call_target="tpu_custom_call" | custom-call | tf_op jit(solution)/shard_map/assemble/pallas_call | solution.py:240
  (47 shorter events, 0.6 us)
Async XLA Ops:
  6.5 109.4 %all-gather.3.cloned.1.call-start = ((), (), s32[]{:S(2)}) async-start(), calls=%async_computation | async-start | bytes 17825792 | tf_op jit(solution)/shard_map/weights/all_gather | solution.py:268
  8.7 9.4 %collective-permute-start = (bf16[384,128]{1,0:T(8,128)(2,1)S(1)}, bf16[384,128]{1,0:T(8,128)(2,1)S(1)}, u32[]{:S(2)}, u32[]{:S(2)}) collective-permute-start(bf16[384,128]{1,0:T(8,128)(2,1)S(1)} %get-tuple-element.32), channel_id=1, source_target_pairs={{0,64},{1,65},{4,68},{5,69},{8,72},{9,73},{12,76},{13,77},{16,80},... | collective-permute-start | bytes 294920 | tf_op jit(solution)/shard_map/kv/ppermute | solution.py:39
  10.7 7.4 %collective-permute-start.1 = (bf16[384,128]{1,0:T(8,128)(2,1)S(1)}, bf16[384,128]{1,0:T(8,128)(2,1)S(1)}, u32[]{:S(2)}, u32[]{:S(2)}) collective-permute-start(bf16[384,128]{1,0:T(8,128)(2,1)S(1)} %get-tuple-element.33), channel_id=1, source_target_pairs={{0,194},{1,195},{4,198},{5,199},{8,202},{9,203},{12,206},{13,207},... | collective-permute-start | bytes 294920 | tf_op jit(solution)/shard_map/kv/ppermute | solution.py:39
  14.7 8.3 %collective-permute-start.2 = (bf16[384,128]{1,0:T(8,128)(2,1)S(1)}, bf16[384,128]{1,0:T(8,128)(2,1)S(1)}, u32[]{:S(2)}, u32[]{:S(2)}) collective-permute-start(bf16[384,128]{1,0:T(8,128)(2,1)S(1)} %get-tuple-element.31), channel_id=1, source_target_pairs={{0,128},{1,129},{4,132},{5,133},{8,136},{9,137},{12,140},{13,141},... | collective-permute-start | bytes 294920 | tf_op jit(solution)/shard_map/kv/ppermute | solution.py:39
  23.0 12.4 %collective-permute-start.3 = (bf16[4,384,128]{2,1,0:T(8,128)(2,1)S(1)}, bf16[4,384,128]{2,1,0:T(8,128)(2,1)S(1)}, u32[]{:S(2)}, u32[]{:S(2)}) collective-permute-start(bf16[4,384,128]{2,1,0:T(8,128)(2,1)S(1)} %pad_maximum_fusion), channel_id=1, source_target_pairs={{0,16},{1,17},{4,20},{5,21},{8,24},{9,25},{12,28},{13,29},{16,32},... | collective-permute-start | bytes 1179656 | tf_op jit(solution)/shard_map/kv/ppermute | solution.py:39
  24.6 16.1 %collective-permute-start.4 = (bf16[4,384,128]{2,1,0:T(8,128)(2,1)S(1)}, bf16[4,384,128]{2,1,0:T(8,128)(2,1)S(1)}, u32[]{:S(2)}, u32[]{:S(2)}) collective-permute-start(bf16[4,384,128]{2,1,0:T(8,128)(2,1)S(1)} %pad_maximum_fusion), channel_id=1, source_target_pairs={{0,48},{1,49},{4,52},{5,53},{8,56},{9,57},{12,60},{13,61},{16,0},{... | collective-permute-start | bytes 1179656 | tf_op jit(solution)/shard_map/kv/ppermute | solution.py:39
  26.4 16.0 %collective-permute-start.5 = (bf16[4,384,128]{2,1,0:T(8,128)(2,1)S(1)}, bf16[4,384,128]{2,1,0:T(8,128)(2,1)S(1)}, u32[]{:S(2)}, u32[]{:S(2)}) collective-permute-start(bf16[4,384,128]{2,1,0:T(8,128)(2,1)S(1)} %pad_maximum_fusion), channel_id=1, source_target_pairs={{0,32},{1,33},{4,36},{5,37},{8,40},{9,41},{12,44},{13,45},{16,48},... | collective-permute-start | bytes 1179656 | tf_op jit(solution)/shard_map/kv/ppermute | solution.py:39
  28.2 14.5 %copy-start.8 = (s32[32]{0:T(128)S(1)}, s32[32]{0:T(128)}, u32[]{:S(2)}) copy-start(s32[32]{0:T(128)} %param.10) | copy-start | bytes 388
  28.2 14.5 %copy-start.9 = (s32[4]{0:T(128)S(1)}, s32[4]{0:T(128)}, u32[]{:S(2)}) copy-start(s32[4]{0:T(128)} %param.11) | copy-start | bytes 52
  28.2 17.8 %copy-start.1 = (bf16[384,512]{1,0:T(8,128)(2,1)S(1)}, bf16[384,512]{1,0:T(8,128)(2,1)}, u32[]{:S(2)}) copy-start(bf16[384,512]{1,0:T(8,128)(2,1)} %q_ref.1) | copy-start | bytes 1179652
  42.4 3.5 %collective-permute-start.6 = (bf16[16,384,128]{2,1,0:T(8,128)(2,1)S(1)}, bf16[16,384,128]{2,1,0:T(8,128)(2,1)S(1)}, u32[]{:S(2)}, u32[]{:S(2)}) collective-permute-start(bf16[16,384,128]{2,1,0:T(8,128)(2,1)S(1)} %constant_dynamic-update-slice_fusion.mine_ref), channel_id=1, source_target_pairs={{0,1},{1,0},{4,5},{5,4},{8,9},{9,8},{12,13},{13,12},{16,17},{17,16... | collective-permute-start | bytes 4718600 | tf_op jit(solution)/shard_map/kv/ppermute | solution.py:39
  53.1 6.2 %collective-permute-start.7 = (bf16[96,512]{1,0:T(8,128)(2,1)S(1)}, bf16[96,512]{1,0:T(8,128)(2,1)S(1)}, u32[]{:S(2)}, u32[]{:S(2)}) collective-permute-start(bf16[96,512]{1,0:T(8,128)(2,1)S(1)} %get-tuple-element.18), channel_id=1, source_target_pairs={{0,1},{1,0},{4,5},{5,4},{8,9},{9,8},{12,13},{13,12},{16,17},{17,16... | collective-permute-start | bytes 294920 | tf_op jit(solution)/shard_map/rows/ppermute | solution.py:39
  53.3 14.2 %collective-permute-start.8 = (bf16[96,512]{1,0:T(8,128)(2,1)S(1)}, bf16[96,512]{1,0:T(8,128)(2,1)S(1)}, u32[]{:S(2)}, u32[]{:S(2)}) collective-permute-start(bf16[96,512]{1,0:T(8,128)(2,1)S(1)} %get-tuple-element.19), channel_id=1, source_target_pairs={{0,2},{1,3},{4,6},{5,7},{8,10},{9,11},{12,14},{13,15},{16,18},{17,... | collective-permute-start | bytes 294920 | tf_op jit(solution)/shard_map/rows/ppermute | solution.py:39
  59.2 13.5 %collective-permute-start.9 = (bf16[96,512]{1,0:T(8,128)(2,1)S(1)}, bf16[96,512]{1,0:T(8,128)(2,1)S(1)}, u32[]{:S(2)}, u32[]{:S(2)}) collective-permute-start(bf16[96,512]{1,0:T(8,128)(2,1)S(1)} %get-tuple-element.20), channel_id=1, source_target_pairs={{0,3},{1,2},{4,7},{5,6},{8,11},{9,10},{12,15},{13,14},{16,19},{17,... | collective-permute-start | bytes 294920 | tf_op jit(solution)/shard_map/rows/ppermute | solution.py:39
  72.8 21.2 %collective-permute-start.10 = (bf16[4,96,512]{2,1,0:T(8,128)(2,1)S(1)}, bf16[4,96,512]{2,1,0:T(8,128)(2,1)S(1)}, u32[]{:S(2)}, u32[]{:S(2)}) collective-permute-start(bf16[4,96,512]{2,1,0:T(8,128)(2,1)S(1)} %pad_maximum_fusion.1.refs_0_), channel_id=1, source_target_pairs={{0,16},{1,17},{4,20},{5,21},{8,24},{9,25},{12,28},{13,29},{16,32},... | collective-permute-start | bytes 1179656 | tf_op jit(solution)/shard_map/rows/ppermute | solution.py:39
  72.9 21.1 %collective-permute-start.11 = (bf16[4,96,512]{2,1,0:T(8,128)(2,1)S(1)}, bf16[4,96,512]{2,1,0:T(8,128)(2,1)S(1)}, u32[]{:S(2)}, u32[]{:S(2)}) collective-permute-start(bf16[4,96,512]{2,1,0:T(8,128)(2,1)S(1)} %pad_maximum_fusion.1.refs_0_), channel_id=1, source_target_pairs={{0,48},{1,49},{4,52},{5,53},{8,56},{9,57},{12,60},{13,61},{16,0},{... | collective-permute-start | bytes 1179656 | tf_op jit(solution)/shard_map/rows/ppermute | solution.py:39
  76.1 17.9 %collective-permute-start.12 = (bf16[4,96,512]{2,1,0:T(8,128)(2,1)S(1)}, bf16[4,96,512]{2,1,0:T(8,128)(2,1)S(1)}, u32[]{:S(2)}, u32[]{:S(2)}) collective-permute-start(bf16[4,96,512]{2,1,0:T(8,128)(2,1)S(1)} %pad_maximum_fusion.1.refs_0_), channel_id=1, source_target_pairs={{0,32},{1,33},{4,36},{5,37},{8,40},{9,41},{12,44},{13,45},{16,48},... | collective-permute-start | bytes 1179656 | tf_op jit(solution)/shard_map/rows/ppermute | solution.py:39
  76.2 49.4 %copy-start = (s32[4]{0:T(128)}, s32[4]{0:T(128)S(1)}, u32[]{:S(2)}) copy-start(s32[4]{0:T(128)S(1)} %pad_add_fusion.meta) | copy-start | bytes 52
  122.8 12.0 %collective-permute-start.20 = (bf16[2,96,1024]{2,1,0:T(8,128)(2,1)S(1)}, bf16[2,96,1024]{2,1,0:T(8,128)(2,1)S(1)}, u32[]{:S(2)}, u32[]{:S(2)}) collective-permute-start(bf16[2,96,1024]{2,1,0:T(8,128)(2,1)S(1)} %get-tuple-element.26), channel_id=1, source_target_pairs={{0,4},{1,5},{4,0},{5,1},{8,12},{9,13},{12,8},{13,9},{16,20},{17,21... | collective-permute-start | bytes 1179656 | tf_op jit(solution)/shard_map/sum/ppermute | solution.py:39
  123.4 13.1 %collective-permute-start.22 = (bf16[2,96,1024]{2,1,0:T(8,128)(2,1)S(1)}, bf16[2,96,1024]{2,1,0:T(8,128)(2,1)S(1)}, u32[]{:S(2)}, u32[]{:S(2)}) collective-permute-start(bf16[2,96,1024]{2,1,0:T(8,128)(2,1)S(1)} %get-tuple-element.28), channel_id=1, source_target_pairs={{0,12},{1,13},{4,8},{5,9},{8,4},{9,5},{12,0},{13,1},{16,28},{17,29... | collective-permute-start | bytes 1179656 | tf_op jit(solution)/shard_map/sum/ppermute | solution.py:39
  132.5 12.1 %collective-permute-start.13 = (bf16[2,96,1024]{2,1,0:T(8,128)(2,1)S(1)}, bf16[2,96,1024]{2,1,0:T(8,128)(2,1)S(1)}, u32[]{:S(2)}, u32[]{:S(2)}) collective-permute-start(bf16[2,96,1024]{2,1,0:T(8,128)(2,1)S(1)} %get-tuple-element.22), channel_id=1, source_target_pairs={{0,4},{1,5},{4,0},{5,1},{8,12},{9,13},{12,8},{13,9},{16,20},{17,21... | collective-permute-start | bytes 1179656 | tf_op jit(solution)/shard_map/sum/ppermute | solution.py:39
  134.1 12.1 %collective-permute-start.15 = (bf16[2,96,1024]{2,1,0:T(8,128)(2,1)S(1)}, bf16[2,96,1024]{2,1,0:T(8,128)(2,1)S(1)}, u32[]{:S(2)}, u32[]{:S(2)}) collective-permute-start(bf16[2,96,1024]{2,1,0:T(8,128)(2,1)S(1)} %get-tuple-element.24), channel_id=1, source_target_pairs={{0,12},{1,13},{4,8},{5,9},{8,4},{9,5},{12,0},{13,1},{16,28},{17,29... | collective-permute-start | bytes 1179656 | tf_op jit(solution)/shard_map/sum/ppermute | solution.py:39
  134.9 15.5 %collective-permute-start.21 = (bf16[96,1024]{1,0:T(8,128)(2,1)S(1)}, bf16[96,1024]{1,0:T(8,128)(2,1)S(1)}, u32[]{:S(2)}, u32[]{:S(2)}) collective-permute-start(bf16[96,1024]{1,0:T(8,128)(2,1)S(1)} %fusion.18), channel_id=1, source_target_pairs={{0,12},{1,13},{4,8},{5,9},{8,4},{9,5},{12,0},{13,1},{16,28},{17,29... | collective-permute-start | bytes 589832 | tf_op jit(solution)/shard_map/sum/ppermute | solution.py:39
  136.6 13.9 %collective-permute-start.23 = (bf16[96,1024]{1,0:T(8,128)(2,1)S(1)}, bf16[96,1024]{1,0:T(8,128)(2,1)S(1)}, u32[]{:S(2)}, u32[]{:S(2)}) collective-permute-start(bf16[96,1024]{1,0:T(8,128)(2,1)S(1)} %fusion.19), channel_id=1, source_target_pairs={{0,4},{1,5},{4,0},{5,1},{8,12},{9,13},{12,8},{13,9},{16,20},{17,21... | collective-permute-start | bytes 589832 | tf_op jit(solution)/shard_map/sum/ppermute | solution.py:39
  144.7 11.5 %collective-permute-start.14 = (bf16[96,1024]{1,0:T(8,128)(2,1)S(1)}, bf16[96,1024]{1,0:T(8,128)(2,1)S(1)}, u32[]{:S(2)}, u32[]{:S(2)}) collective-permute-start(bf16[96,1024]{1,0:T(8,128)(2,1)S(1)} %fusion.16), channel_id=1, source_target_pairs={{0,12},{1,13},{4,8},{5,9},{8,4},{9,5},{12,0},{13,1},{16,28},{17,29... | collective-permute-start | bytes 589832 | tf_op jit(solution)/shard_map/sum/ppermute | solution.py:39
  146.4 10.0 %collective-permute-start.16 = (bf16[96,1024]{1,0:T(8,128)(2,1)S(1)}, bf16[96,1024]{1,0:T(8,128)(2,1)S(1)}, u32[]{:S(2)}, u32[]{:S(2)}) collective-permute-start(bf16[96,1024]{1,0:T(8,128)(2,1)S(1)} %fusion.17), channel_id=1, source_target_pairs={{0,4},{1,5},{4,0},{5,1},{8,12},{9,13},{12,8},{13,9},{16,20},{17,21... | collective-permute-start | bytes 589832 | tf_op jit(solution)/shard_map/sum/ppermute | solution.py:39
  151.3 9.1 %collective-permute-start.24 = (bf16[24,2048]{1,0:T(8,128)(2,1)S(1)}, bf16[24,2048]{1,0:T(8,128)(2,1)S(1)}, u32[]{:S(2)}, u32[]{:S(2)}) collective-permute-start(bf16[24,2048]{1,0:T(8,128)(2,1)S(1)} %get-tuple-element.36), channel_id=1, source_target_pairs={{0,16},{1,17},{4,20},{5,21},{8,24},{9,25},{12,28},{13,29},{16,32},... | collective-permute-start | bytes 294920 | tf_op jit(solution)/shard_map/home/ppermute | solution.py:39
  152.7 8.2 %collective-permute-start.25 = (bf16[24,2048]{1,0:T(8,128)(2,1)S(1)}, bf16[24,2048]{1,0:T(8,128)(2,1)S(1)}, u32[]{:S(2)}, u32[]{:S(2)}) collective-permute-start(bf16[24,2048]{1,0:T(8,128)(2,1)S(1)} %get-tuple-element.37), channel_id=1, source_target_pairs={{0,48},{1,49},{4,52},{5,53},{8,56},{9,57},{12,60},{13,61},{16,0},{... | collective-permute-start | bytes 294920 | tf_op jit(solution)/shard_map/home/ppermute | solution.py:39
  154.5 6.8 %collective-permute-start.26 = (bf16[24,2048]{1,0:T(8,128)(2,1)S(1)}, bf16[24,2048]{1,0:T(8,128)(2,1)S(1)}, u32[]{:S(2)}, u32[]{:S(2)}) collective-permute-start(bf16[24,2048]{1,0:T(8,128)(2,1)S(1)} %get-tuple-element.34), channel_id=1, source_target_pairs={{0,32},{1,33},{4,36},{5,37},{8,40},{9,41},{12,44},{13,45},{16,48},... | collective-permute-start | bytes 294920 | tf_op jit(solution)/shard_map/home/ppermute | solution.py:39
  157.1 5.9 %collective-permute-start.17 = (bf16[24,2048]{1,0:T(8,128)(2,1)S(1)}, bf16[24,2048]{1,0:T(8,128)(2,1)S(1)}, u32[]{:S(2)}, u32[]{:S(2)}) collective-permute-start(bf16[24,2048]{1,0:T(8,128)(2,1)S(1)} %get-tuple-element.40), channel_id=1, source_target_pairs={{0,16},{1,17},{4,20},{5,21},{8,24},{9,25},{12,28},{13,29},{16,32},... | collective-permute-start | bytes 294920 | tf_op jit(solution)/shard_map/home/ppermute | solution.py:39
  157.7 5.9 %collective-permute-start.18 = (bf16[24,2048]{1,0:T(8,128)(2,1)S(1)}, bf16[24,2048]{1,0:T(8,128)(2,1)S(1)}, u32[]{:S(2)}, u32[]{:S(2)}) collective-permute-start(bf16[24,2048]{1,0:T(8,128)(2,1)S(1)} %get-tuple-element.41), channel_id=1, source_target_pairs={{0,48},{1,49},{4,52},{5,53},{8,56},{9,57},{12,60},{13,61},{16,0},{... | collective-permute-start | bytes 294920 | tf_op jit(solution)/shard_map/home/ppermute | solution.py:39
  160.3 6.1 %copy-start.2 = (bf16[24,2048]{1,0:T(8,128)(2,1)}, bf16[24,2048]{1,0:T(8,128)(2,1)S(1)}, u32[]{:S(2)}) copy-start(bf16[24,2048]{1,0:T(8,128)(2,1)S(1)} %collective-permute-done.24.refs_5_) | copy-start | bytes 294916
  160.3 6.1 %collective-permute-start.19 = (bf16[24,2048]{1,0:T(8,128)(2,1)S(1)}, bf16[24,2048]{1,0:T(8,128)(2,1)S(1)}, u32[]{:S(2)}, u32[]{:S(2)}) collective-permute-start(bf16[24,2048]{1,0:T(8,128)(2,1)S(1)} %get-tuple-element.38), channel_id=1, source_target_pairs={{0,32},{1,33},{4,36},{5,37},{8,40},{9,41},{12,44},{13,45},{16,48},... | collective-permute-start | bytes 294920 | tf_op jit(solution)/shard_map/home/ppermute | solution.py:39
  160.9 5.6 %copy-start.3 = (bf16[24,2048]{1,0:T(8,128)(2,1)}, bf16[24,2048]{1,0:T(8,128)(2,1)S(1)}, u32[]{:S(2)}) copy-start(bf16[24,2048]{1,0:T(8,128)(2,1)S(1)} %collective-permute-done.25.refs_6_) | copy-start | bytes 294916
  161.3 5.1 %copy-start.4 = (bf16[24,2048]{1,0:T(8,128)(2,1)}, bf16[24,2048]{1,0:T(8,128)(2,1)S(1)}, u32[]{:S(2)}) copy-start(bf16[24,2048]{1,0:T(8,128)(2,1)S(1)} %collective-permute-done.26.refs_7_) | copy-start | bytes 294916
  163.0 3.5 %copy-start.5 = (bf16[24,2048]{1,0:T(8,128)(2,1)}, bf16[24,2048]{1,0:T(8,128)(2,1)S(1)}, u32[]{:S(2)}) copy-start(bf16[24,2048]{1,0:T(8,128)(2,1)S(1)} %collective-permute-done.17.refs_1_) | copy-start | bytes 294916
  163.6 2.9 %copy-start.6 = (bf16[24,2048]{1,0:T(8,128)(2,1)}, bf16[24,2048]{1,0:T(8,128)(2,1)S(1)}, u32[]{:S(2)}) copy-start(bf16[24,2048]{1,0:T(8,128)(2,1)S(1)} %collective-permute-done.18.refs_2_) | copy-start | bytes 294916
  166.5 0.6 copy-start.7
Sparse Core Ops, SparseCore 0:
  9.2 106.7 all-gather.2

commit v4 on v3

--- a/solution.py
+++ b/solution.py
@@ -171,20 +171,19 @@
 
 
 def project_kernel(meta, *refs):
-    a_refs, w_refs, outs = refs[:4], refs[4:8], refs[8:12]
-    rows, total = refs[12:]
-    y = meta[2]
+    a_refs, w_ref, outs = refs[:4], refs[4], refs[5:9]
+    rows, total = refs[9:]
+    zh, core, y = meta[0], meta[1], meta[2]
 
     @pl.when(pl.program_id(0) == 0)
     def _():
-        for i in range(4):
-            for r in range(4):
-                rows[r, i * 96:(i + 1) * 96, :] = a_refs[i][r]
-
-    t = jnp.dot(rows[0], w_refs[0][0, 0, 0], preferred_element_type=jnp.float32)
-    for r in range(1, 4):
-        t += jnp.dot(rows[r], w_refs[r][0, 0, 0], preferred_element_type=jnp.float32)
-    total[...] = t
+        for r in range(4):
+            at = pl.multiple_of((lax.rem(zh + r // 2, 2) * 2 + lax.rem(core + r % 2, 2)) * 512, 512)
+            for i in range(4):
+                rows[i * 96:(i + 1) * 96, pl.ds(at, 512)] = a_refs[i][r]
+
+    w = w_ref[...].reshape(2048, 1024)
+    total[...] = jnp.dot(rows[...], w, preferred_element_type=jnp.float32)
     for h, (a, b) in enumerate(FLIPS):
         for out, first in ((outs[2 * h], a), (outs[2 * h + 1], 0)):
             for k, flip in enumerate((first, first ^ b)):
@@ -198,11 +197,7 @@
 def project(first, count, meta, pieces, w):
     whole = pl.BlockSpec((4, 96, 512), lambda i, m: (0, 0, 0))
 
-    def w_spec(r):
-        return pl.BlockSpec(
-            (1, 1, 1, 512, 1024),
-            lambda i, m: ((m[0] + r // 2) % 2, first + i, (m[1] + r % 2) % 2, 0, 0),
-        )
+    w_spec = pl.BlockSpec((2, 1, 2, 512, 1024), lambda i, m: (0, first + i, 0, 0, 0))
 
     with jax.named_scope("project"):
         return pl.pallas_call(
@@ -210,29 +205,29 @@
             grid_spec=pltpu.PrefetchScalarGridSpec(
                 num_scalar_prefetch=1,
                 grid=(count,),
-                in_specs=[whole] * 4 + [w_spec(r) for r in range(4)],
+                in_specs=[whole] * 4 + [w_spec],
                 out_specs=[pl.BlockSpec((2, 96, 512), lambda i, m: (0, 0, i))] * 4,
-                scratch_shapes=[pltpu.VMEM((4, 384, 512), jnp.bfloat16), pltpu.VMEM((384, 1024), jnp.float32)],
+                scratch_shapes=[pltpu.VMEM((384, 2048), jnp.bfloat16), pltpu.VMEM((384, 1024), jnp.float32)],
             ),
             out_shape=[jax.ShapeDtypeStruct((2, 96, count * 512), jnp.bfloat16)] * 4,
             compiler_params=pltpu.CompilerParams(vmem_limit_bytes=48 * 2**20),
             cost_estimate=pl.CostEstimate(
                 flops=count * 2 * 384 * 2048 * 1024, bytes_accessed=count * 5 * 10**6, transcendentals=0),
             name="project",
-        )(meta, *pieces, *([w] * 4))
+        )(meta, *pieces, w)
 
 
 def assemble_kernel(meta, *refs):
     out = refs[-1]
     x = meta[3]
     at_z = 0
-    for j, group in enumerate(SPLIT):
+    for group in SPLIT:
         for i, step in enumerate(X_STEPS):
             for g in range(group):
                 for h in range(2):
                     col = pl.multiple_of(((at_z + g) * 4 + lax.rem(x + step, 4)) * 1024 + h * 512, 512)
-                    at = (h * group + g) * 512
-                    out[:, pl.ds(col, 512)] = refs[j * 4 + i][:, at:at + 512]
+                    at = (2 * at_z + h * group + g) * 512
+                    out[:, pl.ds(col, 512)] = refs[i][:, at:at + 512]
         at_z += group
 
 
@@ -242,6 +237,7 @@
         out_shape=jax.ShapeDtypeStruct((24, 16384), jnp.bfloat16),
         in_specs=[pl.BlockSpec(memory_space=pltpu.SMEM)] + [pl.BlockSpec(memory_space=pltpu.VMEM)] * len(pieces),
         out_specs=pl.BlockSpec(memory_space=pltpu.VMEM),
+        compiler_params=pltpu.CompilerParams(vmem_limit_bytes=56 * 2**20),
         name="assemble",
     )(meta, *pieces)
 
@@ -301,10 +297,12 @@
                 last = send((kept[1] + got[1]).astype(jnp.bfloat16), flip=b)
                 halves.append((kept[0] + got[0] + last.astype(jnp.float32)).astype(jnp.bfloat16))
             total = jnp.concatenate(halves, axis=1)
-        with jax.named_scope("home"):
-            own, down, up, far = [total[i * 24:(i + 1) * 24] for i in range(4)]
-            up, down = send(up, dx=1), send(down, dx=-1)
-            done += [own, up, down, send(far, dx=2)]
+        done.append(total)
+    with jax.named_scope("home"):
+        total = jnp.concatenate(done, axis=1)
+        own, down, up, far = [total[i * 24:(i + 1) * 24] for i in range(4)]
+        up, down = send(up, dx=1), send(down, dx=-1)
+        done = [own, up, down, send(far, dx=2)]
     return assemble(where, done)
 
 

time: 176 us -> 176 us (level)
  Pallas kernels: 22.9 us -> 30.1 us
  starting transfers between devices: 39.9 us -> 36.1 us
  waiting for transfers between devices: 93.7 us -> 89.9 us
    pallas_call x1, Pallas kernels: 7.1 us -> 14.4 us  [attend(): pl.pallas_call(attend_kernel, out_shape=[jax.ShapeDtypeStruct((96, HEADS...]
    all_gather x1, waiting for transfers between devices: 22 us -> 16.6 us  [local(): lax.all_gather(out_weight, ('ctx', 'tp'), axis_index_groups=groups, axis=0)]
    ppermute x27 -> x24, starting transfers between devices: 39.9 us -> 36.1 us  [send(): return lax.ppermute(a, ('ctx', 'tp'), perm(**step))]
    ppermute x27 -> x24, waiting for transfers between devices: 71 us -> 72.6 us  [send(): return lax.ppermute(a, ('ctx', 'tp'), perm(**step))]
  transfers between devices with their start and end apart: 28 -> 25, of which waited for: 17 -> 17; matrix products, arithmetic and copies ran while one was open for 3% -> 2% of each run, Pallas kernels for 8% -> 12%
where the time goes in v4:
time: 176 us; the launch traced here: 175 us
  waiting for transfers between devices  89.9 us (51%)
  starting transfers between devices  36.1 us (21%)
  Pallas kernels  30.1 us (17%)
  between operations  14 us (8%)
  other arithmetic  3.45 us (2%)
    ppermute x24, waiting for transfers between devices, send(): return lax.ppermute(a, ('ctx', 'tp'), perm(**step))  72.6 us
    ppermute x24, starting transfers between devices, send(): return lax.ppermute(a, ('ctx', 'tp'), perm(**step))  36.1 us
    all_gather x1, waiting for transfers between devices, local(): lax.all_gather(out_weight, ('ctx', 'tp'), axis_index_groups=groups, axis=0)  16.6 us
    pallas_call x1, Pallas kernels, attend(): pl.pallas_call(attend_kernel, out_shape=[jax.ShapeDtypeStruct((96, HEADS...  14.4 us
    pallas_call x2, Pallas kernels, project(): pl.pallas_call(project_kernel, grid_spec=pltpu.PrefetchScalarGridSpec(num...  13.5 us
  transfers between devices with their start and end apart: 25, of which 17 were waited for; matrix products, arithmetic and copies ran while one was open for 2% of the time, Pallas kernels for 12%

profile of v4, /device:TPU:8, one launch (start us, length us, event | category | flops | bytes accessed | tf_op | source)
XLA Modules:
  0.0 175.2 jit_solution(7777455196623820270)
XLA Ops:
  6.5 0.7 all-gather.3.cloned.1.call-update
  7.4 1.2 dynamic-slice_select_fusion
  8.7 2.0 %collective-permute-start = (bf16[384,128]{1,0:T(8,128)(2,1)S(1)}, bf16[384,128]{1,0:T(8,128)(2,1)S(1)}, u32[]{:S(2)}, u32[]{:S(2)}) collective-permute-start(bf16[384,128]{1,0:T(8,128)(2,1)S(1)} %get-tuple-element.32), channel_id=1, source_target_pairs={{0,64},{1,65},{4,68},{5,69},{8,72},{9,73},{12,76},{13,77},{16,80},... | collective-permute-start | bytes 294920 | tf_op jit(solution)/shard_map/kv/ppermute | solution.py:39
  10.7 4.0 %collective-permute-start.1 = (bf16[384,128]{1,0:T(8,128)(2,1)S(1)}, bf16[384,128]{1,0:T(8,128)(2,1)S(1)}, u32[]{:S(2)}, u32[]{:S(2)}) collective-permute-start(bf16[384,128]{1,0:T(8,128)(2,1)S(1)} %get-tuple-element.33), channel_id=1, source_target_pairs={{0,194},{1,195},{4,198},{5,199},{8,202},{9,203},{12,206},{13,207},... | collective-permute-start | bytes 294920 | tf_op jit(solution)/shard_map/kv/ppermute | solution.py:39
  14.7 1.0 constant_dynamic-update-slice_fusion.6
  15.7 2.4 %collective-permute-done = bf16[384,128]{1,0:T(8,128)(2,1)S(1)} collective-permute-done((bf16[384,128]{1,0:T(8,128)(2,1)S(1)}, bf16[384,128]{1,0:T(8,128)(2,1)S(1)}, u32[]{:S(2)}, u32[]{:S(2)}) %collective-permute-start) | collective-permute-done | bytes 98336 | tf_op jit(solution)/shard_map/kv/ppermute | solution.py:39
  18.1 4.9 %collective-permute-done.2 = bf16[384,128]{1,0:T(8,128)(2,1)S(1)} collective-permute-done((bf16[384,128]{1,0:T(8,128)(2,1)S(1)}, bf16[384,128]{1,0:T(8,128)(2,1)S(1)}, u32[]{:S(2)}, u32[]{:S(2)}) %collective-permute-start.2) | collective-permute-done | bytes 98336 | tf_op jit(solution)/shard_map/kv/ppermute | solution.py:39
  23.0 1.6 collective-permute-start.3
  24.6 1.7 collective-permute-start.4
  26.4 1.8 %collective-permute-start.5 = (bf16[4,384,128]{2,1,0:T(8,128)(2,1)S(1)}, bf16[4,384,128]{2,1,0:T(8,128)(2,1)S(1)}, u32[]{:S(2)}, u32[]{:S(2)}) collective-permute-start(bf16[4,384,128]{2,1,0:T(8,128)(2,1)S(1)} %pad_maximum_fusion.1), channel_id=1, source_target_pairs={{0,32},{1,33},{4,36},{5,37},{8,40},{9,41},{12,44},{13,45},{16,48},... | collective-permute-start | bytes 1179656 | tf_op jit(solution)/shard_map/kv/ppermute | solution.py:39
  28.2 7.2 %collective-permute-done.3 = bf16[4,384,128]{2,1,0:T(8,128)(2,1)S(1)} collective-permute-done((bf16[4,384,128]{2,1,0:T(8,128)(2,1)S(1)}, bf16[4,384,128]{2,1,0:T(8,128)(2,1)S(1)}, u32[]{:S(2)}, u32[]{:S(2)}) %collective-permute-start.3) | collective-permute-done | bytes 393248 | tf_op jit(solution)/shard_map/kv/ppermute | solution.py:39
  35.4 0.1 constant_dynamic-update-slice_fusion.2
  35.4 5.3 %collective-permute-done.4 = bf16[4,384,128]{2,1,0:T(8,128)(2,1)S(1)} collective-permute-done((bf16[4,384,128]{2,1,0:T(8,128)(2,1)S(1)}, bf16[4,384,128]{2,1,0:T(8,128)(2,1)S(1)}, u32[]{:S(2)}, u32[]{:S(2)}) %collective-permute-start.4) | collective-permute-done | bytes 393248 | tf_op jit(solution)/shard_map/kv/ppermute | solution.py:39
  40.7 0.1 constant_dynamic-update-slice_fusion.1
  40.8 1.6 collective-permute-done.5
  42.4 0.1 collective-permute-start.6
  42.7 0.1 concatenate.10.meta
  42.8 3.2 %collective-permute-done.6.theirs_ref = bf16[16,384,128]{2,1,0:T(8,128)(2,1)S(1)} collective-permute-done((bf16[16,384,128]{2,1,0:T(8,128)(2,1)S(1)}, bf16[16,384,128]{2,1,0:T(8,128)(2,1)S(1)}, u32[]{:S(2)}, u32[]{:S(2)}) %collective-permute-start.6) | collective-permute-done | bytes 1572896 | tf_op jit(solution)/shard_map/kv/ppermute | solution.py:39
  45.9 14.4 %attend.1 = (bf16[96,512]{1,0:T(8,128)(2,1)S(1)}, bf16[96,512]{1,0:T(8,128)(2,1)S(1)}, bf16[96,512]{1,0:T(8,128)(2,1)S(1)}, bf16[96,512]{1,0:T(8,128)(2,1)S(1)}) custom-call(s32[55]{0:T(128)S(1)} %concatenate.10.meta, bf16[384,512]{1,0:T(8,128)(2,1)S(1)} %copy-done.1, bf16[16,384,128]{2,1,0:T(8,128)(2,1)S(1)} %constant_dynamic-update-slice_fusion.mine_ref, ...), custom_call_target="tpu_custom_call" | custom-call | flops 4000000000 | bytes 4000000 | tf_op jit(solution)/shard_map/attend/attend/pallas_call | solution.py:153
  60.3 0.2 collective-permute-start.7
  60.6 6.0 %collective-permute-start.8 = (bf16[96,512]{1,0:T(8,128)(2,1)S(1)}, bf16[96,512]{1,0:T(8,128)(2,1)S(1)}, u32[]{:S(2)}, u32[]{:S(2)}) collective-permute-start(bf16[96,512]{1,0:T(8,128)(2,1)S(1)} %get-tuple-element.19), channel_id=1, source_target_pairs={{0,2},{1,3},{4,6},{5,7},{8,10},{9,11},{12,14},{13,15},{16,18},{17,... | collective-permute-start | bytes 294920 | tf_op jit(solution)/shard_map/rows/ppermute | solution.py:39
  66.5 8.1 %collective-permute-done.8 = bf16[96,512]{1,0:T(8,128)(2,1)S(1)} collective-permute-done((bf16[96,512]{1,0:T(8,128)(2,1)S(1)}, bf16[96,512]{1,0:T(8,128)(2,1)S(1)}, u32[]{:S(2)}, u32[]{:S(2)}) %collective-permute-start.8) | collective-permute-done | bytes 98336 | tf_op jit(solution)/shard_map/rows/ppermute | solution.py:39
  74.6 3.8 %collective-permute-done.9 = bf16[96,512]{1,0:T(8,128)(2,1)S(1)} collective-permute-done((bf16[96,512]{1,0:T(8,128)(2,1)S(1)}, bf16[96,512]{1,0:T(8,128)(2,1)S(1)}, u32[]{:S(2)}, u32[]{:S(2)}) %collective-permute-start.9) | collective-permute-done | bytes 98336 | tf_op jit(solution)/shard_map/rows/ppermute | solution.py:39
  78.5 0.1 collective-permute-start.10
  78.5 3.2 %collective-permute-start.11 = (bf16[4,96,512]{2,1,0:T(8,128)(2,1)S(1)}, bf16[4,96,512]{2,1,0:T(8,128)(2,1)S(1)}, u32[]{:S(2)}, u32[]{:S(2)}) collective-permute-start(bf16[4,96,512]{2,1,0:T(8,128)(2,1)S(1)} %pad_maximum_fusion.2.refs_0_), channel_id=1, source_target_pairs={{0,48},{1,49},{4,52},{5,53},{8,56},{9,57},{12,60},{13,61},{16,0},{... | collective-permute-start | bytes 1179656 | tf_op jit(solution)/shard_map/rows/ppermute | solution.py:39
  81.8 0.1 pad_add_fusion.meta
  81.9 17.5 %collective-permute-done.10.refs_1_ = bf16[4,96,512]{2,1,0:T(8,128)(2,1)S(1)} collective-permute-done((bf16[4,96,512]{2,1,0:T(8,128)(2,1)S(1)}, bf16[4,96,512]{2,1,0:T(8,128)(2,1)S(1)}, u32[]{:S(2)}, u32[]{:S(2)}) %collective-permute-start.10) | collective-permute-done | bytes 393248 | tf_op jit(solution)/shard_map/rows/ppermute | solution.py:39
  99.3 16.6 %all-gather.3.cloned.1.call-done = bf16[8192,1024]{1,0:T(8,128)(2,1)} async-done(((bf16[512,1024]{1,0:T(8,128)(2,1)}), bf16[8192,1024]{1,0:T(8,128)(2,1)}) %all-gather.3.cloned.1.call-update) | async-done | bytes 16777232 | tf_op jit(solution)/shard_map/weights/all_gather | solution.py:264
  115.9 6.8 %project.2 = (bf16[2,96,1024]{2,1,0:T(8,128)(2,1)S(1)}, bf16[2,96,1024]{2,1,0:T(8,128)(2,1)S(1)}, bf16[2,96,1024]{2,1,0:T(8,128)(2,1)S(1)}, bf16[2,96,1024]{2,1,0:T(8,128)(2,1)S(1)}) custom-call(s32[4]{0:T(128)S(1)} %pad_add_fusion.meta, bf16[4,96,512]{2,1,0:T(8,128)(2,1)S(1)} %pad_maximum_fusion.2.refs_0_, ...), custom_call_target="tpu_custom_call" | custom-call | flops 3221225472 | bytes 10000000 | tf_op jit(solution)/shard_map/project/project/pallas_call | solution.py:203
  122.7 0.6 collective-permute-start.13
  123.3 2.1 %collective-permute-start.15 = (bf16[2,96,1024]{2,1,0:T(8,128)(2,1)S(1)}, bf16[2,96,1024]{2,1,0:T(8,128)(2,1)S(1)}, u32[]{:S(2)}, u32[]{:S(2)}) collective-permute-start(bf16[2,96,1024]{2,1,0:T(8,128)(2,1)S(1)} %get-tuple-element.24), channel_id=1, source_target_pairs={{0,12},{1,13},{4,8},{5,9},{8,4},{9,5},{12,0},{13,1},{16,28},{17,29... | collective-permute-start | bytes 1179656 | tf_op jit(solution)/shard_map/sum/ppermute | solution.py:39
  125.5 6.8 %project.3 = (bf16[2,96,1024]{2,1,0:T(8,128)(2,1)S(1)}, bf16[2,96,1024]{2,1,0:T(8,128)(2,1)S(1)}, bf16[2,96,1024]{2,1,0:T(8,128)(2,1)S(1)}, bf16[2,96,1024]{2,1,0:T(8,128)(2,1)S(1)}) custom-call(s32[4]{0:T(128)S(1)} %pad_add_fusion.meta, bf16[4,96,512]{2,1,0:T(8,128)(2,1)S(1)} %pad_maximum_fusion.2.refs_0_, ...), custom_call_target="tpu_custom_call" | custom-call | flops 3221225472 | bytes 10000000 | tf_op jit(solution)/shard_map/project/project/pallas_call | solution.py:203
  132.2 0.1 convert_element_type.72
  132.3 0.1 convert_element_type.78
  132.4 1.5 collective-permute-start.17
  133.9 0.1 convert_element_type.84
  134.0 0.6 collective-permute-start.19
  134.6 0.1 convert_element_type.90
  134.7 0.1 convert_element_type.73
  134.9 1.6 collective-permute-start.14
  136.4 0.1 convert_element_type.79
  136.6 1.9 %collective-permute-start.16 = (bf16[96,1024]{1,0:T(8,128)(2,1)S(1)}, bf16[96,1024]{1,0:T(8,128)(2,1)S(1)}, u32[]{:S(2)}, u32[]{:S(2)}) collective-permute-start(bf16[96,1024]{1,0:T(8,128)(2,1)S(1)} %fusion.17), channel_id=1, source_target_pairs={{0,4},{1,5},{4,0},{5,1},{8,12},{9,13},{12,8},{13,9},{16,20},{17,21... | collective-permute-start | bytes 589832 | tf_op jit(solution)/shard_map/sum/ppermute | solution.py:39
  138.4 6.1 %collective-permute-done.17 = bf16[2,96,1024]{2,1,0:T(8,128)(2,1)S(1)} collective-permute-done((bf16[2,96,1024]{2,1,0:T(8,128)(2,1)S(1)}, bf16[2,96,1024]{2,1,0:T(8,128)(2,1)S(1)}, u32[]{:S(2)}, u32[]{:S(2)}) %collective-permute-start.17) | collective-permute-done | bytes 393248 | tf_op jit(solution)/shard_map/sum/ppermute | solution.py:39
  144.5 0.1 convert_element_type.85
  144.6 0.1 collective-permute-start.18
  144.7 1.4 collective-permute-done.19
  146.2 0.1 convert_element_type.91
  146.3 1.9 %collective-permute-start.20 = (bf16[96,1024]{1,0:T(8,128)(2,1)S(1)}, bf16[96,1024]{1,0:T(8,128)(2,1)S(1)}, u32[]{:S(2)}, u32[]{:S(2)}) collective-permute-start(bf16[96,1024]{1,0:T(8,128)(2,1)S(1)} %fusion.19), channel_id=1, source_target_pairs={{0,4},{1,5},{4,0},{5,1},{8,12},{9,13},{12,8},{13,9},{16,20},{17,21... | collective-permute-start | bytes 589832 | tf_op jit(solution)/shard_map/sum/ppermute | solution.py:39
  148.2 2.2 %collective-permute-done.14 = bf16[96,1024]{1,0:T(8,128)(2,1)S(1)} collective-permute-done((bf16[96,1024]{1,0:T(8,128)(2,1)S(1)}, bf16[96,1024]{1,0:T(8,128)(2,1)S(1)}, u32[]{:S(2)}, u32[]{:S(2)}) %collective-permute-start.14) | collective-permute-done | bytes 196640 | tf_op jit(solution)/shard_map/sum/ppermute | solution.py:39
  150.4 0.1 fusion.15
  150.4 0.1 fusion.11
  150.5 2.4 %collective-permute-done.18 = bf16[96,1024]{1,0:T(8,128)(2,1)S(1)} collective-permute-done((bf16[96,1024]{1,0:T(8,128)(2,1)S(1)}, bf16[96,1024]{1,0:T(8,128)(2,1)S(1)}, u32[]{:S(2)}, u32[]{:S(2)}) %collective-permute-start.18) | collective-permute-done | bytes 196640 | tf_op jit(solution)/shard_map/sum/ppermute | solution.py:39
  153.0 0.1 fusion.7
  153.0 0.1 fusion.3
  153.1 0.1 pad_maximum_fusion
  153.2 0.7 fusion.20
  153.9 1.5 collective-permute-start.21
  155.4 1.8 %collective-permute-start.22 = (bf16[24,4096]{1,0:T(8,128)(2,1)S(1)}, bf16[24,4096]{1,0:T(8,128)(2,1)S(1)}, u32[]{:S(2)}, u32[]{:S(2)}) collective-permute-start(bf16[24,4096]{1,0:T(8,128)(2,1)S(1)} %get-tuple-element.35), channel_id=1, source_target_pairs={{0,48},{1,49},{4,52},{5,53},{8,56},{9,57},{12,60},{13,61},{16,0},{... | collective-permute-start | bytes 589832 | tf_op jit(solution)/shard_map/home/ppermute | solution.py:39
  157.1 1.8 %collective-permute-start.23 = (bf16[24,4096]{1,0:T(8,128)(2,1)S(1)}, bf16[24,4096]{1,0:T(8,128)(2,1)S(1)}, u32[]{:S(2)}, u32[]{:S(2)}) collective-permute-start(bf16[24,4096]{1,0:T(8,128)(2,1)S(1)} %get-tuple-element.34), channel_id=1, source_target_pairs={{0,32},{1,33},{4,36},{5,37},{8,40},{9,41},{12,44},{13,45},{16,48},... | collective-permute-start | bytes 589832 | tf_op jit(solution)/shard_map/home/ppermute | solution.py:39
  158.9 3.9 %collective-permute-done.21.refs_1_ = bf16[24,4096]{1,0:T(8,128)(2,1)S(1)} collective-permute-done((bf16[24,4096]{1,0:T(8,128)(2,1)S(1)}, bf16[24,4096]{1,0:T(8,128)(2,1)S(1)}, u32[]{:S(2)}, u32[]{:S(2)}) %collective-permute-start.21) | collective-permute-done | bytes 196640 | tf_op jit(solution)/shard_map/home/ppermute | solution.py:39
  162.8 1.2 collective-permute-done.22.refs_2_
  163.9 1.6 collective-permute-done.23.refs_3_
  165.6 0.7 copy-done.4
  166.2 2.2 %assemble.1 = bf16[24,16384]{1,0:T(8,128)(2,1)} custom-call(s32[4]{0:T(128)} %copy-done, bf16[24,4096]{1,0:T(8,128)(2,1)} %get-tuple-element.37.refs_0_, bf16[24,4096]{1,0:T(8,128)(2,1)} %copy-done.2, bf16[24,4096]{1,0:T(8,128)(2,1)} %copy-done.3, bf16[24,4096]{1,0:T(8,128)(2,1)} %copy-done.4), custom_call_target="tpu_custom_call" | custom-call | tf_op jit(solution)/shard_map/assemble/pallas_call | solution.py:235
  (35 shorter events, 0.4 us)
Async XLA Ops:
  6.5 109.4 %all-gather.3.cloned.1.call-start = ((), (), s32[]{:S(2)}) async-start(), calls=%async_computation | async-start | bytes 17825792 | tf_op jit(solution)/shard_map/weights/all_gather | solution.py:264
  8.7 9.4 %collective-permute-start = (bf16[384,128]{1,0:T(8,128)(2,1)S(1)}, bf16[384,128]{1,0:T(8,128)(2,1)S(1)}, u32[]{:S(2)}, u32[]{:S(2)}) collective-permute-start(bf16[384,128]{1,0:T(8,128)(2,1)S(1)} %get-tuple-element.32), channel_id=1, source_target_pairs={{0,64},{1,65},{4,68},{5,69},{8,72},{9,73},{12,76},{13,77},{16,80},... | collective-permute-start | bytes 294920 | tf_op jit(solution)/shard_map/kv/ppermute | solution.py:39
  10.7 7.4 %collective-permute-start.1 = (bf16[384,128]{1,0:T(8,128)(2,1)S(1)}, bf16[384,128]{1,0:T(8,128)(2,1)S(1)}, u32[]{:S(2)}, u32[]{:S(2)}) collective-permute-start(bf16[384,128]{1,0:T(8,128)(2,1)S(1)} %get-tuple-element.33), channel_id=1, source_target_pairs={{0,194},{1,195},{4,198},{5,199},{8,202},{9,203},{12,206},{13,207},... | collective-permute-start | bytes 294920 | tf_op jit(solution)/shard_map/kv/ppermute | solution.py:39
  14.7 8.3 %collective-permute-start.2 = (bf16[384,128]{1,0:T(8,128)(2,1)S(1)}, bf16[384,128]{1,0:T(8,128)(2,1)S(1)}, u32[]{:S(2)}, u32[]{:S(2)}) collective-permute-start(bf16[384,128]{1,0:T(8,128)(2,1)S(1)} %get-tuple-element.31), channel_id=1, source_target_pairs={{0,128},{1,129},{4,132},{5,133},{8,136},{9,137},{12,140},{13,141},... | collective-permute-start | bytes 294920 | tf_op jit(solution)/shard_map/kv/ppermute | solution.py:39
  23.0 12.4 %collective-permute-start.3 = (bf16[4,384,128]{2,1,0:T(8,128)(2,1)S(1)}, bf16[4,384,128]{2,1,0:T(8,128)(2,1)S(1)}, u32[]{:S(2)}, u32[]{:S(2)}) collective-permute-start(bf16[4,384,128]{2,1,0:T(8,128)(2,1)S(1)} %pad_maximum_fusion.1), channel_id=1, source_target_pairs={{0,16},{1,17},{4,20},{5,21},{8,24},{9,25},{12,28},{13,29},{16,32},... | collective-permute-start | bytes 1179656 | tf_op jit(solution)/shard_map/kv/ppermute | solution.py:39
  24.6 16.1 %collective-permute-start.4 = (bf16[4,384,128]{2,1,0:T(8,128)(2,1)S(1)}, bf16[4,384,128]{2,1,0:T(8,128)(2,1)S(1)}, u32[]{:S(2)}, u32[]{:S(2)}) collective-permute-start(bf16[4,384,128]{2,1,0:T(8,128)(2,1)S(1)} %pad_maximum_fusion.1), channel_id=1, source_target_pairs={{0,48},{1,49},{4,52},{5,53},{8,56},{9,57},{12,60},{13,61},{16,0},{... | collective-permute-start | bytes 1179656 | tf_op jit(solution)/shard_map/kv/ppermute | solution.py:39
  26.4 16.0 %collective-permute-start.5 = (bf16[4,384,128]{2,1,0:T(8,128)(2,1)S(1)}, bf16[4,384,128]{2,1,0:T(8,128)(2,1)S(1)}, u32[]{:S(2)}, u32[]{:S(2)}) collective-permute-start(bf16[4,384,128]{2,1,0:T(8,128)(2,1)S(1)} %pad_maximum_fusion.1), channel_id=1, source_target_pairs={{0,32},{1,33},{4,36},{5,37},{8,40},{9,41},{12,44},{13,45},{16,48},... | collective-permute-start | bytes 1179656 | tf_op jit(solution)/shard_map/kv/ppermute | solution.py:39
  28.2 14.5 %copy-start.5 = (s32[32]{0:T(128)S(1)}, s32[32]{0:T(128)}, u32[]{:S(2)}) copy-start(s32[32]{0:T(128)} %param.10) | copy-start | bytes 388
  28.2 14.5 %copy-start.6 = (s32[4]{0:T(128)S(1)}, s32[4]{0:T(128)}, u32[]{:S(2)}) copy-start(s32[4]{0:T(128)} %param.11) | copy-start | bytes 52
  28.2 17.8 %copy-start.1 = (bf16[384,512]{1,0:T(8,128)(2,1)S(1)}, bf16[384,512]{1,0:T(8,128)(2,1)}, u32[]{:S(2)}) copy-start(bf16[384,512]{1,0:T(8,128)(2,1)} %q_ref.1) | copy-start | bytes 1179652
  42.4 3.5 %collective-permute-start.6 = (bf16[16,384,128]{2,1,0:T(8,128)(2,1)S(1)}, bf16[16,384,128]{2,1,0:T(8,128)(2,1)S(1)}, u32[]{:S(2)}, u32[]{:S(2)}) collective-permute-start(bf16[16,384,128]{2,1,0:T(8,128)(2,1)S(1)} %constant_dynamic-update-slice_fusion.mine_ref), channel_id=1, source_target_pairs={{0,1},{1,0},{4,5},{5,4},{8,9},{9,8},{12,13},{13,12},{16,17},{17,16... | collective-permute-start | bytes 4718600 | tf_op jit(solution)/shard_map/kv/ppermute | solution.py:39
  60.3 6.2 %collective-permute-start.7 = (bf16[96,512]{1,0:T(8,128)(2,1)S(1)}, bf16[96,512]{1,0:T(8,128)(2,1)S(1)}, u32[]{:S(2)}, u32[]{:S(2)}) collective-permute-start(bf16[96,512]{1,0:T(8,128)(2,1)S(1)} %get-tuple-element.18), channel_id=1, source_target_pairs={{0,1},{1,0},{4,5},{5,4},{8,9},{9,8},{12,13},{13,12},{16,17},{17,16... | collective-permute-start | bytes 294920 | tf_op jit(solution)/shard_map/rows/ppermute | solution.py:39
  60.6 14.1 %collective-permute-start.8 = (bf16[96,512]{1,0:T(8,128)(2,1)S(1)}, bf16[96,512]{1,0:T(8,128)(2,1)S(1)}, u32[]{:S(2)}, u32[]{:S(2)}) collective-permute-start(bf16[96,512]{1,0:T(8,128)(2,1)S(1)} %get-tuple-element.19), channel_id=1, source_target_pairs={{0,2},{1,3},{4,6},{5,7},{8,10},{9,11},{12,14},{13,15},{16,18},{17,... | collective-permute-start | bytes 294920 | tf_op jit(solution)/shard_map/rows/ppermute | solution.py:39
  66.5 11.9 %collective-permute-start.9 = (bf16[96,512]{1,0:T(8,128)(2,1)S(1)}, bf16[96,512]{1,0:T(8,128)(2,1)S(1)}, u32[]{:S(2)}, u32[]{:S(2)}) collective-permute-start(bf16[96,512]{1,0:T(8,128)(2,1)S(1)} %get-tuple-element.20), channel_id=1, source_target_pairs={{0,3},{1,2},{4,7},{5,6},{8,11},{9,10},{12,15},{13,14},{16,19},{17,... | collective-permute-start | bytes 294920 | tf_op jit(solution)/shard_map/rows/ppermute | solution.py:39
  78.5 20.9 %collective-permute-start.10 = (bf16[4,96,512]{2,1,0:T(8,128)(2,1)S(1)}, bf16[4,96,512]{2,1,0:T(8,128)(2,1)S(1)}, u32[]{:S(2)}, u32[]{:S(2)}) collective-permute-start(bf16[4,96,512]{2,1,0:T(8,128)(2,1)S(1)} %pad_maximum_fusion.2.refs_0_), channel_id=1, source_target_pairs={{0,16},{1,17},{4,20},{5,21},{8,24},{9,25},{12,28},{13,29},{16,32},... | collective-permute-start | bytes 1179656 | tf_op jit(solution)/shard_map/rows/ppermute | solution.py:39
  78.5 20.8 %collective-permute-start.11 = (bf16[4,96,512]{2,1,0:T(8,128)(2,1)S(1)}, bf16[4,96,512]{2,1,0:T(8,128)(2,1)S(1)}, u32[]{:S(2)}, u32[]{:S(2)}) collective-permute-start(bf16[4,96,512]{2,1,0:T(8,128)(2,1)S(1)} %pad_maximum_fusion.2.refs_0_), channel_id=1, source_target_pairs={{0,48},{1,49},{4,52},{5,53},{8,56},{9,57},{12,60},{13,61},{16,0},{... | collective-permute-start | bytes 1179656 | tf_op jit(solution)/shard_map/rows/ppermute | solution.py:39
  81.8 17.6 %collective-permute-start.12 = (bf16[4,96,512]{2,1,0:T(8,128)(2,1)S(1)}, bf16[4,96,512]{2,1,0:T(8,128)(2,1)S(1)}, u32[]{:S(2)}, u32[]{:S(2)}) collective-permute-start(bf16[4,96,512]{2,1,0:T(8,128)(2,1)S(1)} %pad_maximum_fusion.2.refs_0_), channel_id=1, source_target_pairs={{0,32},{1,33},{4,36},{5,37},{8,40},{9,41},{12,44},{13,45},{16,48},... | collective-permute-start | bytes 1179656 | tf_op jit(solution)/shard_map/rows/ppermute | solution.py:39
  81.9 43.6 %copy-start = (s32[4]{0:T(128)}, s32[4]{0:T(128)S(1)}, u32[]{:S(2)}) copy-start(s32[4]{0:T(128)S(1)} %pad_add_fusion.meta) | copy-start | bytes 52
  122.7 12.0 %collective-permute-start.13 = (bf16[2,96,1024]{2,1,0:T(8,128)(2,1)S(1)}, bf16[2,96,1024]{2,1,0:T(8,128)(2,1)S(1)}, u32[]{:S(2)}, u32[]{:S(2)}) collective-permute-start(bf16[2,96,1024]{2,1,0:T(8,128)(2,1)S(1)} %get-tuple-element.22), channel_id=1, source_target_pairs={{0,4},{1,5},{4,0},{5,1},{8,12},{9,13},{12,8},{13,9},{16,20},{17,21... | collective-permute-start | bytes 1179656 | tf_op jit(solution)/shard_map/sum/ppermute | solution.py:39
  123.3 13.1 %collective-permute-start.15 = (bf16[2,96,1024]{2,1,0:T(8,128)(2,1)S(1)}, bf16[2,96,1024]{2,1,0:T(8,128)(2,1)S(1)}, u32[]{:S(2)}, u32[]{:S(2)}) collective-permute-start(bf16[2,96,1024]{2,1,0:T(8,128)(2,1)S(1)} %get-tuple-element.24), channel_id=1, source_target_pairs={{0,12},{1,13},{4,8},{5,9},{8,4},{9,5},{12,0},{13,1},{16,28},{17,29... | collective-permute-start | bytes 1179656 | tf_op jit(solution)/shard_map/sum/ppermute | solution.py:39
  132.4 12.1 %collective-permute-start.17 = (bf16[2,96,1024]{2,1,0:T(8,128)(2,1)S(1)}, bf16[2,96,1024]{2,1,0:T(8,128)(2,1)S(1)}, u32[]{:S(2)}, u32[]{:S(2)}) collective-permute-start(bf16[2,96,1024]{2,1,0:T(8,128)(2,1)S(1)} %get-tuple-element.26), channel_id=1, source_target_pairs={{0,4},{1,5},{4,0},{5,1},{8,12},{9,13},{12,8},{13,9},{16,20},{17,21... | collective-permute-start | bytes 1179656 | tf_op jit(solution)/shard_map/sum/ppermute | solution.py:39
  134.0 12.1 %collective-permute-start.19 = (bf16[2,96,1024]{2,1,0:T(8,128)(2,1)S(1)}, bf16[2,96,1024]{2,1,0:T(8,128)(2,1)S(1)}, u32[]{:S(2)}, u32[]{:S(2)}) collective-permute-start(bf16[2,96,1024]{2,1,0:T(8,128)(2,1)S(1)} %get-tuple-element.28), channel_id=1, source_target_pairs={{0,12},{1,13},{4,8},{5,9},{8,4},{9,5},{12,0},{13,1},{16,28},{17,29... | collective-permute-start | bytes 1179656 | tf_op jit(solution)/shard_map/sum/ppermute | solution.py:39
  134.9 15.5 %collective-permute-start.14 = (bf16[96,1024]{1,0:T(8,128)(2,1)S(1)}, bf16[96,1024]{1,0:T(8,128)(2,1)S(1)}, u32[]{:S(2)}, u32[]{:S(2)}) collective-permute-start(bf16[96,1024]{1,0:T(8,128)(2,1)S(1)} %fusion.16), channel_id=1, source_target_pairs={{0,12},{1,13},{4,8},{5,9},{8,4},{9,5},{12,0},{13,1},{16,28},{17,29... | collective-permute-start | bytes 589832 | tf_op jit(solution)/shard_map/sum/ppermute | solution.py:39
  136.6 13.9 %collective-permute-start.16 = (bf16[96,1024]{1,0:T(8,128)(2,1)S(1)}, bf16[96,1024]{1,0:T(8,128)(2,1)S(1)}, u32[]{:S(2)}, u32[]{:S(2)}) collective-permute-start(bf16[96,1024]{1,0:T(8,128)(2,1)S(1)} %fusion.17), channel_id=1, source_target_pairs={{0,4},{1,5},{4,0},{5,1},{8,12},{9,13},{12,8},{13,9},{16,20},{17,21... | collective-permute-start | bytes 589832 | tf_op jit(solution)/shard_map/sum/ppermute | solution.py:39
  144.6 8.3 %collective-permute-start.18 = (bf16[96,1024]{1,0:T(8,128)(2,1)S(1)}, bf16[96,1024]{1,0:T(8,128)(2,1)S(1)}, u32[]{:S(2)}, u32[]{:S(2)}) collective-permute-start(bf16[96,1024]{1,0:T(8,128)(2,1)S(1)} %fusion.18), channel_id=1, source_target_pairs={{0,12},{1,13},{4,8},{5,9},{8,4},{9,5},{12,0},{13,1},{16,28},{17,29... | collective-permute-start | bytes 589832 | tf_op jit(solution)/shard_map/sum/ppermute | solution.py:39
  146.3 6.8 %collective-permute-start.20 = (bf16[96,1024]{1,0:T(8,128)(2,1)S(1)}, bf16[96,1024]{1,0:T(8,128)(2,1)S(1)}, u32[]{:S(2)}, u32[]{:S(2)}) collective-permute-start(bf16[96,1024]{1,0:T(8,128)(2,1)S(1)} %fusion.19), channel_id=1, source_target_pairs={{0,4},{1,5},{4,0},{5,1},{8,12},{9,13},{12,8},{13,9},{16,20},{17,21... | collective-permute-start | bytes 589832 | tf_op jit(solution)/shard_map/sum/ppermute | solution.py:39
  153.9 8.9 %collective-permute-start.21 = (bf16[24,4096]{1,0:T(8,128)(2,1)S(1)}, bf16[24,4096]{1,0:T(8,128)(2,1)S(1)}, u32[]{:S(2)}, u32[]{:S(2)}) collective-permute-start(bf16[24,4096]{1,0:T(8,128)(2,1)S(1)} %get-tuple-element.36), channel_id=1, source_target_pairs={{0,16},{1,17},{4,20},{5,21},{8,24},{9,25},{12,28},{13,29},{16,32},... | collective-permute-start | bytes 589832 | tf_op jit(solution)/shard_map/home/ppermute | solution.py:39
  155.4 8.6 %collective-permute-start.22 = (bf16[24,4096]{1,0:T(8,128)(2,1)S(1)}, bf16[24,4096]{1,0:T(8,128)(2,1)S(1)}, u32[]{:S(2)}, u32[]{:S(2)}) collective-permute-start(bf16[24,4096]{1,0:T(8,128)(2,1)S(1)} %get-tuple-element.35), channel_id=1, source_target_pairs={{0,48},{1,49},{4,52},{5,53},{8,56},{9,57},{12,60},{13,61},{16,0},{... | collective-permute-start | bytes 589832 | tf_op jit(solution)/shard_map/home/ppermute | solution.py:39
  157.1 8.4 %collective-permute-start.23 = (bf16[24,4096]{1,0:T(8,128)(2,1)S(1)}, bf16[24,4096]{1,0:T(8,128)(2,1)S(1)}, u32[]{:S(2)}, u32[]{:S(2)}) collective-permute-start(bf16[24,4096]{1,0:T(8,128)(2,1)S(1)} %get-tuple-element.34), channel_id=1, source_target_pairs={{0,32},{1,33},{4,36},{5,37},{8,40},{9,41},{12,44},{13,45},{16,48},... | collective-permute-start | bytes 589832 | tf_op jit(solution)/shard_map/home/ppermute | solution.py:39
  162.8 2.8 %copy-start.2 = (bf16[24,4096]{1,0:T(8,128)(2,1)}, bf16[24,4096]{1,0:T(8,128)(2,1)S(1)}, u32[]{:S(2)}) copy-start(bf16[24,4096]{1,0:T(8,128)(2,1)S(1)} %collective-permute-done.21.refs_1_) | copy-start | bytes 589828
  163.9 1.6 copy-start.3
  165.6 0.7 copy-start.4
Sparse Core Ops, SparseCore 0:
  9.2 106.7 all-gather.2
